TPU v7x, 256 devices: a whole 4x4x8 slice. The times are simulated.
256 devices in a mesh: rep: 16 (over y, z_hi, core), fsdp: 16 (over x, z_lo).
Axes of the slice: x: 4, y: 4, z: 8 (z_hi: 2, z_lo: 4; z = z_hi * 4 + z_lo), core: 2. Of those that a mesh axis runs over, the one named last changes fastest.
Arguments:
- tokens: bfloat16 [98304, 4096], P(('rep', 'fsdp')), may hold values from -24 to 24
- cotangent: bfloat16 [98304, 1024], P(('rep', 'fsdp')), may hold values from -6 to 6
- weight: bfloat16 [4096, 1024], P('fsdp'), may hold values from -0.1875 to 0.1875
- moment: float32 [4096, 640], P('fsdp'), may hold values from -6 to 6
- second: float32 [4096, 640], P('fsdp'), may hold values from 0.25 to 4
- delayed: float32 [16, 4096, 384], P('rep', 'fsdp'), may hold values from -0.12 to 0.12
Outputs:
- grad_input: bfloat16 [98304, 4096], P(('rep', 'fsdp'))
- moment_next: float32 [4096, 640], P('fsdp')
- second_next: float32 [4096, 640], P('fsdp')
- adam_step: float32 [4096, 640], P('fsdp')
- host_grad: float32 [4096, 384], P('fsdp')
All inputs are finite; a program needn't handle non-finite values.
Results may differ from a plain program's by a relative error of at most 0.0038.
Values may be sent and summed in bfloat16 or wider, within the bound.
No kernel may reach another device: no remote copies, remote signals or barrier semaphores. Data moves between devices by JAX's collectives and lax.ppermute only.
A program may use at most 128 MiB of HBM per device.

v0:
```python
import jax
import jax.numpy as jnp
from jax import lax
from jax.sharding import PartitionSpec as P


def from_root(value, axis, source):
    kept = jnp.where(lax.axis_index(axis) == source, value, 0).astype(value.dtype)
    return lax.psum(kept, axis)


def on_device(tokens, cotangent, weight, moment, second, delayed):
    device_cols = moment.shape[1]
    pending = from_root(delayed, "rep", 0)[0]
    refreshed = (weight[:, device_cols:].astype(jnp.float32) + pending).astype(jnp.bfloat16)
    current = jnp.concatenate([weight[:, :device_cols], refreshed], axis=1)
    norm_factor = (tokens.shape[0] * lax.axis_size("rep") * lax.axis_size("fsdp")) ** (-0.5)
    grad_input = lax.dot_general(
        cotangent,
        lax.all_gather(current, "fsdp", axis=0, tiled=True),
        (((1,), (1,)), ((), ())),
        preferred_element_type=jnp.float32,
    ).astype(jnp.bfloat16)
    grad_block = lax.psum_scatter(
        lax.dot_general(
            tokens, cotangent, (((0,), (0,)), ((), ())), preferred_element_type=jnp.float32
        ),
        "fsdp",
        scatter_dimension=0,
        tiled=True,
    )
    grad = lax.psum(grad_block, "rep") * norm_factor
    device_grad = grad[:, :device_cols]
    moment_next = 0.9 * moment + 0.1 * device_grad
    second_next = 0.95 * second + 0.05 * device_grad * device_grad
    adam_step = moment_next / (1.0 - 0.9**20) / (jnp.sqrt(second_next / (1.0 - 0.95**20)) + 1e-08)
    return (grad_input, moment_next, second_next, adam_step, grad[:, device_cols:])


def solution(mesh):
    placed = (
        P(("rep", "fsdp"), None),
        P(("rep", "fsdp"), None),
        P("fsdp", None),
        P("fsdp", None),
        P("fsdp", None),
        P("rep", "fsdp", None),
    )
    return jax.shard_map(
        on_device,
        mesh=mesh,
        in_specs=placed,
        out_specs=(
            P(("rep", "fsdp"), None),
            P("fsdp", None),
            P("fsdp", None),
            P("fsdp", None),
            P("fsdp", None),
        ),
        check_vma=False,
    )
```

profile of v0, /device:TPU:1, one launch (start us, length us, event | category | flops | bytes accessed | tf_op | source)
XLA Modules:
  0.0 776.0 jit_solution(1318638703192295992)
XLA Ops:
  7.2 0.0 copy-start
  7.2 0.0 reduce-scatter.2.cloned.1.call-start
  7.2 1.8 copy-done
  9.1 9.2 %fusion.3 = f32[4096,1024]{1,0:T(8,128)} fusion(bf16[384,4096]{1,0:T(8,128)(2,1)S(1)} %copy-done, bf16[384,1024]{1,0:T(8,128)(2,1)} %param.7), kind=kOutput, calls=%fused_computation.10 | convolution fusion | flops 3221225472 | bytes 20709376 | tf_op jit(solution)/shard_map/dot_general | solution.py:25
  18.3 0.0 slice-start
  18.3 0.0 reduce-scatter.2.cloned.1.call-update
  18.3 0.0 all-reduce.3.cloned.1.call-start
  18.4 0.8 select_bitcast_fusion
  19.2 358.6 %reduce-scatter.2.cloned.1.call-done = f32[256,1024]{1,0:T(8,128)} async-done(((f32[4096,1024]{1,0:T(8,128)}), f32[256,1024]{1,0:T(8,128)}) %reduce-scatter.2.cloned.1.call-update) | async-done | bytes 1048592 | tf_op jit(solution)/shard_map/reduce_scatter | solution.py:24
  377.8 0.0 all-reduce.3.cloned.1.call-update
  377.8 0.0 all-gather.2.cloned.1.call-start
  377.9 186.2 %all-reduce.3.cloned.1.call-done = (f32[256,384]{1,0:T(8,128)}, f32[256,1024]{1,0:T(8,128)}) async-done(((f32[256,384]{1,0:T(8,128)}, f32[256,1024]{1,0:T(8,128)}), (f32[256,384]{1,0:T(8,128)}, f32[256,1024]{1,0:T(8,128)})) %all-reduce.3.cloned.1.call-update) | async-done | bytes 1441808 | tf_op jit(solution)/shard_map/psum | solution.py:9
  564.0 1.1 add_convert_fusion
  565.1 0.0 slice-done
  565.1 0.9 pad_maximum_fusion
  566.0 0.0 all-gather.2.cloned.1.call-update
  566.0 1.3 broadcast_multiply_fusion
  567.4 0.8 slice.17
  568.1 2.8 add_divide_fusion
  570.9 184.1 %all-gather.2.cloned.1.call-done = bf16[4096,1024]{1,0:T(8,128)(2,1)} async-done(((bf16[256,1024]{1,0:T(8,128)(2,1)}), bf16[4096,1024]{1,0:T(8,128)(2,1)}) %all-gather.2.cloned.1.call-update) | async-done | bytes 8388624 | tf_op jit(solution)/shard_map/all_gather | solution.py:20
  755.0 9.8 %fusion = bf16[384,4096]{0,1:T(8,128)(2,1)} fusion(bf16[4096,1024]{1,0:T(8,128)(2,1)} %all-gather.2.cloned.1.call-done, bf16[384,1024]{1,0:T(8,128)(2,1)} %param.7), kind=kOutput, calls=%fused_computation.1 | convolution fusion | flops 3222798336 | bytes 12320768 | tf_op jit(solution)/shard_map/dot_general | solution.py:18
  764.8 4.6 copy.11
Async XLA Ops:
  7.2 1.9 copy-start
  7.2 370.6 %reduce-scatter.2.cloned.1.call-start = ((), (), s32[]{:S(2)}) async-start(), calls=%async_computation.2 | async-start | bytes 17825792 | tf_op jit(solution)/shard_map/reduce_scatter | solution.py:24
  18.3 546.8 %slice-start = ((bf16[256,1024]{1,0:T(8,128)(2,1)}), bf16[256,640]{1,0:T(8,128)(2,1)S(1)}, s32[]{:S(2)}) async-start(bf16[256,1024]{1,0:T(8,128)(2,1)} %param.8), calls=%async_computation.4 | async-start | bytes 655360 | tf_op jit(solution)/shard_map/slice | solution.py:16
  18.3 545.7 %all-reduce.3.cloned.1.call-start = ((), (), s32[]{:S(2)}) async-start(), calls=%async_computation.3 | async-start | bytes 2883584 | tf_op jit(solution)/shard_map/psum | solution.py:9
  377.8 377.2 %all-gather.2.cloned.1.call-start = ((), (), s32[]{:S(2)}) async-start(), calls=%async_computation.1 | async-start | bytes 8912896 | tf_op jit(solution)/shard_map/all_gather | solution.py:20
Sparse Core Ops, SparseCore 0:
  18.5 359.2 reduce-scatter.1
  381.1 182.9 all-reduce.2
  566.4 188.5 all-gather.1
where the time goes:
time: 776 us
  waiting for transfers between devices  729 us (94%)
  matrix products  19 us (2%)
  between operations  13.8 us (2%)
    reduce_scatter x1, waiting for transfers between devices, on_device(): lax.psum_scatter(lax.dot_general(tokens, cotangent, (((0,), (0,)), ((), (...  359 us
    psum x1, waiting for transfers between devices, from_root(): return lax.psum(kept, axis)  186 us
    all_gather x1, waiting for transfers between devices, on_device(): lax.all_gather(current, 'fsdp', axis=0, tiled=True)  184 us
  transfers between devices with their start and end apart: 3, of which 3 were waited for; matrix products, arithmetic and copies ran while one was open for 1% of the time, Pallas kernels for 0%

commit v1 on v0

v1 whole, which is shorter than its diff:
```python
import jax
import jax.numpy as jnp
from jax import lax
from jax.experimental import pallas as pl
from jax.experimental.pallas import tpu as pltpu
from jax.sharding import PartitionSpec as P

AXES = ("rep", "fsdp")
SIZES = {"y": 4, "zh": 2, "c": 2, "x": 4, "zl": 4}
F32 = jnp.float32
BF16 = jnp.bfloat16


def unflatten(i):
    c = {}
    for name in ("zl", "x", "c", "zh", "y"):
        c[name] = i % SIZES[name]
        i //= SIZES[name]
    return c


def flatten(c):
    i = 0
    for name in ("y", "zh", "c", "x", "zl"):
        i = i * SIZES[name] + c[name]
    return i


def send(value, route):
    pairs = []
    for i in range(256):
        target = route(unflatten(i))
        if target is not None:
            pairs.append((i, flatten(target)))
    return lax.ppermute(value, AXES, pairs)


def partner(axis, first):
    def route(c):
        mask = 1 if (c["c"] == 0) == first else 3
        t = dict(c)
        t[axis] = c[axis] ^ mask
        if axis == "zl" and mask == 3 and c["zl"] in (0, 3):
            t["zh"] = 1 - c["zh"]
        return t

    return route


def flip(axis):
    def route(c):
        t = dict(c)
        t[axis] = 1 - c[axis]
        return t

    return route


def where_am_i():
    rep, fsdp = lax.axis_index("rep"), lax.axis_index("fsdp")
    return {"y": rep // 4, "zh": rep // 2 % 2, "c": rep % 2, "x": fsdp // 4, "zl": fsdp % 4}


def pick(value, index, dim):
    return lax.dynamic_index_in_dim(value, index, dim, keepdims=False)


def halve(value, dim, axis, me, wire):
    p = me[axis]
    a = jnp.where(me["c"] == 0, 1, 3)
    b = 4 - a
    got = send(
        jnp.stack([pick(value, p ^ a, dim), pick(value, p ^ 2, dim)]).astype(wire), partner(axis, True)
    )
    far = pick(value, p ^ b, dim) + got[1].astype(F32)
    near = pick(value, p, dim) + got[0].astype(F32)
    return near + send(far.astype(wire), partner(axis, False)).astype(F32)


def double(value, axis):
    pair = jnp.stack([value, send(value, partner(axis, False))])
    return jnp.concatenate([pair, send(pair, partner(axis, True))])


def places(p, core):
    b = jnp.where(core == 0, 3, 1)
    out = []
    for j in range(4):
        r = p ^ j
        out.append(jnp.where(r == 0, 0, jnp.where(r == b, 1, jnp.where(r == 2, 3, 2))))
    return out


def half_kernel(s_ref, t_ref, o_ref):
    other = 1 - s_ref[0]
    for j in range(16):
        start = pl.multiple_of(j * 256 + other * 128, 128)
        o_ref[:, j * 128 : (j + 1) * 128] = t_ref[:, pl.ds(start, 128)]


def mates_half(core, tokens):
    return pl.pallas_call(
        half_kernel,
        out_shape=jax.ShapeDtypeStruct((384, 2048), BF16),
        grid_spec=pltpu.PrefetchScalarGridSpec(
            num_scalar_prefetch=1,
            grid=(4,),
            in_specs=[pl.BlockSpec((96, 4096), lambda i, s: (i, 0))],
            out_specs=pl.BlockSpec((96, 2048), lambda i, s: (i, 0)),
        ),
        cost_estimate=pl.CostEstimate(flops=0, bytes_accessed=6 << 20, transcendentals=0),
    )(core, tokens)


def grad_kernel(s_ref, t_ref, u_ref, c_ref, d_ref, one_ref, two_ref):
    over_tokens = (((0,), (0,)), ((), ()))
    total = lax.dot_general(t_ref[...], c_ref[...], over_tokens, preferred_element_type=F32)
    total += lax.dot_general(u_ref[...], d_ref[...], over_tokens, preferred_element_type=F32)
    for y in range(4):
        one_ref[y, 0] = total[:, y * 256 : y * 256 + 128]
        two_ref[y, 0] = total[:, y * 256 + 128 : y * 256 + 256]


def chip_gradient(core, tokens, their_tokens, cot, their_cot):
    part = jax.ShapeDtypeStruct((4, 16, 128, 128), F32)
    whole = pl.BlockSpec((384, 1024), lambda j, s: (0, 0))
    return pl.pallas_call(
        grad_kernel,
        out_shape=(part, part),
        grid_spec=pltpu.PrefetchScalarGridSpec(
            num_scalar_prefetch=1,
            grid=(16,),
            in_specs=[
                pl.BlockSpec((384, 128), lambda j, s: (0, 2 * j + s[0])),
                pl.BlockSpec((384, 128), lambda j, s: (0, j)),
                whole,
                whole,
            ],
            out_specs=[pl.BlockSpec((4, 1, 128, 128), lambda j, s: (0, j, 0, 0))] * 2,
        ),
        compiler_params=pltpu.CompilerParams(vmem_limit_bytes=32 << 20),
        cost_estimate=pl.CostEstimate(
            flops=2 * 768 * 2048 * 1024, bytes_accessed=14 << 20, transcendentals=0
        ),
    )(core, tokens, their_tokens, cot, their_cot)


def product(s_ref, cot_ref, w_ref, r_ref, zl):
    at = s_ref[5 + zl]
    rows = jnp.concatenate([w_ref[s_ref[9 + y], at, 0] for y in range(4)])
    host = jnp.concatenate([r_ref[at, s_ref[9 + y], 0] for y in range(4)])
    last = (((1,), (1,)), ((), ()))
    split = rows.shape[1]
    total = lax.dot_general(cot_ref[:, :split], rows, last, preferred_element_type=F32)
    total += lax.dot_general(cot_ref[:, split:], host, last, preferred_element_type=F32)
    return total.astype(BF16)


def theirs_kernel(s_ref, cot_ref, w_ref, r_ref, o_ref):
    for zl in range(4):
        o_ref[:, zl * 128 : zl * 128 + 128] = product(s_ref, cot_ref, w_ref, r_ref, zl)


def ours_kernel(s_ref, cot_ref, w_ref, r_ref, got_ref, o_ref):
    core = s_ref[0]
    for zl in range(4):
        mine = pl.multiple_of(zl * 256 + core * 128, 128)
        other = pl.multiple_of(zl * 256 + 128 - core * 128, 128)
        o_ref[:, pl.ds(mine, 128)] = product(s_ref, cot_ref, w_ref, r_ref, zl)
        o_ref[:, pl.ds(other, 128)] = got_ref[:, zl * 128 : zl * 128 + 128]


def input_gradient(kernel, where, cot, kept, host, got=None):
    width = 512 if got is None else 1024
    more = [] if got is None else [pl.BlockSpec((384, 512), lambda x, s: (0, x))]
    return pl.pallas_call(
        kernel,
        out_shape=jax.ShapeDtypeStruct((384, 4 * width), BF16),
        grid_spec=pltpu.PrefetchScalarGridSpec(
            num_scalar_prefetch=1,
            grid=(4,),
            in_specs=[
                pl.BlockSpec((384, 1024), lambda x, s: (0, 0)),
                pl.BlockSpec((4, 4, 1, 32, kept.shape[-1]), lambda x, s: (0, 0, s[1 + x], 0, 0)),
                pl.BlockSpec((4, 4, 1, 32, host.shape[-1]), lambda x, s: (0, 0, s[1 + x], 0, 0)),
            ]
            + more,
            out_specs=pl.BlockSpec((384, width), lambda x, s: (0, x)),
        ),
        compiler_params=pltpu.CompilerParams(vmem_limit_bytes=32 << 20),
        cost_estimate=pl.CostEstimate(
            flops=2 * 384 * 2048 * 1024, bytes_accessed=7 << 20, transcendentals=0
        ),
    )(*([where, cot, kept, host] + ([] if got is None else [got])))


def scatter_from_root(refreshed, me):
    pieces = refreshed.reshape(2, 4, 32, refreshed.shape[1])

    def over_y(y):
        return lambda c: dict(c, y=y) if (c["y"], c["zh"], c["c"]) == (0, 0, 0) else None

    def over_rest(zh, core):
        return lambda c: dict(c, zh=zh, c=core) if (c["zh"], c["c"]) == (0, 0) else None

    got = [pieces[:, 0]] + [send(pieces[:, y], over_y(y)) for y in (1, 2, 3)]
    y = me["y"]
    both = jnp.where(y == 0, got[0], jnp.where(y == 1, got[1], jnp.where(y == 2, got[2], got[3])))
    rest = {(0, 0): both[0]}
    for zh, core in ((1, 1), (1, 0), (0, 1)):
        rest[zh, core] = send(both[core], over_rest(zh, core))
    zero = jnp.where(me["c"] == 0, rest[0, 0], rest[0, 1])
    one = jnp.where(me["c"] == 0, rest[1, 0], rest[1, 1])
    return jnp.where(me["zh"] == 0, zero, one)


def on_device(tokens, cotangent, weight, moment, second, delayed):
    me = where_am_i()
    device_cols = moment.shape[1]
    norm_factor = (tokens.shape[0] * lax.axis_size("rep") * lax.axis_size("fsdp")) ** (-0.5)
    core = me["c"].astype(jnp.int32).reshape(1)

    their_cot = send(cotangent, flip("c"))
    their_tokens = send(mates_half(core, tokens), flip("c"))

    refreshed = (weight[:, device_cols:].astype(F32) + delayed[0]).astype(BF16)
    kept = lax.dynamic_slice(weight, (me["c"] * 128 + me["y"] * 32, 0), (32, device_cols))
    kept = double(double(double(kept, "x"), "zl"), "y")
    host = scatter_from_root(refreshed, me)
    host = double(double(double(host, "x"), "y"), "zl")

    one, two = chip_gradient(core, tokens, their_tokens, cotangent, their_cot)
    one = one.reshape(4, 4, 4, 128, 128)
    two = two.reshape(4, 4, 4, 128, 128)
    one = halve(one, 1, "x", me, BF16)
    two = halve(two, 2, "zl", me, BF16)
    one = halve(one, 0, "y", me, BF16)
    two = halve(two, 1, "x", me, BF16)
    one = halve(one, 0, "zl", me, F32)
    two = halve(two, 0, "y", me, F32)
    total = jnp.stack([one, two]).astype(BF16)
    total = total.astype(F32) + send(total, flip("zh")).astype(F32)
    mine = double(total, "y")
    other = send(mine, flip("c"))

    def in_place(blocks, of_core):
        at = places(me["y"], of_core)
        return jnp.concatenate([pick(blocks, at[y], 0)[h] for y in range(4) for h in range(2)], axis=1)

    is_first = me["c"] == 0
    mine, other = in_place(mine, me["c"]), in_place(other, 1 - me["c"])
    grad = norm_factor * jnp.concatenate(
        [jnp.where(is_first, mine, other), jnp.where(is_first, other, mine)]
    )
    device_grad = grad[:, :device_cols]
    moment_next = 0.9 * moment + 0.1 * device_grad
    second_next = 0.95 * second + 0.05 * device_grad * device_grad
    adam_step = moment_next / (1.0 - 0.9**20) / (jnp.sqrt(second_next / (1.0 - 0.95**20)) + 1e-08)

    where = jnp.stack(
        [me["c"]] + [at for axis in ("x", "zl", "y") for at in places(me[axis], me["c"])]
    ).astype(jnp.int32)
    got = send(input_gradient(theirs_kernel, where, their_cot, kept, host), flip("c"))
    grad_input = input_gradient(ours_kernel, where, cotangent, kept, host, got)
    return (grad_input, moment_next, second_next, adam_step, grad[:, device_cols:])


def solution(mesh):
    placed = (
        P(("rep", "fsdp"), None),
        P(("rep", "fsdp"), None),
        P("fsdp", None),
        P("fsdp", None),
        P("fsdp", None),
        P("rep", "fsdp", None),
    )
    return jax.shard_map(
        on_device,
        mesh=mesh,
        in_specs=placed,
        out_specs=(
            P(("rep", "fsdp"), None),
            P("fsdp", None),
            P("fsdp", None),
            P("fsdp", None),
            P("fsdp", None),
        ),
        check_vma=False,
    )
```

time: 776 us -> 183 us (0.24)
  waiting for transfers between devices: 729 us -> 62.1 us
  starting transfers between devices: 0.12 us -> 68.8 us
  Pallas kernels: 0 us -> 26.2 us
  matrix products: 19 us -> 0 us
  between operations: 13.8 us -> 1.43 us
  other arithmetic: 6.85 us -> 16.7 us
    reduce_scatter x1 -> x0, waiting for transfers between devices: 359 us -> none  [on_device(): lax.psum_scatter(lax.dot_general(tokens, cotangent, (((0,), (0,)), ((), (...]
    psum x1 -> x0, waiting for transfers between devices: 186 us -> none  [from_root(): return lax.psum(kept, axis)]
    all_gather x1 -> x0, waiting for transfers between devices: 184 us -> none  [on_device(): lax.all_gather(current, 'fsdp', axis=0, tiled=True)]
    ppermute x0 -> x37, starting transfers between devices: none -> 68.8 us  [send(): return lax.ppermute(value, AXES, pairs)]
    ppermute x0 -> x37, waiting for transfers between devices: none -> 62.1 us  [send(): return lax.ppermute(value, AXES, pairs)]
    pallas_call x0 -> x4, Pallas kernels: none -> 26.2 us  [the longest x2 12.9 us: input_gradient(): pl.pallas_call(kernel, out_shape=jax.ShapeDtypeStruct((384, 4 * width), B...]
    dot_general x2 -> x0, matrix products: 19 us -> none  [the longest x1 9.8 us: on_device(): lax.dot_general(cotangent, lax.all_gather(current, 'fsdp', axis=0, tiled=...]
  transfers between devices with their start and end apart: 3 -> 37, of which waited for: 3 -> 19; matrix products, arithmetic and copies ran while one was open for 1% -> 9% of each run, Pallas kernels for 0% -> 12%
where the time goes in v1:
time: 183 us; the launch traced here: 182 us
  starting transfers between devices  68.8 us (38%)
  waiting for transfers between devices  62.1 us (34%)
  Pallas kernels  26.2 us (14%)
  other arithmetic  16.7 us (9%)
  local copies, waits for them, and re-layouts  6.23 us (3%)
    ppermute x37, starting transfers between devices, send(): return lax.ppermute(value, AXES, pairs)  68.8 us
    ppermute x37, waiting for transfers between devices, send(): return lax.ppermute(value, AXES, pairs)  62.1 us
    pallas_call x2, Pallas kernels, input_gradient(): pl.pallas_call(kernel, out_shape=jax.ShapeDtypeStruct((384, 4 * width), B...  12.9 us
    pallas_call x1, Pallas kernels, chip_gradient(): pl.pallas_call(grad_kernel, out_shape=(part, part), grid_spec=pltpu.Prefe...  9.22 us
    another operation x12, other arithmetic, double(): pair = jnp.stack([value, send(value, partner(axis, False))])  6.06 us
    concatenate x3, other arithmetic, double(): return jnp.concatenate([pair, send(pair, partner(axis, True))])  4.17 us
    pallas_call x1, Pallas kernels, mates_half(): pl.pallas_call(half_kernel, out_shape=jax.ShapeDtypeStruct((384, 2048), B...  4.11 us
  transfers between devices with their start and end apart: 37, of which 19 were waited for; matrix products, arithmetic and copies ran while one was open for 9% of the time, Pallas kernels for 12%

profile of v1, /device:TPU:1, one launch (start us, length us, event | category | flops | bytes accessed | tf_op | source)
XLA Modules:
  0.0 181.5 jit_solution(14410288115235333737)
XLA Ops:
  0.7 4.1 %shard_map.103 = bf16[384,2048]{1,0:T(8,128)(2,1)} custom-call(s32[1]{0:T(128)} %bitcast.s_ref, bf16[384,4096]{1,0:T(8,128)(2,1)} %t_ref.3), custom_call_target="tpu_custom_call" | custom-call | bytes 6291456 | tf_op jit(solution)/shard_map/pallas_call | solution.py:102
  4.8 3.2 %collective-permute-start.20 = (bf16[384,2048]{1,0:T(8,128)(2,1)}, bf16[384,2048]{1,0:T(8,128)(2,1)S(1)}, u32[]{:S(2)}, u32[]{:S(2)}) collective-permute-start(bf16[384,2048]{1,0:T(8,128)(2,1)} %shard_map.103), channel_id=1, source_target_pairs={{0,16},{1,17},{2,18},{3,19},{4,20},{5,21},{6,22},{7,23},{8,24},{9,... | collective-permute-start | bytes 4718600 | tf_op jit(solution)/shard_map/ppermute | solution.py:35
  8.1 0.7 collective-permute-start.6
  8.8 0.7 collective-permute-start.7
  9.4 0.7 collective-permute-start.8
  10.3 2.8 %collective-permute-done = bf16[32,640]{1,0:T(8,128)(2,1)S(1)} collective-permute-done((bf16[32,640]{1,0:T(8,128)(2,1)S(1)}, bf16[32,640]{1,0:T(8,128)(2,1)S(1)}, u32[]{:S(2)}, u32[]{:S(2)}) %collective-permute-start) | collective-permute-done | bytes 40992 | tf_op jit(solution)/shard_map/ppermute | solution.py:35
  13.1 0.8 collective-permute-start.1
  14.0 4.1 %collective-permute-done.1 = bf16[2,32,640]{2,1,0:T(8,128)(2,1)S(1)} collective-permute-done((bf16[2,32,640]{2,1,0:T(8,128)(2,1)S(1)}, bf16[2,32,640]{2,1,0:T(8,128)(2,1)S(1)}, u32[]{:S(2)}, u32[]{:S(2)}) %collective-permute-start.1) | collective-permute-done | bytes 81952 | tf_op jit(solution)/shard_map/ppermute | solution.py:35
  18.2 0.8 collective-permute-start.11
  19.0 1.3 collective-permute-start.9
  20.3 0.7 collective-permute-start.10
  21.0 1.7 collective-permute-done.2
  22.7 3.3 %collective-permute-start.3 = (bf16[2,4,32,640]{3,2,1,0:T(8,128)(2,1)S(1)}, bf16[2,4,32,640]{3,2,1,0:T(8,128)(2,1)S(1)}, u32[]{:S(2)}, u32[]{:S(2)}) collective-permute-start(bf16[2,4,32,640]{3,2,1,0:T(8,128)(2,1)S(1)} %pad_maximum_fusion.9), channel_id=1, source_target_pairs={{0,1},{1,0},{2,3},{3,2},{4,5},{5,4},{6,7},{7,6},{8,9},{9,8},{10,11... | collective-permute-start | bytes 983048 | tf_op jit(solution)/shard_map/ppermute | solution.py:35
  26.0 2.0 %collective-permute-done.9 = bf16[32,384]{1,0:T(8,128)(2,1)S(1)} collective-permute-done((bf16[32,384]{1,0:T(8,128)(2,1)S(1)}, bf16[32,384]{1,0:T(8,128)(2,1)S(1)}, u32[]{:S(2)}, u32[]{:S(2)}) %collective-permute-start.9) | collective-permute-done | bytes 24608 | tf_op jit(solution)/shard_map/ppermute | solution.py:35
  28.1 3.0 %collective-permute-done.12 = bf16[32,384]{1,0:T(8,128)(2,1)S(1)} collective-permute-done((bf16[32,384]{1,0:T(8,128)(2,1)S(1)}, bf16[32,384]{1,0:T(8,128)(2,1)S(1)}, u32[]{:S(2)}, u32[]{:S(2)}) %collective-permute-start.12) | collective-permute-done | bytes 24608 | tf_op jit(solution)/shard_map/ppermute | solution.py:35
  31.1 2.6 %collective-permute-start.13 = (bf16[2,32,384]{2,1,0:T(8,128)(2,1)S(1)}, bf16[2,32,384]{2,1,0:T(8,128)(2,1)S(1)}, u32[]{:S(2)}, u32[]{:S(2)}) collective-permute-start(bf16[2,32,384]{2,1,0:T(8,128)(2,1)S(1)} %pad_maximum_fusion.20), channel_id=1, source_target_pairs={{0,4},{1,5},{2,6},{3,7},{4,0},{5,1},{6,2},{7,3},{8,12},{9,13},{10,... | collective-permute-start | bytes 147464 | tf_op jit(solution)/shard_map/ppermute | solution.py:35
  33.7 1.2 fusion.46
  34.8 1.0 collective-permute-start.4
  35.8 6.6 %collective-permute-start.18 = (bf16[384,1024]{1,0:T(8,128)(2,1)S(1)}, bf16[384,1024]{1,0:T(8,128)(2,1)S(1)}, u32[]{:S(2)}, u32[]{:S(2)}) collective-permute-start(bf16[384,1024]{1,0:T(8,128)(2,1)S(1)} %copy-done.6), channel_id=1, source_target_pairs={{0,16},{1,17},{2,18},{3,19},{4,20},{5,21},{6,22},{7,23},{8,24},{9,... | collective-permute-start | bytes 2359304 | tf_op jit(solution)/shard_map/ppermute | solution.py:35
  42.5 3.5 %collective-permute-done.14 = bf16[4,32,384]{2,1,0:T(8,128)(2,1)S(1)} collective-permute-done((bf16[4,32,384]{2,1,0:T(8,128)(2,1)S(1)}, bf16[4,32,384]{2,1,0:T(8,128)(2,1)S(1)}, u32[]{:S(2)}, u32[]{:S(2)}) %collective-permute-start.14) | collective-permute-done | bytes 98336 | tf_op jit(solution)/shard_map/ppermute | solution.py:35
  46.0 0.7 pad_maximum_fusion.13
  46.7 3.4 %collective-permute-start.15 = (bf16[2,4,32,384]{3,2,1,0:T(8,128)(2,1)}, bf16[2,4,32,384]{3,2,1,0:T(8,128)(2,1)S(1)}, u32[]{:S(2)}, u32[]{:S(2)}) collective-permute-start(bf16[2,4,32,384]{3,2,1,0:T(8,128)(2,1)} %pad_maximum_fusion.13), channel_id=1, source_target_pairs={{0,64},{1,65},{2,66},{3,67},{4,68},{5,69},{6,70},{7,71},{8,72},{9,... | collective-permute-start | bytes 589832 | tf_op jit(solution)/shard_map/ppermute | solution.py:35
  50.1 5.8 %collective-permute-done.15 = bf16[2,4,32,384]{3,2,1,0:T(8,128)(2,1)S(1)} collective-permute-done((bf16[2,4,32,384]{3,2,1,0:T(8,128)(2,1)}, bf16[2,4,32,384]{3,2,1,0:T(8,128)(2,1)S(1)}, u32[]{:S(2)}, u32[]{:S(2)}) %collective-permute-start.15) | collective-permute-done | bytes 196640 | tf_op jit(solution)/shard_map/ppermute | solution.py:35
  56.0 1.2 collective-permute-start.16
  57.2 2.3 %pad_maximum_fusion.2 = bf16[2,4,4,32,640]{4,3,2,1,0:T(8,128)(2,1)} fusion(bf16[1,4,4,32,640]{4,3,2,1,0:T(8,128)(2,1)} %bitcast.18, bf16[1,4,4,32,640]{4,3,2,1,0:T(8,128)(2,1)S(1)} %copy-done.9), kind=kLoop, calls=%fused_computation.2 | loop fusion | flops 655360 | bytes 2621440 | tf_op jit(solution)/shard_map/stack | solution.py:81
  59.5 9.2 %shard_map.104 = (f32[4,16,128,128]{3,2,1,0:T(8,128)S(1)}, f32[4,16,128,128]{3,2,1,0:T(8,128)S(1)}) custom-call(s32[1]{0:T(128)} %bitcast.s_ref, bf16[384,4096]{1,0:T(8,128)(2,1)S(1)} %copy-done.2, bf16[384,2048]{1,0:T(8,128)(2,1)S(1)} %collective-permute-done.20.u_ref, bf16[384,1024]{1,0:T(8,128)(2,1)S(1)} %copy-done.6, ...), custom_call_target="tpu_custom_call" | custom-call | flops 3221225472 | bytes 14680064 | tf_op jit(solution)/shard_map/pallas_call | solution.py:127
  69.1 2.4 %collective-permute-start.21 = (bf16[2,4,4,128,128]{4,3,2,1,0:T(8,128)(2,1)S(1)}, bf16[2,4,4,128,128]{4,3,2,1,0:T(8,128)(2,1)S(1)}, u32[]{:S(2)}, u32[]{:S(2)}) collective-permute-start(bf16[2,4,4,128,128]{4,3,2,1,0:T(8,128)(2,1)S(1)} %pad_maximum_fusion.3), channel_id=1, source_target_pairs={{0,4},{1,5},{2,6},{3,7},{4,0},{5,1},{6,2},{7,3},{8,12},{9,13},{10,... | collective-permute-start | bytes 3145736 | tf_op jit(solution)/shard_map/ppermute | solution.py:35
  71.7 1.1 pad_maximum_fusion.4
  72.8 3.0 %collective-permute-start.27 = (bf16[2,4,4,128,128]{4,3,1,2,0:T(8,128)(2,1)}, bf16[2,4,4,128,128]{4,3,1,2,0:T(8,128)(2,1)}, u32[]{:S(2)}, u32[]{:S(2)}) collective-permute-start(bf16[2,4,4,128,128]{4,3,1,2,0:T(8,128)(2,1)} %pad_maximum_fusion.4), channel_id=1, source_target_pairs={{0,1},{1,0},{2,3},{3,2},{4,5},{5,4},{6,7},{7,6},{8,9},{9,8},{10,11... | collective-permute-start | bytes 3145736 | tf_op jit(solution)/shard_map/ppermute | solution.py:35
  75.8 1.0 pad_maximum_fusion.5
  76.8 1.9 %constant_dynamic-slice_fusion.2 = (f32[4,4,1,128,128]{4,3,2,1,0:T(8,128)S(1)}, f32[4,4,1,128,128]{4,3,2,1,0:T(8,128)S(1)}) fusion(f32[4,4,4,128,128]{4,3,2,1,0:T(8,128)} %bitcast.219, s32[]{:T(128)S(6)} %select_n.383, s32[]{:T(128)S(6)} %select_n.380), kind=kLoop, calls=%fused_computation.122 | loop fusion | bytes 4194312 | tf_op jit(solution)/shard_map/jit(dynamic_index_in_dim)/dynamic_slice | solution.py:65
  78.8 5.2 %collective-permute-done.21 = bf16[2,4,4,128,128]{4,3,2,1,0:T(8,128)(2,1)S(1)} collective-permute-done((bf16[2,4,4,128,128]{4,3,2,1,0:T(8,128)(2,1)S(1)}, bf16[2,4,4,128,128]{4,3,2,1,0:T(8,128)(2,1)S(1)}, u32[]{:S(2)}, u32[]{:S(2)}) %collective-permute-start.21) | collective-permute-done | bytes 1048608 | tf_op jit(solution)/shard_map/ppermute | solution.py:35
  84.2 1.5 collective-permute-start.22
  85.7 11.0 %collective-permute-done.17 = bf16[2,4,4,32,384]{4,3,2,1,0:T(8,128)(2,1)} collective-permute-done((bf16[2,4,4,32,384]{4,3,2,1,0:T(8,128)(2,1)}, bf16[2,4,4,32,384]{4,3,2,1,0:T(8,128)(2,1)}, u32[]{:S(2)}, u32[]{:S(2)}) %collective-permute-start.17) | collective-permute-done | bytes 786464 | tf_op jit(solution)/shard_map/ppermute | solution.py:35
  96.7 1.3 pad_maximum_fusion.1.r_ref
  98.1 1.7 fusion
  99.9 1.9 %pad_maximum_fusion.w_ref = bf16[4,4,4,32,640]{4,3,2,1,0:T(8,128)(2,1)S(1)} fusion(bf16[2,4,4,32,640]{4,3,2,1,0:T(8,128)(2,1)} %collective-permute-done.5, bf16[1,4,4,32,640]{4,3,2,1,0:T(8,128)(2,1)} %bitcast.18, bf16[1,4,4,32,640]{4,3,2,1,0:T(8,128)(2,1)S(1)} %copy-done.10), kind=kLoop, calls=%fused_computation | loop fusion | flops 2621440 | bytes 5242880 | tf_op jit(solution)/shard_map/concatenate | solution.py:82
  102.0 2.0 %collective-permute-start.23 = (bf16[2,4,128,128]{3,2,1,0:T(8,128)(2,1)S(1)}, bf16[2,4,128,128]{3,2,1,0:T(8,128)(2,1)S(1)}, u32[]{:S(2)}, u32[]{:S(2)}) collective-permute-start(bf16[2,4,128,128]{3,2,1,0:T(8,128)(2,1)S(1)} %pad_maximum_fusion.10), channel_id=1, source_target_pairs={{0,64},{1,65},{2,66},{3,67},{4,68},{5,69},{6,70},{7,71},{8,72},{9,... | collective-permute-start | bytes 786440 | tf_op jit(solution)/shard_map/ppermute | solution.py:35
  104.0 5.7 %collective-permute-done.28 = bf16[4,4,128,128]{3,2,0,1:T(8,128)(2,1)S(1)} collective-permute-done((bf16[4,4,128,128]{3,2,0,1:T(8,128)(2,1)S(1)}, bf16[4,4,128,128]{3,2,0,1:T(8,128)(2,1)S(1)}, u32[]{:S(2)}, u32[]{:S(2)}) %collective-permute-start.28) | collective-permute-done | bytes 524320 | tf_op jit(solution)/shard_map/ppermute | solution.py:35
  109.7 1.3 fusion.1
  111.1 2.5 %collective-permute-start.29 = (bf16[2,4,128,128]{3,2,1,0:T(8,128)(2,1)S(1)}, bf16[2,4,128,128]{3,2,1,0:T(8,128)(2,1)S(1)}, u32[]{:S(2)}, u32[]{:S(2)}) collective-permute-start(bf16[2,4,128,128]{3,2,1,0:T(8,128)(2,1)S(1)} %pad_maximum_fusion.11), channel_id=1, source_target_pairs={{0,4},{1,5},{2,6},{3,7},{4,0},{5,1},{6,2},{7,3},{8,12},{9,13},{10,... | collective-permute-start | bytes 786440 | tf_op jit(solution)/shard_map/ppermute | solution.py:35
  113.6 5.8 %shard_map.101 = bf16[384,2048]{1,0:T(8,128)(2,1)} custom-call(s32[13]{0:T(128)S(1)} %stack.182.s_ref, bf16[384,1024]{1,0:T(8,128)(2,1)S(1)} %copy-done.8, bf16[4,4,4,32,640]{4,3,2,1,0:T(8,128)(2,1)S(1)} %pad_maximum_fusion.w_ref, bf16[4,4,4,32,384]{4,3,2,1,0:T(8,128)(2,1)S(1)} %pad_maximum_fusion.1.r_ref), custom_call_target="tpu_custom_call" | custom-call | flops 1610612736 | bytes 7340032 | tf_op jit(solution)/shard_map/pallas_call | solution.py:176
  119.4 10.5 %collective-permute-start.19 = (bf16[384,2048]{1,0:T(8,128)(2,1)}, bf16[384,2048]{1,0:T(8,128)(2,1)}, u32[]{:S(2)}, u32[]{:S(2)}) collective-permute-start(bf16[384,2048]{1,0:T(8,128)(2,1)} %shard_map.101), channel_id=1, source_target_pairs={{0,16},{1,17},{2,18},{3,19},{4,20},{5,21},{6,22},{7,23},{8,24},{9,... | collective-permute-start | bytes 4718600 | tf_op jit(solution)/shard_map/ppermute | solution.py:35
  130.0 4.9 %collective-permute-start.24 = (bf16[4,128,128]{2,1,0:T(8,128)(2,1)S(1)}, bf16[4,128,128]{2,1,0:T(8,128)(2,1)S(1)}, u32[]{:S(2)}, u32[]{:S(2)}) collective-permute-start(bf16[4,128,128]{2,1,0:T(8,128)(2,1)S(1)} %fusion.12), channel_id=1, source_target_pairs={{0,192},{1,193},{2,194},{3,195},{4,196},{5,197},{6,198},{7,199},{8... | collective-permute-start | bytes 393224 | tf_op jit(solution)/shard_map/ppermute | solution.py:35
  135.0 2.2 %collective-permute-done.24 = bf16[4,128,128]{2,1,0:T(8,128)(2,1)S(1)} collective-permute-done((bf16[4,128,128]{2,1,0:T(8,128)(2,1)S(1)}, bf16[4,128,128]{2,1,0:T(8,128)(2,1)S(1)}, u32[]{:S(2)}, u32[]{:S(2)}) %collective-permute-start.24) | collective-permute-done | bytes 131104 | tf_op jit(solution)/shard_map/ppermute | solution.py:35
  137.4 1.4 collective-permute-done.30
  139.0 3.4 %collective-permute-done.25 = f32[2,128,128]{2,1,0:T(8,128)S(1)} collective-permute-done((f32[2,128,128]{2,1,0:T(8,128)S(1)}, f32[2,128,128]{2,1,0:T(8,128)S(1)}, u32[]{:S(2)}, u32[]{:S(2)}) %collective-permute-start.25) | collective-permute-done | bytes 131104 | tf_op jit(solution)/shard_map/ppermute | solution.py:35
  142.5 1.5 collective-permute-done.31
  144.4 1.2 collective-permute-done.26
  145.7 1.6 collective-permute-done.32
  147.3 5.7 %collective-permute-start.33 = (bf16[2,128,128]{2,1,0:T(8,128)(2,1)S(1)}, bf16[2,128,128]{2,1,0:T(8,128)(2,1)S(1)}, u32[]{:S(2)}, u32[]{:S(2)}) collective-permute-start(bf16[2,128,128]{2,1,0:T(8,128)(2,1)S(1)} %pad_maximum_fusion.19), channel_id=1, source_target_pairs={{0,32},{1,33},{2,34},{3,35},{4,36},{5,37},{6,38},{7,39},{8,40},{9,... | collective-permute-start | bytes 196616 | tf_op jit(solution)/shard_map/ppermute | solution.py:35
  153.0 1.7 collective-permute-done.33
  154.6 0.9 collective-permute-start.34
  155.6 3.0 %collective-permute-done.34 = f32[2,128,128]{2,1,0:T(8,128)S(1)} collective-permute-done((f32[2,128,128]{2,1,0:T(8,128)S(1)}, f32[2,128,128]{2,1,0:T(8,128)S(1)}, u32[]{:S(2)}, u32[]{:S(2)}) %collective-permute-start.34) | collective-permute-done | bytes 131104 | tf_op jit(solution)/shard_map/ppermute | solution.py:35
  158.6 0.7 copy-done.17
  159.2 0.7 pad_maximum_fusion.12
  159.9 1.4 collective-permute-start.35
  161.3 1.4 copy-done.1
  162.7 7.1 %shard_map.102 = bf16[384,4096]{1,0:T(8,128)(2,1)} custom-call(s32[13]{0:T(128)S(1)} %stack.182.s_ref, bf16[384,1024]{1,0:T(8,128)(2,1)S(1)} %copy-done.6, bf16[4,4,4,32,640]{4,3,2,1,0:T(8,128)(2,1)S(1)} %pad_maximum_fusion.w_ref, bf16[4,4,4,32,384]{4,3,2,1,0:T(8,128)(2,1)S(1)} %copy-done.1, bf16[384,2048]{1,0:T(8,128)(2,1)} %collective-permute-done.19.got_ref), custom_call_target="tpu_custom_call" | custom-call | flops 1610612736 | bytes 7340032 | tf_op jit(solution)/shard_map/pallas_call | solution.py:176
  169.8 1.0 pad_maximum_fusion.7
  170.8 6.0 %collective-permute-start.36 = (f32[4,2,128,128]{3,2,1,0:T(8,128)S(1)}, f32[4,2,128,128]{3,2,1,0:T(8,128)S(1)}, u32[]{:S(2)}, u32[]{:S(2)}) collective-permute-start(f32[4,2,128,128]{3,2,1,0:T(8,128)S(1)} %pad_maximum_fusion.7), channel_id=1, source_target_pairs={{0,16},{1,17},{2,18},{3,19},{4,20},{5,21},{6,22},{7,23},{8,24},{9,... | collective-permute-start | bytes 1572872 | tf_op jit(solution)/shard_map/ppermute | solution.py:35
  176.9 1.4 collective-permute-done.36
  178.7 0.8 slice.185
  180.0 1.5 add_divide_fusion
  (126 shorter events, 3.9 us)
Async XLA Ops:
  0.6 7.4 %copy-start.19 = (f32[1,256,384]{2,1,0:T(8,128)S(1)}, f32[1,256,384]{2,1,0:T(8,128)}, u32[]{:S(2)}) copy-start(f32[1,256,384]{2,1,0:T(8,128)} %param.11) | copy-start | bytes 1179652
  0.7 7.4 %copy-start.20 = (bf16[256,1024]{1,0:T(8,128)(2,1)S(1)}, bf16[256,1024]{1,0:T(8,128)(2,1)}, u32[]{:S(2)}) copy-start(bf16[256,1024]{1,0:T(8,128)(2,1)} %param.8) | copy-start | bytes 1572868
  4.8 54.8 %collective-permute-start.20 = (bf16[384,2048]{1,0:T(8,128)(2,1)}, bf16[384,2048]{1,0:T(8,128)(2,1)S(1)}, u32[]{:S(2)}, u32[]{:S(2)}) collective-permute-start(bf16[384,2048]{1,0:T(8,128)(2,1)} %shard_map.103), channel_id=1, source_target_pairs={{0,16},{1,17},{2,18},{3,19},{4,20},{5,21},{6,22},{7,23},{8,24},{9,... | collective-permute-start | bytes 4718600 | tf_op jit(solution)/shard_map/ppermute | solution.py:35
  8.1 5.8 %collective-permute-start.6 = (bf16[2,32,384]{2,1,0:T(8,128)(2,1)S(1)}, bf16[2,32,384]{2,1,0:T(8,128)(2,1)S(1)}, u32[]{:S(2)}, u32[]{:S(2)}) collective-permute-start(bf16[2,32,384]{2,1,0:T(8,128)(2,1)S(1)} %get-tuple-element.34), channel_id=1, source_target_pairs={{0,64},{1,65},{2,66},{3,67},{4,68},{5,69},{6,70},{7,71},{8,72},{9,... | collective-permute-start | bytes 147464 | tf_op jit(solution)/shard_map/ppermute | solution.py:35
  8.8 5.2 %collective-permute-start.7 = (bf16[2,32,384]{2,1,0:T(8,128)(2,1)S(1)}, bf16[2,32,384]{2,1,0:T(8,128)(2,1)S(1)}, u32[]{:S(2)}, u32[]{:S(2)}) collective-permute-start(bf16[2,32,384]{2,1,0:T(8,128)(2,1)S(1)} %get-tuple-element.33), channel_id=1, source_target_pairs={{0,128},{1,129},{2,130},{3,131},{4,132},{5,133},{6,134},{7,135},{8... | collective-permute-start | bytes 147464 | tf_op jit(solution)/shard_map/ppermute | solution.py:35
  9.4 4.5 %collective-permute-start.8 = (bf16[2,32,384]{2,1,0:T(8,128)(2,1)S(1)}, bf16[2,32,384]{2,1,0:T(8,128)(2,1)S(1)}, u32[]{:S(2)}, u32[]{:S(2)}) collective-permute-start(bf16[2,32,384]{2,1,0:T(8,128)(2,1)S(1)} %get-tuple-element.32), channel_id=1, source_target_pairs={{0,192},{1,193},{2,194},{3,195},{4,196},{5,197},{6,198},{7,199},{8... | collective-permute-start | bytes 147464 | tf_op jit(solution)/shard_map/ppermute | solution.py:35
  10.2 2.9 %collective-permute-start = (bf16[32,640]{1,0:T(8,128)(2,1)S(1)}, bf16[32,640]{1,0:T(8,128)(2,1)S(1)}, u32[]{:S(2)}, u32[]{:S(2)}) collective-permute-start(bf16[32,640]{1,0:T(8,128)(2,1)S(1)} %constant_dynamic-slice_fusion.8), channel_id=1, source_target_pairs={{0,12},{1,13},{2,14},{3,15},{4,8},{5,9},{6,10},{7,11},{8,4},{9,5},... | collective-permute-start | bytes 122888 | tf_op jit(solution)/shard_map/ppermute | solution.py:35
  13.1 4.9 %collective-permute-start.1 = (bf16[2,32,640]{2,1,0:T(8,128)(2,1)S(1)}, bf16[2,32,640]{2,1,0:T(8,128)(2,1)S(1)}, u32[]{:S(2)}, u32[]{:S(2)}) collective-permute-start(bf16[2,32,640]{2,1,0:T(8,128)(2,1)S(1)} %pad_maximum_fusion.18), channel_id=1, source_target_pairs={{0,4},{1,5},{2,6},{3,7},{4,0},{5,1},{6,2},{7,3},{8,12},{9,13},{10,... | collective-permute-start | bytes 245768 | tf_op jit(solution)/shard_map/ppermute | solution.py:35
  18.1 17.8 %copy-start.6 = (bf16[384,1024]{1,0:T(8,128)(2,1)S(1)}, bf16[384,1024]{1,0:T(8,128)(2,1)}, u32[]{:S(2)}) copy-start(bf16[384,1024]{1,0:T(8,128)(2,1)} %c_ref.1) | copy-start | bytes 2359300
  18.1 4.6 %collective-permute-start.2 = (bf16[4,32,640]{2,1,0:T(8,128)(2,1)S(1)}, bf16[4,32,640]{2,1,0:T(8,128)(2,1)S(1)}, u32[]{:S(2)}, u32[]{:S(2)}) collective-permute-start(bf16[4,32,640]{2,1,0:T(8,128)(2,1)S(1)} %get-tuple-element.36), channel_id=1, source_target_pairs={{0,35},{1,2},{2,1},{3,32},{4,39},{5,6},{6,5},{7,36},{8,43},{9,10},... | collective-permute-start | bytes 491528 | tf_op jit(solution)/shard_map/ppermute | solution.py:35
  18.2 7.8 %collective-permute-start.11 = (bf16[32,384]{1,0:T(8,128)(2,1)S(1)}, bf16[32,384]{1,0:T(8,128)(2,1)S(1)}, u32[]{:S(2)}, u32[]{:S(2)}) collective-permute-start(bf16[32,384]{1,0:T(8,128)(2,1)S(1)} %get-tuple-element.41), channel_id=1, source_target_pairs={{0,48},{1,49},{2,50},{3,51},{4,52},{5,53},{6,54},{7,55},{8,56},{9,... | collective-permute-start | bytes 73736 | tf_op jit(solution)/shard_map/ppermute | solution.py:35
  19.0 9.0 %collective-permute-start.9 = (bf16[32,384]{1,0:T(8,128)(2,1)S(1)}, bf16[32,384]{1,0:T(8,128)(2,1)S(1)}, u32[]{:S(2)}, u32[]{:S(2)}) collective-permute-start(bf16[32,384]{1,0:T(8,128)(2,1)S(1)} %get-tuple-element.41), channel_id=1, source_target_pairs={{0,16},{1,17},{2,18},{3,19},{4,20},{5,21},{6,22},{7,23},{8,24},{9,... | collective-permute-start | bytes 73736 | tf_op jit(solution)/shard_map/ppermute | solution.py:35
  20.3 5.7 %collective-permute-start.10 = (bf16[32,384]{1,0:T(8,128)(2,1)S(1)}, bf16[32,384]{1,0:T(8,128)(2,1)S(1)}, u32[]{:S(2)}, u32[]{:S(2)}) collective-permute-start(bf16[32,384]{1,0:T(8,128)(2,1)S(1)} %get-tuple-element.42), channel_id=1, source_target_pairs={{0,32},{1,33},{2,34},{3,35},{4,36},{5,37},{6,38},{7,39},{8,40},{9,... | collective-permute-start | bytes 73736 | tf_op jit(solution)/shard_map/ppermute | solution.py:35
  22.7 11.0 %collective-permute-start.3 = (bf16[2,4,32,640]{3,2,1,0:T(8,128)(2,1)S(1)}, bf16[2,4,32,640]{3,2,1,0:T(8,128)(2,1)S(1)}, u32[]{:S(2)}, u32[]{:S(2)}) collective-permute-start(bf16[2,4,32,640]{3,2,1,0:T(8,128)(2,1)S(1)} %pad_maximum_fusion.9), channel_id=1, source_target_pairs={{0,1},{1,0},{2,3},{3,2},{4,5},{5,4},{6,7},{7,6},{8,9},{9,8},{10,11... | collective-permute-start | bytes 983048 | tf_op jit(solution)/shard_map/ppermute | solution.py:35
  28.0 3.1 %collective-permute-start.12 = (bf16[32,384]{1,0:T(8,128)(2,1)S(1)}, bf16[32,384]{1,0:T(8,128)(2,1)S(1)}, u32[]{:S(2)}, u32[]{:S(2)}) collective-permute-start(bf16[32,384]{1,0:T(8,128)(2,1)S(1)} %select_select_fusion), channel_id=1, source_target_pairs={{0,12},{1,13},{2,14},{3,15},{4,8},{5,9},{6,10},{7,11},{8,4},{9,5},... | collective-permute-start | bytes 73736 | tf_op jit(solution)/shard_map/ppermute | solution.py:35
  31.1 11.3 %collective-permute-start.13 = (bf16[2,32,384]{2,1,0:T(8,128)(2,1)S(1)}, bf16[2,32,384]{2,1,0:T(8,128)(2,1)S(1)}, u32[]{:S(2)}, u32[]{:S(2)}) collective-permute-start(bf16[2,32,384]{2,1,0:T(8,128)(2,1)S(1)} %pad_maximum_fusion.20), channel_id=1, source_target_pairs={{0,4},{1,5},{2,6},{3,7},{4,0},{5,1},{6,2},{7,3},{8,12},{9,13},{10,... | collective-permute-start | bytes 147464 | tf_op jit(solution)/shard_map/ppermute | solution.py:35
  34.8 22.4 %collective-permute-start.4 = (bf16[4,4,32,640]{3,2,1,0:T(8,128)(2,1)}, bf16[4,4,32,640]{3,2,1,0:T(8,128)(2,1)}, u32[]{:S(2)}, u32[]{:S(2)}) collective-permute-start(bf16[4,4,32,640]{3,2,1,0:T(8,128)(2,1)} %get-tuple-element.25), channel_id=1, source_target_pairs={{0,192},{1,193},{2,194},{3,195},{4,196},{5,197},{6,198},{7,199},{8... | collective-permute-start | bytes 1966088 | tf_op jit(solution)/shard_map/ppermute | solution.py:35
  35.8 23.7 %collective-permute-start.18 = (bf16[384,1024]{1,0:T(8,128)(2,1)S(1)}, bf16[384,1024]{1,0:T(8,128)(2,1)S(1)}, u32[]{:S(2)}, u32[]{:S(2)}) collective-permute-start(bf16[384,1024]{1,0:T(8,128)(2,1)S(1)} %copy-done.6), channel_id=1, source_target_pairs={{0,16},{1,17},{2,18},{3,19},{4,20},{5,21},{6,22},{7,23},{8,24},{9,... | collective-permute-start | bytes 2359304 | tf_op jit(solution)/shard_map/ppermute | solution.py:35
  42.4 3.6 %collective-permute-start.14 = (bf16[4,32,384]{2,1,0:T(8,128)(2,1)S(1)}, bf16[4,32,384]{2,1,0:T(8,128)(2,1)S(1)}, u32[]{:S(2)}, u32[]{:S(2)}) collective-permute-start(bf16[4,32,384]{2,1,0:T(8,128)(2,1)S(1)} %get-tuple-element.40), channel_id=1, source_target_pairs={{0,192},{1,193},{2,194},{3,195},{4,196},{5,197},{6,198},{7,199},{8... | collective-permute-start | bytes 294920 | tf_op jit(solution)/shard_map/ppermute | solution.py:35
  46.7 9.2 %collective-permute-start.15 = (bf16[2,4,32,384]{3,2,1,0:T(8,128)(2,1)}, bf16[2,4,32,384]{3,2,1,0:T(8,128)(2,1)S(1)}, u32[]{:S(2)}, u32[]{:S(2)}) collective-permute-start(bf16[2,4,32,384]{3,2,1,0:T(8,128)(2,1)} %pad_maximum_fusion.13), channel_id=1, source_target_pairs={{0,64},{1,65},{2,66},{3,67},{4,68},{5,69},{6,70},{7,71},{8,72},{9,... | collective-permute-start | bytes 589832 | tf_op jit(solution)/shard_map/ppermute | solution.py:35
  50.1 7.2 %copy-start.9 = (bf16[1,4,4,32,640]{4,3,2,1,0:T(8,128)(2,1)S(1)}, bf16[1,4,4,32,640]{4,3,2,1,0:T(8,128)(2,1)}, u32[]{:S(2)}) copy-start(bf16[1,4,4,32,640]{4,3,2,1,0:T(8,128)(2,1)} %get-tuple-element.24) | copy-start | bytes 1966084
  55.9 3.6 %copy-start.2 = (bf16[384,4096]{1,0:T(8,128)(2,1)S(1)}, bf16[384,4096]{1,0:T(8,128)(2,1)}, u32[]{:S(2)}) copy-start(bf16[384,4096]{1,0:T(8,128)(2,1)} %t_ref.3) | copy-start | bytes 9437188
  56.0 19.8 %copy-start.11 = (bf16[1,4,4,32,384]{4,3,2,1,0:T(8,128)(2,1)}, bf16[1,4,4,32,384]{4,3,2,1,0:T(8,128)(2,1)S(1)}, u32[]{:S(2)}) copy-start(bf16[1,4,4,32,384]{4,3,2,1,0:T(8,128)(2,1)S(1)} %get-tuple-element.26) | copy-start | bytes 1179652
  56.0 19.8 %collective-permute-start.16 = (bf16[4,4,32,384]{3,2,1,0:T(8,128)(2,1)S(1)}, bf16[4,4,32,384]{3,2,1,0:T(8,128)(2,1)S(1)}, u32[]{:S(2)}, u32[]{:S(2)}) collective-permute-start(bf16[4,4,32,384]{3,2,1,0:T(8,128)(2,1)S(1)} %get-tuple-element.27), channel_id=1, source_target_pairs={{0,35},{1,2},{2,1},{3,32},{4,39},{5,6},{6,5},{7,36},{8,43},{9,10},... | collective-permute-start | bytes 1179656 | tf_op jit(solution)/shard_map/ppermute | solution.py:35
  59.5 40.3 %collective-permute-start.5 = (bf16[2,4,4,32,640]{4,3,2,1,0:T(8,128)(2,1)}, bf16[2,4,4,32,640]{4,3,2,1,0:T(8,128)(2,1)}, u32[]{:S(2)}, u32[]{:S(2)}) collective-permute-start(bf16[2,4,4,32,640]{4,3,2,1,0:T(8,128)(2,1)} %pad_maximum_fusion.2), channel_id=1, source_target_pairs={{0,64},{1,65},{2,66},{3,67},{4,68},{5,69},{6,70},{7,71},{8,72},{9,... | collective-permute-start | bytes 3932168 | tf_op jit(solution)/shard_map/ppermute | solution.py:35
  59.5 9.3 %copy-start.7 = (bf16[384,1024]{1,0:T(8,128)(2,1)}, bf16[384,1024]{1,0:T(8,128)(2,1)S(1)}, u32[]{:S(2)}) copy-start(bf16[384,1024]{1,0:T(8,128)(2,1)S(1)} %collective-permute-done.18.cot_ref.d_ref) | copy-start | bytes 2359300
  68.8 2.7 %copy-start.3 = (f32[4,16,128,128]{3,2,1,0:T(8,128)}, f32[4,16,128,128]{3,2,1,0:T(8,128)S(1)}, u32[]{:S(2)}) copy-start(f32[4,16,128,128]{3,2,1,0:T(8,128)S(1)} %get-tuple-element.8) | copy-start | bytes 12582916
  68.8 4.0 %copy-start.4 = (f32[4,16,128,128]{3,2,1,0:T(8,128)}, f32[4,16,128,128]{3,2,1,0:T(8,128)S(1)}, u32[]{:S(2)}) copy-start(f32[4,16,128,128]{3,2,1,0:T(8,128)S(1)} %get-tuple-element.7) | copy-start | bytes 12582916
  69.1 14.9 %collective-permute-start.21 = (bf16[2,4,4,128,128]{4,3,2,1,0:T(8,128)(2,1)S(1)}, bf16[2,4,4,128,128]{4,3,2,1,0:T(8,128)(2,1)S(1)}, u32[]{:S(2)}, u32[]{:S(2)}) collective-permute-start(bf16[2,4,4,128,128]{4,3,2,1,0:T(8,128)(2,1)S(1)} %pad_maximum_fusion.3), channel_id=1, source_target_pairs={{0,4},{1,5},{2,6},{3,7},{4,0},{5,1},{6,2},{7,3},{8,12},{9,13},{10,... | collective-permute-start | bytes 3145736 | tf_op jit(solution)/shard_map/ppermute | solution.py:35
  72.8 25.3 %collective-permute-start.27 = (bf16[2,4,4,128,128]{4,3,1,2,0:T(8,128)(2,1)}, bf16[2,4,4,128,128]{4,3,1,2,0:T(8,128)(2,1)}, u32[]{:S(2)}, u32[]{:S(2)}) collective-permute-start(bf16[2,4,4,128,128]{4,3,1,2,0:T(8,128)(2,1)} %pad_maximum_fusion.4), channel_id=1, source_target_pairs={{0,1},{1,0},{2,3},{3,2},{4,5},{5,4},{6,7},{7,6},{8,9},{9,8},{10,11... | collective-permute-start | bytes 3145736 | tf_op jit(solution)/shard_map/ppermute | solution.py:35
  76.7 20.0 %collective-permute-start.17 = (bf16[2,4,4,32,384]{4,3,2,1,0:T(8,128)(2,1)}, bf16[2,4,4,32,384]{4,3,2,1,0:T(8,128)(2,1)}, u32[]{:S(2)}, u32[]{:S(2)}) collective-permute-start(bf16[2,4,4,32,384]{4,3,2,1,0:T(8,128)(2,1)} %pad_maximum_fusion.5), channel_id=1, source_target_pairs={{0,1},{1,0},{2,3},{3,2},{4,5},{5,4},{6,7},{7,6},{8,9},{9,8},{10,11... | collective-permute-start | bytes 2359304 | tf_op jit(solution)/shard_map/ppermute | solution.py:35
  76.8 7.2 %copy-start.5 = (f32[4,16,128,128]{3,2,1,0:T(8,128)S(1)}, f32[4,16,128,128]{3,2,1,0:T(8,128)}, u32[]{:S(2)}) copy-start(f32[4,16,128,128]{3,2,1,0:T(8,128)} %copy-done.4) | copy-start | bytes 12582916
  78.8 17.9 %copy-start.12 = (bf16[1,4,4,32,384]{4,3,2,1,0:T(8,128)(2,1)S(1)}, bf16[1,4,4,32,384]{4,3,2,1,0:T(8,128)(2,1)}, u32[]{:S(2)}) copy-start(bf16[1,4,4,32,384]{4,3,2,1,0:T(8,128)(2,1)} %copy-done.11) | copy-start | bytes 1179652
  84.0 14.0 %copy-start.13 = (bf16[2,4,4,128,128]{4,3,2,1,0:T(8,128)(2,1)}, bf16[2,4,4,128,128]{4,3,2,1,0:T(8,128)(2,1)S(1)}, u32[]{:S(2)}) copy-start(bf16[2,4,4,128,128]{4,3,2,1,0:T(8,128)(2,1)S(1)} %collective-permute-done.21) | copy-start | bytes 3145732
  84.2 17.5 %collective-permute-start.22 = (bf16[4,4,128,128]{3,2,1,0:T(8,128)(2,1)S(1)}, bf16[4,4,128,128]{3,2,1,0:T(8,128)(2,1)S(1)}, u32[]{:S(2)}, u32[]{:S(2)}) collective-permute-start(bf16[4,4,128,128]{3,2,1,0:T(8,128)(2,1)S(1)} %fusion.2), channel_id=1, source_target_pairs={{0,12},{1,13},{2,14},{3,15},{4,8},{5,9},{6,10},{7,11},{8,4},{9,5},... | collective-permute-start | bytes 1572872 | tf_op jit(solution)/shard_map/ppermute | solution.py:35
  98.0 15.6 %copy-start = (bf16[4,4,4,32,384]{4,3,2,1,0:T(8,128)(2,1)}, bf16[4,4,4,32,384]{4,3,2,1,0:T(8,128)(2,1)S(1)}, u32[]{:S(2)}) copy-start(bf16[4,4,4,32,384]{4,3,2,1,0:T(8,128)(2,1)S(1)} %pad_maximum_fusion.1.r_ref) | copy-start | bytes 4718596
  98.0 1.8 %copy-start.10 = (bf16[1,4,4,32,640]{4,3,2,1,0:T(8,128)(2,1)S(1)}, bf16[1,4,4,32,640]{4,3,2,1,0:T(8,128)(2,1)}, u32[]{:S(2)}) copy-start(bf16[1,4,4,32,640]{4,3,2,1,0:T(8,128)(2,1)} %get-tuple-element.24) | copy-start | bytes 1966084
  99.7 2.0 %copy-start.14 = (bf16[2,4,4,128,128]{4,3,2,1,0:T(8,128)(2,1)S(1)}, bf16[2,4,4,128,128]{4,3,2,1,0:T(8,128)(2,1)}, u32[]{:S(2)}) copy-start(bf16[2,4,4,128,128]{4,3,2,1,0:T(8,128)(2,1)} %copy-done.13) | copy-start | bytes 3145732
  99.7 10.0 %collective-permute-start.28 = (bf16[4,4,128,128]{3,2,0,1:T(8,128)(2,1)S(1)}, bf16[4,4,128,128]{3,2,0,1:T(8,128)(2,1)S(1)}, u32[]{:S(2)}, u32[]{:S(2)}) collective-permute-start(bf16[4,4,128,128]{3,2,0,1:T(8,128)(2,1)S(1)} %fusion), channel_id=1, source_target_pairs={{0,35},{1,2},{2,1},{3,32},{4,39},{5,6},{6,5},{7,36},{8,43},{9,10},... | collective-permute-start | bytes 1572872 | tf_op jit(solution)/shard_map/ppermute | solution.py:35
  102.0 27.9 %collective-permute-start.23 = (bf16[2,4,128,128]{3,2,1,0:T(8,128)(2,1)S(1)}, bf16[2,4,128,128]{3,2,1,0:T(8,128)(2,1)S(1)}, u32[]{:S(2)}, u32[]{:S(2)}) collective-permute-start(bf16[2,4,128,128]{3,2,1,0:T(8,128)(2,1)S(1)} %pad_maximum_fusion.10), channel_id=1, source_target_pairs={{0,64},{1,65},{2,66},{3,67},{4,68},{5,69},{6,70},{7,71},{8,72},{9,... | collective-permute-start | bytes 786440 | tf_op jit(solution)/shard_map/ppermute | solution.py:35
  109.7 3.9 %copy-start.8 = (bf16[384,1024]{1,0:T(8,128)(2,1)S(1)}, bf16[384,1024]{1,0:T(8,128)(2,1)}, u32[]{:S(2)}) copy-start(bf16[384,1024]{1,0:T(8,128)(2,1)} %copy-done.7) | copy-start | bytes 2359300
  111.1 23.8 %collective-permute-start.29 = (bf16[2,4,128,128]{3,2,1,0:T(8,128)(2,1)S(1)}, bf16[2,4,128,128]{3,2,1,0:T(8,128)(2,1)S(1)}, u32[]{:S(2)}, u32[]{:S(2)}) collective-permute-start(bf16[2,4,128,128]{3,2,1,0:T(8,128)(2,1)S(1)} %pad_maximum_fusion.11), channel_id=1, source_target_pairs={{0,4},{1,5},{2,6},{3,7},{4,0},{5,1},{6,2},{7,3},{8,12},{9,13},{10,... | collective-permute-start | bytes 786440 | tf_op jit(solution)/shard_map/ppermute | solution.py:35
  119.4 41.9 %collective-permute-start.19 = (bf16[384,2048]{1,0:T(8,128)(2,1)}, bf16[384,2048]{1,0:T(8,128)(2,1)}, u32[]{:S(2)}, u32[]{:S(2)}) collective-permute-start(bf16[384,2048]{1,0:T(8,128)(2,1)} %shard_map.101), channel_id=1, source_target_pairs={{0,16},{1,17},{2,18},{3,19},{4,20},{5,21},{6,22},{7,23},{8,24},{9,... | collective-permute-start | bytes 4718600 | tf_op jit(solution)/shard_map/ppermute | solution.py:35
  130.0 7.2 %collective-permute-start.24 = (bf16[4,128,128]{2,1,0:T(8,128)(2,1)S(1)}, bf16[4,128,128]{2,1,0:T(8,128)(2,1)S(1)}, u32[]{:S(2)}, u32[]{:S(2)}) collective-permute-start(bf16[4,128,128]{2,1,0:T(8,128)(2,1)S(1)} %fusion.12), channel_id=1, source_target_pairs={{0,192},{1,193},{2,194},{3,195},{4,196},{5,197},{6,198},{7,199},{8... | collective-permute-start | bytes 393224 | tf_op jit(solution)/shard_map/ppermute | solution.py:35
  134.9 3.9 %collective-permute-start.30 = (bf16[4,128,128]{2,1,0:T(8,128)(2,1)S(1)}, bf16[4,128,128]{2,1,0:T(8,128)(2,1)S(1)}, u32[]{:S(2)}, u32[]{:S(2)}) collective-permute-start(bf16[4,128,128]{2,1,0:T(8,128)(2,1)S(1)} %fusion.10), channel_id=1, source_target_pairs={{0,12},{1,13},{2,14},{3,15},{4,8},{5,9},{6,10},{7,11},{8,4},{9,5},... | collective-permute-start | bytes 393224 | tf_op jit(solution)/shard_map/ppermute | solution.py:35
  137.3 5.1 %collective-permute-start.25 = (f32[2,128,128]{2,1,0:T(8,128)S(1)}, f32[2,128,128]{2,1,0:T(8,128)S(1)}, u32[]{:S(2)}, u32[]{:S(2)}) collective-permute-start(f32[2,128,128]{2,1,0:T(8,128)S(1)} %pad_maximum_fusion.15), channel_id=1, source_target_pairs={{0,1},{1,0},{2,3},{3,2},{4,5},{5,4},{6,7},{7,6},{8,9},{9,8},{10,11... | collective-permute-start | bytes 393224 | tf_op jit(solution)/shard_map/ppermute | solution.py:35
  138.9 5.1 %collective-permute-start.31 = (f32[2,128,128]{2,1,0:T(8,128)S(1)}, f32[2,128,128]{2,1,0:T(8,128)S(1)}, u32[]{:S(2)}, u32[]{:S(2)}) collective-permute-start(f32[2,128,128]{2,1,0:T(8,128)S(1)} %pad_maximum_fusion.16), channel_id=1, source_target_pairs={{0,64},{1,65},{2,66},{3,67},{4,68},{5,69},{6,70},{7,71},{8,72},{9,... | collective-permute-start | bytes 393224 | tf_op jit(solution)/shard_map/ppermute | solution.py:35
  142.4 3.2 %collective-permute-start.26 = (f32[128,128]{1,0:T(8,128)S(1)}, f32[128,128]{1,0:T(8,128)S(1)}, u32[]{:S(2)}, u32[]{:S(2)}) collective-permute-start(f32[128,128]{1,0:T(8,128)S(1)} %fusion.35), channel_id=1, source_target_pairs={{0,35},{1,2},{2,1},{3,32},{4,39},{5,6},{6,5},{7,36},{8,43},{9,10},... | collective-permute-start | bytes 196616 | tf_op jit(solution)/shard_map/ppermute | solution.py:35
  144.0 3.2 %collective-permute-start.32 = (f32[128,128]{1,0:T(8,128)S(1)}, f32[128,128]{1,0:T(8,128)S(1)}, u32[]{:S(2)}, u32[]{:S(2)}) collective-permute-start(f32[128,128]{1,0:T(8,128)S(1)} %fusion.31), channel_id=1, source_target_pairs={{0,192},{1,193},{2,194},{3,195},{4,196},{5,197},{6,198},{7,199},{8... | collective-permute-start | bytes 196616 | tf_op jit(solution)/shard_map/ppermute | solution.py:35
  147.3 7.4 %collective-permute-start.33 = (bf16[2,128,128]{2,1,0:T(8,128)(2,1)S(1)}, bf16[2,128,128]{2,1,0:T(8,128)(2,1)S(1)}, u32[]{:S(2)}, u32[]{:S(2)}) collective-permute-start(bf16[2,128,128]{2,1,0:T(8,128)(2,1)S(1)} %pad_maximum_fusion.19), channel_id=1, source_target_pairs={{0,32},{1,33},{2,34},{3,35},{4,36},{5,37},{6,38},{7,39},{8,40},{9,... | collective-permute-start | bytes 196616 | tf_op jit(solution)/shard_map/ppermute | solution.py:35
  154.6 3.9 %collective-permute-start.34 = (f32[2,128,128]{2,1,0:T(8,128)S(1)}, f32[2,128,128]{2,1,0:T(8,128)S(1)}, u32[]{:S(2)}, u32[]{:S(2)}) collective-permute-start(f32[2,128,128]{2,1,0:T(8,128)S(1)} %get-tuple-element.38), channel_id=1, source_target_pairs={{0,192},{1,193},{2,194},{3,195},{4,196},{5,197},{6,198},{7,199},{8... | collective-permute-start | bytes 393224 | tf_op jit(solution)/shard_map/ppermute | solution.py:35
  158.5 0.7 copy-start.17
  159.9 9.9 %collective-permute-start.35 = (f32[2,2,128,128]{3,2,1,0:T(8,128)}, f32[2,2,128,128]{3,2,1,0:T(8,128)}, u32[]{:S(2)}, u32[]{:S(2)}) collective-permute-start(f32[2,2,128,128]{3,2,1,0:T(8,128)} %pad_maximum_fusion.12), channel_id=1, source_target_pairs={{0,64},{1,65},{2,66},{3,67},{4,68},{5,69},{6,70},{7,71},{8,72},{9,... | collective-permute-start | bytes 786440 | tf_op jit(solution)/shard_map/ppermute | solution.py:35
  161.3 1.4 copy-start.1
  162.7 7.1 %copy-start.18 = (f32[2,128,128]{2,1,0:T(8,128)S(1)}, f32[2,128,128]{2,1,0:T(8,128)}, u32[]{:S(2)}) copy-start(f32[2,128,128]{2,1,0:T(8,128)} %copy-done.17) | copy-start | bytes 393220
  170.8 7.6 %collective-permute-start.36 = (f32[4,2,128,128]{3,2,1,0:T(8,128)S(1)}, f32[4,2,128,128]{3,2,1,0:T(8,128)S(1)}, u32[]{:S(2)}, u32[]{:S(2)}) collective-permute-start(f32[4,2,128,128]{3,2,1,0:T(8,128)S(1)} %pad_maximum_fusion.7), channel_id=1, source_target_pairs={{0,16},{1,17},{2,18},{3,19},{4,20},{5,21},{6,22},{7,23},{8,24},{9,... | collective-permute-start | bytes 1572872 | tf_op jit(solution)/shard_map/ppermute | solution.py:35
  178.6 1.1 copy-start.15
  178.6 1.4 copy-start.16

commit v2 on v0

v2 whole, which is shorter than its diff:
```python
import functools

import jax
import jax.numpy as jnp
from jax import lax
from jax.experimental import pallas as pl
from jax.experimental.pallas import tpu as pltpu
from jax.sharding import PartitionSpec as P

AXES = ("rep", "fsdp")
SIZES = {"y": 4, "zh": 2, "c": 2, "x": 4, "zl": 4}
HOST_PLACES = (
    (0, 1, 2, 3),
    (1, 0, 2, 3),
    (3, 2, 0, 1),
    (3, 2, 1, 0),
    (1, 0, 3, 2),
    (0, 1, 3, 2),
    (2, 3, 1, 0),
    (2, 3, 0, 1),
)
F32 = jnp.float32
BF16 = jnp.bfloat16


def unflatten(i):
    c = {}
    for name in ("zl", "x", "c", "zh", "y"):
        c[name] = i % SIZES[name]
        i //= SIZES[name]
    c["c"] ^= c["x"] + c["y"] + c["zl"] & 1
    return c


def flatten(c):
    c = dict(c, c=c["c"] ^ (c["x"] + c["y"] + c["zl"] & 1))
    i = 0
    for name in ("y", "zh", "c", "x", "zl"):
        i = i * SIZES[name] + c[name]
    return i


def send(value, route):
    pairs = []
    for i in range(256):
        target = route(unflatten(i))
        if target is not None:
            pairs.append((i, flatten(target)))
    return lax.ppermute(value, AXES, pairs)


def neighbour(axis, mask):
    def route(c):
        t = dict(c)
        t[axis] = c[axis] ^ mask
        if axis == "zl" and mask == 3 and c["zl"] in (0, 3):
            t["zh"] = 1 - c["zh"]
        return t

    return route


def partner(axis, first):
    def route(c):
        return neighbour(axis, 1 if (c["c"] == 0) == first else 3)(c)

    return route


def flip(axis):
    def route(c):
        t = dict(c)
        t[axis] = 1 - c[axis]
        return t

    return route


def where_am_i():
    rep, fsdp = lax.axis_index("rep"), lax.axis_index("fsdp")
    y, x, zl = rep // 4, fsdp // 4, fsdp % 4
    return {"y": y, "zh": rep // 2 % 2, "c": rep % 2 ^ (x + y + zl) % 2, "x": x, "zl": zl}


def ride(value, rider, route):
    rows = value.size // 128
    got = send(jnp.concatenate([value.reshape(rows, 128), rider]), route)
    return got[:rows].reshape(value.shape), got[rows:]


def together(*values):
    return lax.optimization_barrier(values)


def places(p, core):
    b = jnp.where(core == 0, 3, 1)
    out = []
    for j in range(4):
        r = p ^ j
        out.append(jnp.where(r == 0, 0, jnp.where(r == b, 1, jnp.where(r == 2, 3, 2))))
    return out


def orders(p, core):
    a = jnp.where(core == 0, 1, 3)
    return [p ^ 2, p ^ a, p ^ a ^ 2, p]


def chosen(s_ref, t_ref):
    cuts = [pl.multiple_of(s_ref[5 + k] * 256 + s_ref[0] * 128, 128) for k in range(4)]
    return jnp.concatenate([t_ref[:, pl.ds(cut, 128)] for cut in cuts], axis=1)


def columns(s_ref, c_ref, half, places):
    cuts = [pl.multiple_of(s_ref[9 + y] * 256 + half * 128, 128) for y in places]
    return jnp.concatenate([c_ref[:, pl.ds(cut, 128)] for cut in cuts], axis=1).T


def grad_kernel(keep, s_ref, t_hbm, u_hbm, c_hbm, d_hbm, one_ref, two_ref, t, u, c, d, sems):
    places = (2, 3) if keep else (0, 1)
    loads = [pltpu.make_async_copy(c_hbm, c, sems.at[0]), pltpu.make_async_copy(d_hbm, d, sems.at[1])]
    for i in range(4):
        cut = pl.ds(pl.multiple_of(s_ref[1 + i] * 1024, 1024), 1024)
        loads.append(pltpu.make_async_copy(t_hbm.at[:, cut], t.at[i], sems.at[2 + 2 * i]))
        loads.append(pltpu.make_async_copy(u_hbm.at[:, cut], u.at[i], sems.at[3 + 2 * i]))
    for load in loads:
        load.start()
    for load in loads[:2]:
        load.wait()
    one_cot = jnp.concatenate([columns(s_ref, r, 0, range(4)) for r in (c, d)], axis=1)
    two_cot = jnp.concatenate([columns(s_ref, r, 1, places) for r in (c, d)], axis=1)
    for i in range(4):
        for load in loads[2 + 2 * i : 4 + 2 * i]:
            load.wait()
        rows = jnp.concatenate([chosen(s_ref, r) for r in (t.at[i], u.at[i])], axis=0)
        if i in places:
            total = jnp.dot(one_cot, rows, preferred_element_type=F32).astype(one_ref.dtype)
            for y in range(4):
                for k in range(4):
                    one_ref[i - places[0], y, k] = total[y * 128 : y * 128 + 128, k * 128 : k * 128 + 128]
        total = jnp.dot(two_cot, rows, preferred_element_type=F32).astype(two_ref.dtype)
        for y in range(2):
            for k in range(4):
                two_ref[y, i, k] = total[y * 128 : y * 128 + 128, k * 128 : k * 128 + 128]


def chip_gradient(keep, order, tokens, their_tokens, cot, their_cot):
    dtype = F32 if keep else BF16
    vmem = pl.BlockSpec(memory_space=pltpu.VMEM)
    return pl.pallas_call(
        functools.partial(grad_kernel, keep),
        out_shape=(jax.ShapeDtypeStruct((2, 4, 4, 128, 128), dtype),) * 2,
        in_specs=[pl.BlockSpec(memory_space=pltpu.SMEM)] + [pl.BlockSpec(memory_space=pl.ANY)] * 4,
        out_specs=[vmem] * 2,
        scratch_shapes=[pltpu.VMEM((4, 384, 1024), BF16)] * 2
        + [pltpu.VMEM((384, 1024), BF16)] * 2
        + [pltpu.SemaphoreType.DMA((10,))],
        compiler_params=pltpu.CompilerParams(vmem_limit_bytes=56 << 20),
        cost_estimate=pl.CostEstimate(
            flops=768 * 2048 * 1024, bytes_accessed=9 << 20, transcendentals=0
        ),
    )(order, tokens, their_tokens, cot, their_cot)


def rows_kernel(s_ref, w_ref, d_ref, kept_ref, host_ref):
    mine = pl.ds(pl.multiple_of(s_ref[0] * 128, 128), 128)
    kept_ref[...] = w_ref[mine, :640].T
    host_ref[...] = (w_ref[:, 640:].astype(F32) + d_ref[0]).astype(BF16).T


def projection_rows(order, weight, delayed):
    vmem = pl.BlockSpec(memory_space=pltpu.VMEM)
    return pl.pallas_call(
        rows_kernel,
        out_shape=(jax.ShapeDtypeStruct((640, 128), BF16), jax.ShapeDtypeStruct((384, 256), BF16)),
        in_specs=[pl.BlockSpec(memory_space=pltpu.SMEM), vmem, vmem],
        out_specs=(vmem, vmem),
        compiler_params=pltpu.CompilerParams(vmem_limit_bytes=16 << 20),
        cost_estimate=pl.CostEstimate(flops=1 << 17, bytes_accessed=1 << 20, transcendentals=0),
    )(order, weight, delayed)


def product(s_ref, cot_ref, w_ref, r_ref, at):
    width = w_ref.shape[-2]
    kept = jnp.concatenate([w_ref[s_ref[5 + zl], at] for zl in range(4)], axis=1)
    host = jnp.concatenate([r_ref[at, s_ref[9 + zl]] for zl in range(4)], axis=1)
    total = jnp.dot(cot_ref[:, :width], kept, preferred_element_type=F32)
    total += jnp.dot(cot_ref[:, width:], host, preferred_element_type=F32)
    return total.astype(BF16)


def theirs_kernel(s_ref, cot_ref, w_ref, r_ref, o_ref):
    for x in range(4):
        at = s_ref[1 + x]
        o_ref[:, x * 512 : x * 512 + 512] = product(s_ref, cot_ref, w_ref, r_ref, at)


def ours_kernel(s_ref, cot_ref, w_ref, r_ref, got_ref, o_ref):
    core = s_ref[0]
    total = product(s_ref, cot_ref, w_ref, r_ref, s_ref[1 + pl.program_id(0)])
    for zl in range(4):
        mine = pl.multiple_of(zl * 256 + core * 128, 128)
        other = pl.multiple_of(zl * 256 + 128 - core * 128, 128)
        o_ref[:, pl.ds(mine, 128)] = total[:, zl * 128 : zl * 128 + 128]
        o_ref[:, pl.ds(other, 128)] = got_ref[:, zl * 128 : zl * 128 + 128]


def their_input_gradient(where, cot, kept, host):
    vmem = pl.BlockSpec(memory_space=pltpu.VMEM)
    return pl.pallas_call(
        theirs_kernel,
        out_shape=jax.ShapeDtypeStruct((384, 2048), BF16),
        in_specs=[pl.BlockSpec(memory_space=pltpu.SMEM), vmem, vmem, vmem],
        out_specs=vmem,
        compiler_params=pltpu.CompilerParams(vmem_limit_bytes=32 << 20),
        cost_estimate=pl.CostEstimate(
            flops=2 * 384 * 2048 * 1024, bytes_accessed=3 << 20, transcendentals=0
        ),
    )(where, cot, kept, host)


def our_input_gradient(where, cot, kept, host, got):
    vmem = pl.BlockSpec(memory_space=pltpu.VMEM)
    return pl.pallas_call(
        ours_kernel,
        out_shape=jax.ShapeDtypeStruct((384, 4096), BF16),
        grid=(4,),
        in_specs=[
            pl.BlockSpec(memory_space=pltpu.SMEM),
            vmem,
            vmem,
            vmem,
            pl.BlockSpec((384, 512), lambda x: (0, x)),
        ],
        out_specs=pl.BlockSpec((384, 1024), lambda x: (0, x)),
        compiler_params=pltpu.CompilerParams(vmem_limit_bytes=48 << 20),
        cost_estimate=pl.CostEstimate(
            flops=2 * 384 * 2048 * 1024, bytes_accessed=9 << 20, transcendentals=0
        ),
    )(where, cot, kept, host, got)


def finish_kernel(norm_factor, s_ref, mine_ref, other_ref, m_ref, v_ref, m_out, v_out, step_out, host_out):
    is_mine = pl.program_id(0) == s_ref[0]
    for tile in range(8):
        y, half = tile // 2, tile % 2
        cols = slice(tile * 128, tile * 128 + 128)
        grad = norm_factor * jnp.where(
            is_mine, mine_ref[s_ref[1 + y], half], other_ref[s_ref[5 + y], half]
        ).T
        if tile < 5:
            moment = 0.9 * m_ref[:, cols] + 0.1 * grad
            second = 0.95 * v_ref[:, cols] + 0.05 * grad * grad
            m_out[:, cols] = moment
            v_out[:, cols] = second
            step_out[:, cols] = (
                moment / (1.0 - 0.9**20) / (jnp.sqrt(second / (1.0 - 0.95**20)) + 1e-08)
            )
        else:
            host_out[:, tile * 128 - 640 : tile * 128 - 512] = grad


def finish(norm_factor, where, mine, other, moment, second):
    vmem = pl.BlockSpec(memory_space=pltpu.VMEM)
    wide = pl.BlockSpec((128, 640), lambda i: (i, 0))
    return pl.pallas_call(
        functools.partial(finish_kernel, norm_factor),
        out_shape=(jax.ShapeDtypeStruct((256, 640), F32),) * 3 + (jax.ShapeDtypeStruct((256, 384), F32),),
        grid=(2,),
        in_specs=[pl.BlockSpec(memory_space=pltpu.SMEM), vmem, vmem, wide, wide],
        out_specs=(wide, wide, wide, pl.BlockSpec((128, 384), lambda i: (i, 0))),
        compiler_params=pltpu.CompilerParams(vmem_limit_bytes=32 << 20),
        cost_estimate=pl.CostEstimate(flops=1 << 22, bytes_accessed=6 << 20, transcendentals=0),
    )(where, mine, other, moment, second)


def has_host(c):
    return c["c"] == c["x"] + c["zl"] + c["zh"] & 1


def on_device(tokens, cotangent, weight, moment, second, delayed):
    me = where_am_i()
    device_cols = moment.shape[1]
    norm_factor = (tokens.shape[0] * lax.axis_size("rep") * lax.axis_size("fsdp")) ** (-0.5)
    y, zh, core = me["y"], me["zh"], me["c"]
    order = jnp.stack([core] + [at for axis in ("x", "zl", "y") for at in orders(me[axis], core)])
    order = order.astype(jnp.int32)
    host_places = lax.dynamic_slice(jnp.array(HOST_PLACES, jnp.int32), (zh * 4 + me["zl"], 0), (1, 4))
    where = jnp.stack([core] + places(me["x"], core) + places(me["zl"], core)).astype(jnp.int32)
    where = jnp.concatenate([where, host_places[0]])
    where_y = jnp.stack([core] + places(y, core) + places(y, 1 - core)).astype(jnp.int32)

    their_cot = send(cotangent, flip("c"))
    their_tokens = send(tokens, flip("c"))
    kept, refreshed = projection_rows(order, weight, delayed)
    kept_got = send(kept, partner("x", False))
    for_zh = send(
        refreshed,
        lambda c: dict(c, zh=1, zl=c["zl"] ^ 1) if c["y"] == c["zh"] == 0 and has_host(c) else None,
    )
    order, kept, kept_got = together(order, kept, kept_got)
    kept = jnp.stack([kept, kept_got])
    kept_got = send(kept, partner("x", True))
    order, kept = together(order, kept)
    one_out, two_out = chip_gradient(False, order, tokens, their_tokens, cotangent, their_cot)
    one_out, two_out, order, kept, kept_got, refreshed, for_zh = together(
        one_out, two_out, order, kept, kept_got, refreshed, for_zh
    )

    one_got = send(one_out, partner("x", True))
    two_got = send(two_out, partner("y", True))
    kept = jnp.concatenate([kept, kept_got])
    kept_a = send(kept, partner("zl", True))
    kept_b = send(kept, partner("zl", False))
    refreshed = jnp.where(zh == 0, refreshed, for_zh)
    first = core == (me["x"] + me["zl"] + zh) % 2
    lower, upper = refreshed[:, :128], refreshed[:, 128:]
    for_core = send(
        jnp.where(core == 0, upper, lower),
        lambda c: dict(c, c=1 - c["c"]) if c["y"] == 0 and has_host(c) else None,
    )
    one_held, two_held = chip_gradient(True, order, tokens, their_tokens, cotangent, their_cot)
    one_far = (one_held[0] + one_got[0].astype(F32)).astype(BF16)
    two_far = (two_held[0] + two_got[0].astype(F32)).astype(BF16)
    host = jnp.where(first, jnp.where(core == 0, lower, upper), for_core)
    one_far, two_far, kept, kept_a, kept_b, host = together(
        one_far, two_far, kept, kept_a, kept_b, host
    )

    one_got2 = send(one_far, partner("x", False))
    two_got2, host_got = ride(two_far, host, partner("y", False))
    kept_c = send(kept_b, partner("zl", True))
    one = one_held[1] + one_got[1].astype(F32) + one_got2.astype(F32)
    two = two_held[1] + two_got[1].astype(F32) + two_got2.astype(F32)
    host = jnp.where(y == jnp.where(core == 0, 3, 1), host_got, host)
    one, two, host, kept_c = together(one, two, host, kept_c)

    one_got, host_got = ride(one[:2].astype(BF16), host, partner("y", True))
    two_got = send(two[:2].astype(BF16), partner("x", True))
    one_far = (one[2] + one_got[0].astype(F32)).astype(BF16)
    two_far = (two[2] + two_got[0].astype(F32)).astype(BF16)
    host = jnp.where((y == 2) | (y == jnp.where(core == 0, 1, 3)), host_got, host)
    one_far, two_far, host = together(one_far, two_far, host)

    one_got2 = send(one_far, partner("y", False))
    two_got2 = send(two_far, partner("x", False))
    host_got = send(host, neighbour("zl", 1))
    both = jnp.stack(
        [
            one[3] + one_got[1].astype(F32) + one_got2.astype(F32),
            two[3] + two_got[1].astype(F32) + two_got2.astype(F32),
        ],
        axis=1,
    )
    both, host, host_got = together(both, host, host_got)

    got = send(both[:2], partner("zl", True))
    host = jnp.stack([host, host_got])
    host_got = send(host, neighbour("zl", 3))
    kept = jnp.stack([kept, kept_b, kept_a, kept_c])
    far = both[2] + got[0]
    far, host, host_got, kept = together(far, host, host_got, kept)
    got2 = send(far, partner("zl", False))
    host = jnp.concatenate([host, host_got])
    host_got = send(host, partner("x", False))
    total = (both[3] + got[1] + got2).astype(BF16)
    total, host = together(total, host)
    zh_got = send(total, flip("zh"))
    host = jnp.stack([host, host_got])
    host_got = send(host, partner("x", True))
    total = total.astype(F32) + zh_got.astype(F32)
    mine_got = send(total, partner("y", False))
    mine = jnp.stack([total, mine_got])
    mine, host = together(mine, host)
    mine_got = send(mine, partner("y", True))

    host = jnp.concatenate([host, host_got])
    theirs = their_input_gradient(where, their_cot, kept, host)
    got = send(theirs, flip("c"))
    mine = jnp.concatenate([mine, mine_got])
    mine, theirs = together(mine, theirs)
    other = send(mine, flip("c"))
    grad_input = our_input_gradient(where, cotangent, kept, host, got)
    mine, grad_input = together(mine, grad_input)
    return (grad_input, *finish(norm_factor, where_y, mine, other, moment, second))


def solution(mesh):
    placed = (
        P(("rep", "fsdp"), None),
        P(("rep", "fsdp"), None),
        P("fsdp", None),
        P("fsdp", None),
        P("fsdp", None),
        P("rep", "fsdp", None),
    )
    return jax.shard_map(
        on_device,
        mesh=mesh,
        in_specs=placed,
        out_specs=(
            P(("rep", "fsdp"), None),
            P("fsdp", None),
            P("fsdp", None),
            P("fsdp", None),
            P("fsdp", None),
        ),
        check_vma=False,
    )
```

time: 776 us -> 139 us (0.18)
  waiting for transfers between devices: 729 us -> 55.3 us
  starting transfers between devices: 0.12 us -> 37.2 us
  Pallas kernels: 0 us -> 26.7 us
  matrix products: 19 us -> 0 us
  between operations: 13.8 us -> 1.31 us
    reduce_scatter x1 -> x0, waiting for transfers between devices: 359 us -> none  [on_device(): lax.psum_scatter(lax.dot_general(tokens, cotangent, (((0,), (0,)), ((), (...]
    psum x1 -> x0, waiting for transfers between devices: 186 us -> none  [from_root(): return lax.psum(kept, axis)]
    all_gather x1 -> x0, waiting for transfers between devices: 184 us -> none  [on_device(): lax.all_gather(current, 'fsdp', axis=0, tiled=True)]
    ppermute x0 -> x28, waiting for transfers between devices: none -> 55.3 us  [send(): return lax.ppermute(value, AXES, pairs)]
    ppermute x0 -> x28, starting transfers between devices: none -> 37.2 us  [send(): return lax.ppermute(value, AXES, pairs)]
    pallas_call x0 -> x6, Pallas kernels: none -> 26.7 us  [the longest x2 13.4 us: chip_gradient(): pl.pallas_call(functools.partial(grad_kernel, keep), out_shape=(jax.Shape...]
    dot_general x2 -> x0, matrix products: 19 us -> none  [the longest x1 9.8 us: on_device(): lax.dot_general(cotangent, lax.all_gather(current, 'fsdp', axis=0, tiled=...]
  transfers between devices with their start and end apart: 3 -> 28, of which waited for: 3 -> 17; matrix products, arithmetic and copies ran while one was open for 1% -> 8% of each run, Pallas kernels for 0% -> 15%
where the time goes in v2:
time: 139 us; the launch traced here: 138 us
  waiting for transfers between devices  55.3 us (40%)
  starting transfers between devices  37.2 us (27%)
  Pallas kernels  26.7 us (19%)
  local copies, waits for them, and re-layouts  9.21 us (7%)
  other arithmetic  8.73 us (6%)
    ppermute x28, waiting for transfers between devices, send(): return lax.ppermute(value, AXES, pairs)  55.3 us
    ppermute x28, starting transfers between devices, send(): return lax.ppermute(value, AXES, pairs)  37.2 us
    pallas_call x2, Pallas kernels, chip_gradient(): pl.pallas_call(functools.partial(grad_kernel, keep), out_shape=(jax.Shape...  13.4 us
    pallas_call x1, Pallas kernels, our_input_gradient(): pl.pallas_call(ours_kernel, out_shape=jax.ShapeDtypeStruct((384, 4096), B...  6.44 us
    unnamed x49, local copies, waits for them, and re-layouts  5.76 us
    pallas_call x1, Pallas kernels, their_input_gradient(): pl.pallas_call(theirs_kernel, out_shape=jax.ShapeDtypeStruct((384, 2048),...  3.92 us
  transfers between devices with their start and end apart: 28, of which 17 were waited for; matrix products, arithmetic and copies ran while one was open for 8% of the time, Pallas kernels for 15%

profile of v2, /device:TPU:1, one launch (start us, length us, event | category | flops | bytes accessed | tf_op | source)
XLA Modules:
  0.0 138.5 jit_solution(17117687446651388185)
XLA Ops:
  0.6 3.3 %collective-permute-start.1 = (bf16[384,4096]{1,0:T(8,128)(2,1)}, bf16[384,4096]{1,0:T(8,128)(2,1)}, u32[]{:S(2)}, u32[]{:S(2)}) collective-permute-start(bf16[384,4096]{1,0:T(8,128)(2,1)} %t_hbm.3), channel_id=1, source_target_pairs={{0,16},{1,17},{2,18},{3,19},{4,20},{5,21},{6,22},{7,23},{8,24},{9,... | collective-permute-start | bytes 9437192 | tf_op jit(solution)/shard_map/ppermute | solution.py:49
  4.0 0.1 collective-permute-start.2
  4.2 1.0 copy-done.8
  5.2 1.0 copy-done.9
  6.2 0.7 shard_map.110
  6.9 0.1 collective-permute-start
  7.0 5.0 %collective-permute-done = bf16[640,128]{1,0:T(8,128)(2,1)S(1)} collective-permute-done((bf16[640,128]{1,0:T(8,128)(2,1)S(1)}, bf16[640,128]{1,0:T(8,128)(2,1)S(1)}, u32[]{:S(2)}, u32[]{:S(2)}) %collective-permute-start) | collective-permute-done | bytes 163872 | tf_op jit(solution)/shard_map/ppermute | solution.py:49
  12.1 0.8 collective-permute-start.3
  12.9 0.7 collective-permute-start.4
  13.6 0.9 copy-done.4
  14.6 6.3 %shard_map.111 = (bf16[2,4,4,128,128]{4,3,2,1,0:T(8,128)(2,1)}, bf16[2,4,4,128,128]{4,3,2,1,0:T(8,128)(2,1)}) custom-call(s32[13]{0:T(128)} %copy-done.10, bf16[384,4096]{1,0:T(8,128)(2,1)} %t_hbm.3, bf16[384,4096]{1,0:T(8,128)(2,1)} %collective-permute-done.1.u_hbm, bf16[384,1024]{1,0:T(8,128)(2,1)} %cot_ref.1, bf16[384,1024]{1,0:T(8,128)(2,1)} %copy-done.4), custom_call_target="tpu_custom_call" | custom-call | flops 1610612736 | bytes 9437184 | tf_op jit(solution)/shard_map/pallas_call | solution.py:150
  20.9 8.3 %collective-permute-start.5 = (bf16[2,4,4,128,128]{4,3,2,1,0:T(8,128)(2,1)}, bf16[2,4,4,128,128]{4,3,2,1,0:T(8,128)(2,1)S(1)}, u32[]{:S(2)}, u32[]{:S(2)}) collective-permute-start(bf16[2,4,4,128,128]{4,3,2,1,0:T(8,128)(2,1)} %get-tuple-element.65), channel_id=1, source_target_pairs={{0,20},{1,29},{2,22},{3,31},{4,24},{5,17},{6,26},{7,19},{8,28},{9,... | collective-permute-start | bytes 3145736 | tf_op jit(solution)/shard_map/ppermute | solution.py:49
  29.3 0.1 collective-permute-start.7
  29.4 1.7 %collective-permute-start.8 = (bf16[4,640,128]{2,1,0:T(8,128)(2,1)S(1)}, bf16[4,640,128]{2,1,0:T(8,128)(2,1)}, u32[]{:S(2)}, u32[]{:S(2)}) collective-permute-start(bf16[4,640,128]{2,1,0:T(8,128)(2,1)S(1)} %constant_dynamic-update-slice_fusion), channel_id=1, source_target_pairs={{0,51},{1,16},{2,17},{3,18},{4,21},{5,22},{6,23},{7,52},{8,59},{9,... | collective-permute-start | bytes 1966088 | tf_op jit(solution)/shard_map/ppermute | solution.py:49
  31.2 1.3 collective-permute-start.9
  32.5 7.1 %shard_map.112 = (f32[2,4,4,128,128]{4,3,2,1,0:T(8,128)}, f32[2,4,4,128,128]{4,3,2,1,0:T(8,128)}) custom-call(s32[13]{0:T(128)} %copy-done.10, bf16[384,4096]{1,0:T(8,128)(2,1)} %t_hbm.3, bf16[384,4096]{1,0:T(8,128)(2,1)} %collective-permute-done.1.u_hbm, bf16[384,1024]{1,0:T(8,128)(2,1)} %cot_ref.1, bf16[384,1024]{1,0:T(8,128)(2,1)} %copy-done.4), custom_call_target="tpu_custom_call" | custom-call | flops 1610612736 | bytes 9437184 | tf_op jit(solution)/shard_map/pallas_call | solution.py:150
  39.6 2.7 %collective-permute-done.5 = bf16[2,4,4,128,128]{4,3,2,1,0:T(8,128)(2,1)S(1)} collective-permute-done((bf16[2,4,4,128,128]{4,3,2,1,0:T(8,128)(2,1)}, bf16[2,4,4,128,128]{4,3,2,1,0:T(8,128)(2,1)S(1)}, u32[]{:S(2)}, u32[]{:S(2)}) %collective-permute-start.5) | collective-permute-done | bytes 1048608 | tf_op jit(solution)/shard_map/ppermute | solution.py:49
  42.3 1.7 %fusion = bf16[4,4,128,128]{3,2,1,0:T(8,128)(2,1)S(1)} fusion(f32[2,4,4,128,128]{4,3,2,1,0:T(8,128)} %get-tuple-element.64, bf16[2,4,4,128,128]{4,3,2,1,0:T(8,128)(2,1)S(1)} %collective-permute-done.5), kind=kLoop, calls=%fused_computation.7 | loop fusion | flops 786432 | bytes 2097152 | tf_op jit(solution)/shard_map/convert_element_type | solution.py:323
  44.0 3.1 %collective-permute-done.6 = bf16[2,4,4,128,128]{4,3,2,1,0:T(8,128)(2,1)S(1)} collective-permute-done((bf16[2,4,4,128,128]{4,3,2,1,0:T(8,128)(2,1)}, bf16[2,4,4,128,128]{4,3,2,1,0:T(8,128)(2,1)S(1)}, u32[]{:S(2)}, u32[]{:S(2)}) %collective-permute-start.6) | collective-permute-done | bytes 1048608 | tf_op jit(solution)/shard_map/ppermute | solution.py:49
  47.2 0.1 fusion.1
  47.3 0.4 collective-permute-done.7
  47.7 0.9 pad_maximum_fusion.2
  48.6 0.1 copy-done.19
  48.7 1.7 %collective-permute-start.12 = (bf16[4,640,128]{2,1,0:T(8,128)(2,1)}, bf16[4,640,128]{2,1,0:T(8,128)(2,1)S(1)}, u32[]{:S(2)}, u32[]{:S(2)}) collective-permute-start(bf16[4,640,128]{2,1,0:T(8,128)(2,1)} %collective-permute-done.8), channel_id=1, source_target_pairs={{0,17},{1,18},{2,19},{3,48},{4,55},{5,20},{6,21},{7,22},{8,25},{9,... | collective-permute-start | bytes 1966088 | tf_op jit(solution)/shard_map/ppermute | solution.py:49
  50.5 6.2 %collective-permute-done.10 = bf16[4,4,128,128]{3,2,1,0:T(8,128)(2,1)} collective-permute-done((bf16[4,4,128,128]{3,2,1,0:T(8,128)(2,1)S(1)}, bf16[4,4,128,128]{3,2,1,0:T(8,128)(2,1)}, u32[]{:S(2)}, u32[]{:S(2)}) %collective-permute-start.10) | collective-permute-done | bytes 524320 | tf_op jit(solution)/shard_map/ppermute | solution.py:49
  56.7 1.4 bitcast_add_fusion
  58.1 0.9 collective-permute-done.11
  59.0 1.1 slice.125
  60.1 0.9 slice_select_fusion.1
  61.0 0.2 convert_add_fusion
  61.3 1.6 %collective-permute-start.14 = (bf16[2,4,128,128]{3,2,1,0:T(8,128)(2,1)S(1)}, bf16[2,4,128,128]{3,2,1,0:T(8,128)(2,1)S(1)}, u32[]{:S(2)}, u32[]{:S(2)}) collective-permute-start(bf16[2,4,128,128]{3,2,1,0:T(8,128)(2,1)S(1)} %slice.176), channel_id=1, source_target_pairs={{0,20},{1,29},{2,22},{3,31},{4,24},{5,17},{6,26},{7,19},{8,28},{9,... | collective-permute-start | bytes 786440 | tf_op jit(solution)/shard_map/ppermute | solution.py:49
  62.9 0.1 collective-permute-start.13
  63.0 5.4 %collective-permute-done.14 = bf16[2,4,128,128]{3,2,1,0:T(8,128)(2,1)S(1)} collective-permute-done((bf16[2,4,128,128]{3,2,1,0:T(8,128)(2,1)S(1)}, bf16[2,4,128,128]{3,2,1,0:T(8,128)(2,1)S(1)}, u32[]{:S(2)}, u32[]{:S(2)}) %collective-permute-start.14) | collective-permute-done | bytes 262176 | tf_op jit(solution)/shard_map/ppermute | solution.py:49
  68.4 2.6 %collective-permute-done.13 = bf16[1408,128]{1,0:T(8,128)(2,1)S(1)} collective-permute-done((bf16[1408,128]{1,0:T(8,128)(2,1)S(1)}, bf16[1408,128]{1,0:T(8,128)(2,1)S(1)}, u32[]{:S(2)}, u32[]{:S(2)}) %collective-permute-start.13) | collective-permute-done | bytes 360480 | tf_op jit(solution)/shard_map/ppermute | solution.py:49
  71.2 0.9 collective-permute-start.16
  72.0 0.8 collective-permute-start.17
  72.8 3.1 %collective-permute-done.16 = bf16[4,128,128]{2,1,0:T(8,128)(2,1)S(1)} collective-permute-done((bf16[4,128,128]{2,1,0:T(8,128)(2,1)S(1)}, bf16[4,128,128]{2,1,0:T(8,128)(2,1)S(1)}, u32[]{:S(2)}, u32[]{:S(2)}) %collective-permute-start.16) | collective-permute-done | bytes 131104 | tf_op jit(solution)/shard_map/ppermute | solution.py:49
  76.0 0.7 collective-permute-done.15
  76.8 1.3 collective-permute-start.18
  78.2 1.4 %pad_maximum_fusion.w_ref = bf16[4,4,640,128]{3,2,1,0:T(8,128)(2,1)S(1)} fusion(bf16[1,4,640,128]{3,2,1,0:T(8,128)(2,1)S(1)} %bitcast.89, bf16[1,4,640,128]{3,2,1,0:T(8,128)(2,1)S(1)} %bitcast.88, bf16[1,4,640,128]{3,2,1,0:T(8,128)(2,1)} %bitcast.35, bf16[1,4,640,128]{3,2,1,0:T(8,128)(2,1)S(1)} %bitcast.85), kind=kLoop, calls=%fused_computation | loop fusion | flops 3932160 | bytes 5242880 | tf_op jit(solution)/shard_map/stack | solution.py:360
  79.6 1.8 %collective-permute-start.19 = (bf16[2,384,128]{2,1,0:T(8,128)(2,1)S(1)}, bf16[2,384,128]{2,1,0:T(8,128)(2,1)S(1)}, u32[]{:S(2)}, u32[]{:S(2)}) collective-permute-start(bf16[2,384,128]{2,1,0:T(8,128)(2,1)S(1)} %pad_maximum_fusion.8), channel_id=1, source_target_pairs={{0,51},{1,18},{2,17},{3,48},{4,55},{5,22},{6,21},{7,52},{8,59},{9,... | collective-permute-start | bytes 589832 | tf_op jit(solution)/shard_map/ppermute | solution.py:49
  81.4 2.5 %collective-permute-done.18 = f32[2,2,128,128]{3,2,1,0:T(8,128)S(1)} collective-permute-done((f32[2,2,128,128]{3,2,1,0:T(8,128)S(1)}, f32[2,2,128,128]{3,2,1,0:T(8,128)S(1)}, u32[]{:S(2)}, u32[]{:S(2)}) %collective-permute-start.18) | collective-permute-done | bytes 262176 | tf_op jit(solution)/shard_map/ppermute | solution.py:49
  84.0 3.8 %collective-permute-done.19 = bf16[2,384,128]{2,1,0:T(8,128)(2,1)S(1)} collective-permute-done((bf16[2,384,128]{2,1,0:T(8,128)(2,1)S(1)}, bf16[2,384,128]{2,1,0:T(8,128)(2,1)S(1)}, u32[]{:S(2)}, u32[]{:S(2)}) %collective-permute-start.19) | collective-permute-done | bytes 196640 | tf_op jit(solution)/shard_map/ppermute | solution.py:49
  87.8 1.9 %collective-permute-start.23 = (bf16[4,384,128]{2,1,0:T(8,128)(2,1)S(1)}, bf16[4,384,128]{2,1,0:T(8,128)(2,1)S(1)}, u32[]{:S(2)}, u32[]{:S(2)}) collective-permute-start(bf16[4,384,128]{2,1,0:T(8,128)(2,1)S(1)} %constant_dynamic-update-slice_fusion.2), channel_id=1, source_target_pairs={{0,28},{1,21},{2,30},{3,23},{4,16},{5,25},{6,18},{7,27},{8,20},{9,... | collective-permute-start | bytes 1179656 | tf_op jit(solution)/shard_map/ppermute | solution.py:49
  89.7 4.7 %collective-permute-done.20 = f32[2,128,128]{2,1,0:T(8,128)S(1)} collective-permute-done((f32[2,128,128]{2,1,0:T(8,128)S(1)}, f32[2,128,128]{2,1,0:T(8,128)S(1)}, u32[]{:S(2)}, u32[]{:S(2)}) %collective-permute-start.20) | collective-permute-done | bytes 131104 | tf_op jit(solution)/shard_map/ppermute | solution.py:49
  94.4 1.0 collective-permute-done.23
  95.6 1.0 collective-permute-start.25
  96.5 3.2 %collective-permute-start.21 = (bf16[2,128,128]{2,1,0:T(8,128)(2,1)S(1)}, bf16[2,128,128]{2,1,0:T(8,128)(2,1)S(1)}, u32[]{:S(2)}, u32[]{:S(2)}) collective-permute-start(bf16[2,128,128]{2,1,0:T(8,128)(2,1)S(1)} %fusion.10), channel_id=1, source_target_pairs={{0,32},{1,33},{2,34},{3,35},{4,36},{5,37},{6,38},{7,39},{8,40},{9,... | collective-permute-start | bytes 196616 | tf_op jit(solution)/shard_map/ppermute | solution.py:49
  99.8 3.9 %collective-permute-done.21 = bf16[2,128,128]{2,1,0:T(8,128)(2,1)S(1)} collective-permute-done((bf16[2,128,128]{2,1,0:T(8,128)(2,1)S(1)}, bf16[2,128,128]{2,1,0:T(8,128)(2,1)S(1)}, u32[]{:S(2)}, u32[]{:S(2)}) %collective-permute-start.21) | collective-permute-done | bytes 65568 | tf_op jit(solution)/shard_map/ppermute | solution.py:49
  103.7 0.7 fusion.11
  104.3 3.2 %collective-permute-start.22 = (f32[2,128,128]{2,1,0:T(8,128)}, f32[2,128,128]{2,1,0:T(8,128)}, u32[]{:S(2)}, u32[]{:S(2)}) collective-permute-start(f32[2,128,128]{2,1,0:T(8,128)} %get-tuple-element.106), channel_id=1, source_target_pairs={{0,208},{1,81},{2,210},{3,83},{4,84},{5,213},{6,86},{7,215},{8,216... | collective-permute-start | bytes 393224 | tf_op jit(solution)/shard_map/ppermute | solution.py:49
  107.5 0.7 dynamic-slice_bitcast_fusion
  108.3 2.2 %collective-permute-done.22 = f32[2,128,128]{2,1,0:T(8,128)} collective-permute-done((f32[2,128,128]{2,1,0:T(8,128)}, f32[2,128,128]{2,1,0:T(8,128)}, u32[]{:S(2)}, u32[]{:S(2)}) %collective-permute-start.22) | collective-permute-done | bytes 131104 | tf_op jit(solution)/shard_map/ppermute | solution.py:49
  110.5 0.9 pad_maximum_fusion.7
  111.5 1.2 constant_dynamic-update-slice_fusion.4.r_ref
  112.8 1.1 copy-done.5
  113.9 3.9 %shard_map.113 = bf16[384,2048]{1,0:T(8,128)(2,1)} custom-call(s32[13]{0:T(128)S(1)} %concatenate.26.s_ref, bf16[384,1024]{1,0:T(8,128)(2,1)S(1)} %copy-done.5, bf16[4,4,640,128]{3,2,1,0:T(8,128)(2,1)S(1)} %pad_maximum_fusion.w_ref, bf16[4,4,384,128]{3,2,1,0:T(8,128)(2,1)S(1)} %constant_dynamic-update-slice_fusion.4.r_ref), custom_call_target="tpu_custom_call" | custom-call | flops 1610612736 | bytes 3145728 | tf_op jit(solution)/shard_map/pallas_call | solution.py:210
  117.8 3.2 %collective-permute-start.26 = (bf16[384,2048]{1,0:T(8,128)(2,1)}, bf16[384,2048]{1,0:T(8,128)(2,1)S(1)}, u32[]{:S(2)}, u32[]{:S(2)}) collective-permute-start(bf16[384,2048]{1,0:T(8,128)(2,1)} %shard_map.113), channel_id=1, source_target_pairs={{0,16},{1,17},{2,18},{3,19},{4,20},{5,21},{6,22},{7,23},{8,24},{9,... | collective-permute-start | bytes 4718600 | tf_op jit(solution)/shard_map/ppermute | solution.py:49
  121.0 7.0 %collective-permute-done.24 = f32[2,2,128,128]{3,2,1,0:T(8,128)S(1)} collective-permute-done((f32[2,2,128,128]{3,2,1,0:T(8,128)S(1)}, f32[2,2,128,128]{3,2,1,0:T(8,128)S(1)}, u32[]{:S(2)}, u32[]{:S(2)}) %collective-permute-start.24) | collective-permute-done | bytes 262176 | tf_op jit(solution)/shard_map/ppermute | solution.py:49
  128.0 0.1 collective-permute-start.27
  128.2 0.1 stack.205.s_ref
  128.3 1.4 %copy-done.2 = bf16[4,4,384,128]{3,2,1,0:T(8,128)(2,1)S(1)} copy-done((bf16[4,4,384,128]{3,2,1,0:T(8,128)(2,1)S(1)}, bf16[4,4,384,128]{3,2,1,0:T(8,128)(2,1)}, u32[]{:S(2)}) %copy-start.2) | copy-done | bytes 1572888
  129.7 6.4 %shard_map.114 = bf16[384,4096]{1,0:T(8,128)(2,1)} custom-call(s32[13]{0:T(128)S(1)} %concatenate.26.s_ref, bf16[384,1024]{1,0:T(8,128)(2,1)S(1)} %copy-done.3, bf16[4,4,640,128]{3,2,1,0:T(8,128)(2,1)} %copy-done, bf16[4,4,384,128]{3,2,1,0:T(8,128)(2,1)S(1)} %copy-done.2, bf16[384,2048]{1,0:T(8,128)(2,1)S(1)} %collective-permute-done.26.got_ref), custom_call_target="tpu_custom_call" | custom-call | flops 1610612736 | bytes 9437184 | tf_op jit(solution)/shard_map/pallas_call | solution.py:224
  136.2 2.3 %shard_map.115 = (f32[256,640]{1,0:T(8,128)}, f32[256,640]{1,0:T(8,128)}, f32[256,640]{1,0:T(8,128)}, f32[256,384]{1,0:T(8,128)}) custom-call(s32[9]{0:T(128)S(1)} %stack.205.s_ref, f32[4,2,128,128]{3,2,1,0:T(8,128)S(1)} %pad_maximum_fusion.4.mine_ref, f32[4,2,128,128]{3,2,1,0:T(8,128)S(1)} %collective-permute-done.27.other_ref, f32[256,640]{1,0:T(8,128)S(1)} %copy-done.6, ...), custom_call_target="tpu_custom_call" | custom-call | flops 4194304 | bytes 6291456 | tf_op jit(solution)/shard_map/pallas_call | solution.py:266
  (84 shorter events, 1.1 us)
Async XLA Ops:
  0.6 13.0 %collective-permute-start.1 = (bf16[384,4096]{1,0:T(8,128)(2,1)}, bf16[384,4096]{1,0:T(8,128)(2,1)}, u32[]{:S(2)}, u32[]{:S(2)}) collective-permute-start(bf16[384,4096]{1,0:T(8,128)(2,1)} %t_hbm.3), channel_id=1, source_target_pairs={{0,16},{1,17},{2,18},{3,19},{4,20},{5,21},{6,22},{7,23},{8,24},{9,... | collective-permute-start | bytes 9437192 | tf_op jit(solution)/shard_map/ppermute | solution.py:49
  4.0 9.7 %collective-permute-start.2 = (bf16[384,1024]{1,0:T(8,128)(2,1)}, bf16[384,1024]{1,0:T(8,128)(2,1)S(1)}, u32[]{:S(2)}, u32[]{:S(2)}) collective-permute-start(bf16[384,1024]{1,0:T(8,128)(2,1)} %cot_ref.1), channel_id=1, source_target_pairs={{0,16},{1,17},{2,18},{3,19},{4,20},{5,21},{6,22},{7,23},{8,24},{9,... | collective-permute-start | bytes 2359304 | tf_op jit(solution)/shard_map/ppermute | solution.py:49
  4.1 1.0 copy-start.8
  5.2 1.0 copy-start.9
  6.2 7.4 %copy-start.10 = (s32[13]{0:T(128)}, s32[13]{0:T(128)S(1)}, u32[]{:S(2)}) copy-start(s32[13]{0:T(128)S(1)} %stack.168.s_ref) | copy-start | bytes 160
  6.9 5.1 %collective-permute-start = (bf16[640,128]{1,0:T(8,128)(2,1)S(1)}, bf16[640,128]{1,0:T(8,128)(2,1)S(1)}, u32[]{:S(2)}, u32[]{:S(2)}) collective-permute-start(bf16[640,128]{1,0:T(8,128)(2,1)S(1)} %get-tuple-element.56), channel_id=1, source_target_pairs={{0,28},{1,21},{2,30},{3,23},{4,16},{5,25},{6,18},{7,27},{8,20},{9,... | collective-permute-start | bytes 491528 | tf_op jit(solution)/shard_map/ppermute | solution.py:49
  12.1 8.9 %collective-permute-start.3 = (bf16[2,640,128]{2,1,0:T(8,128)(2,1)S(1)}, bf16[2,640,128]{2,1,0:T(8,128)(2,1)S(1)}, u32[]{:S(2)}, u32[]{:S(2)}) collective-permute-start(bf16[2,640,128]{2,1,0:T(8,128)(2,1)S(1)} %pad_maximum_fusion.6), channel_id=1, source_target_pairs={{0,20},{1,29},{2,22},{3,31},{4,24},{5,17},{6,26},{7,19},{8,28},{9,... | collective-permute-start | bytes 983048 | tf_op jit(solution)/shard_map/ppermute | solution.py:49
  12.9 8.0 %collective-permute-start.4 = (bf16[384,256]{1,0:T(8,128)(2,1)S(1)}, bf16[384,256]{1,0:T(8,128)(2,1)S(1)}, u32[]{:S(2)}, u32[]{:S(2)}) collective-permute-start(bf16[384,256]{1,0:T(8,128)(2,1)S(1)} %get-tuple-element.70), channel_id=1, source_target_pairs={{0,49},{1,48},{2,51},{3,50},{4,53},{5,52},{6,55},{7,54},{8,57},{9,... | collective-permute-start | bytes 589832 | tf_op jit(solution)/shard_map/ppermute | solution.py:49
  13.6 0.9 copy-start.4
  20.9 21.4 %collective-permute-start.5 = (bf16[2,4,4,128,128]{4,3,2,1,0:T(8,128)(2,1)}, bf16[2,4,4,128,128]{4,3,2,1,0:T(8,128)(2,1)S(1)}, u32[]{:S(2)}, u32[]{:S(2)}) collective-permute-start(bf16[2,4,4,128,128]{4,3,2,1,0:T(8,128)(2,1)} %get-tuple-element.65), channel_id=1, source_target_pairs={{0,20},{1,29},{2,22},{3,31},{4,24},{5,17},{6,26},{7,19},{8,28},{9,... | collective-permute-start | bytes 3145736 | tf_op jit(solution)/shard_map/ppermute | solution.py:49
  29.3 10.3 %copy-start.14 = (bf16[4,640,128]{2,1,0:T(8,128)(2,1)}, bf16[4,640,128]{2,1,0:T(8,128)(2,1)S(1)}, u32[]{:S(2)}) copy-start(bf16[4,640,128]{2,1,0:T(8,128)(2,1)S(1)} %constant_dynamic-update-slice_fusion) | copy-start | bytes 1966084
  29.3 18.4 %collective-permute-start.7 = (bf16[4,640,128]{2,1,0:T(8,128)(2,1)S(1)}, bf16[4,640,128]{2,1,0:T(8,128)(2,1)S(1)}, u32[]{:S(2)}, u32[]{:S(2)}) collective-permute-start(bf16[4,640,128]{2,1,0:T(8,128)(2,1)S(1)} %constant_dynamic-update-slice_fusion), channel_id=1, source_target_pairs={{0,17},{1,18},{2,19},{3,48},{4,55},{5,20},{6,21},{7,22},{8,25},{9,... | collective-permute-start | bytes 1966088 | tf_op jit(solution)/shard_map/ppermute | solution.py:49
  29.4 18.3 %collective-permute-start.8 = (bf16[4,640,128]{2,1,0:T(8,128)(2,1)S(1)}, bf16[4,640,128]{2,1,0:T(8,128)(2,1)}, u32[]{:S(2)}, u32[]{:S(2)}) collective-permute-start(bf16[4,640,128]{2,1,0:T(8,128)(2,1)S(1)} %constant_dynamic-update-slice_fusion), channel_id=1, source_target_pairs={{0,51},{1,16},{2,17},{3,18},{4,21},{5,22},{6,23},{7,52},{8,59},{9,... | collective-permute-start | bytes 1966088 | tf_op jit(solution)/shard_map/ppermute | solution.py:49
  31.1 16.0 %collective-permute-start.6 = (bf16[2,4,4,128,128]{4,3,2,1,0:T(8,128)(2,1)}, bf16[2,4,4,128,128]{4,3,2,1,0:T(8,128)(2,1)S(1)}, u32[]{:S(2)}, u32[]{:S(2)}) collective-permute-start(bf16[2,4,4,128,128]{4,3,2,1,0:T(8,128)(2,1)} %get-tuple-element.67), channel_id=1, source_target_pairs={{0,80},{1,209},{2,82},{3,211},{4,212},{5,85},{6,214},{7,87},{8,88}... | collective-permute-start | bytes 3145736 | tf_op jit(solution)/shard_map/ppermute | solution.py:49
  31.2 8.4 %collective-permute-start.9 = (bf16[384,128]{1,0:T(8,128)(2,1)S(1)}, bf16[384,128]{1,0:T(8,128)(2,1)S(1)}, u32[]{:S(2)}, u32[]{:S(2)}) collective-permute-start(bf16[384,128]{1,0:T(8,128)(2,1)S(1)} %broadcast_select_fusion.1), channel_id=1, source_target_pairs={{0,16},{1,17},{2,18},{3,19},{4,20},{5,21},{6,22},{7,23},{8,24},{9,... | collective-permute-start | bytes 294920 | tf_op jit(solution)/shard_map/ppermute | solution.py:49
  39.6 7.6 %copy-start.11 = (f32[2,4,4,128,128]{4,3,2,1,0:T(8,128)S(1)}, f32[2,4,4,128,128]{4,3,2,1,0:T(8,128)}, u32[]{:S(2)}) copy-start(f32[2,4,4,128,128]{4,3,2,1,0:T(8,128)} %get-tuple-element.66) | copy-start | bytes 6291460
  42.3 6.3 %copy-start.16 = (bf16[2,4,4,128,128]{4,3,2,1,0:T(8,128)(2,1)}, bf16[2,4,4,128,128]{4,3,2,1,0:T(8,128)(2,1)S(1)}, u32[]{:S(2)}) copy-start(bf16[2,4,4,128,128]{4,3,2,1,0:T(8,128)(2,1)S(1)} %collective-permute-done.5) | copy-start | bytes 3145732
  44.0 12.6 %copy-start.13 = (f32[2,4,4,128,128]{4,3,2,1,0:T(8,128)S(1)}, f32[2,4,4,128,128]{4,3,2,1,0:T(8,128)}, u32[]{:S(2)}) copy-start(f32[2,4,4,128,128]{4,3,2,1,0:T(8,128)} %get-tuple-element.64) | copy-start | bytes 6291460
  47.2 1.4 %copy-start.17 = (bf16[2,4,4,128,128]{4,3,2,1,0:T(8,128)(2,1)}, bf16[2,4,4,128,128]{4,3,2,1,0:T(8,128)(2,1)S(1)}, u32[]{:S(2)}) copy-start(bf16[2,4,4,128,128]{4,3,2,1,0:T(8,128)(2,1)S(1)} %collective-permute-done.6) | copy-start | bytes 3145732
  47.7 1.0 copy-start.19
  47.7 9.0 %collective-permute-start.10 = (bf16[4,4,128,128]{3,2,1,0:T(8,128)(2,1)S(1)}, bf16[4,4,128,128]{3,2,1,0:T(8,128)(2,1)}, u32[]{:S(2)}, u32[]{:S(2)}) collective-permute-start(bf16[4,4,128,128]{3,2,1,0:T(8,128)(2,1)S(1)} %fusion), channel_id=1, source_target_pairs={{0,28},{1,21},{2,30},{3,23},{4,16},{5,25},{6,18},{7,27},{8,20},{9,... | collective-permute-start | bytes 1572872 | tf_op jit(solution)/shard_map/ppermute | solution.py:49
  48.7 10.3 %collective-permute-start.11 = (bf16[2432,128]{1,0:T(8,128)(2,1)}, bf16[2432,128]{1,0:T(8,128)(2,1)}, u32[]{:S(2)}, u32[]{:S(2)}) collective-permute-start(bf16[2432,128]{1,0:T(8,128)(2,1)} %pad_maximum_fusion.2), channel_id=1, source_target_pairs={{0,208},{1,81},{2,210},{3,83},{4,84},{5,213},{6,86},{7,215},{8,216... | collective-permute-start | bytes 1867784 | tf_op jit(solution)/shard_map/ppermute | solution.py:49
  48.7 12.3 %copy-start.12 = (f32[2,4,4,128,128]{4,3,2,1,0:T(8,128)S(1)}, f32[2,4,4,128,128]{4,3,2,1,0:T(8,128)}, u32[]{:S(2)}) copy-start(f32[2,4,4,128,128]{4,3,2,1,0:T(8,128)} %get-tuple-element.66) | copy-start | bytes 6291460
  48.7 12.3 %copy-start.18 = (bf16[2,4,4,128,128]{4,3,2,1,0:T(8,128)(2,1)S(1)}, bf16[2,4,4,128,128]{4,3,2,1,0:T(8,128)(2,1)}, u32[]{:S(2)}) copy-start(bf16[2,4,4,128,128]{4,3,2,1,0:T(8,128)(2,1)} %copy-done.17) | copy-start | bytes 3145732
  48.7 12.4 %collective-permute-start.12 = (bf16[4,640,128]{2,1,0:T(8,128)(2,1)}, bf16[4,640,128]{2,1,0:T(8,128)(2,1)S(1)}, u32[]{:S(2)}, u32[]{:S(2)}) collective-permute-start(bf16[4,640,128]{2,1,0:T(8,128)(2,1)} %collective-permute-done.8), channel_id=1, source_target_pairs={{0,17},{1,18},{2,19},{3,48},{4,55},{5,20},{6,21},{7,22},{8,25},{9,... | collective-permute-start | bytes 1966088 | tf_op jit(solution)/shard_map/ppermute | solution.py:49
  61.2 1.7 %copy-start.21 = (bf16[4,640,128]{2,1,0:T(8,128)(2,1)}, bf16[4,640,128]{2,1,0:T(8,128)(2,1)S(1)}, u32[]{:S(2)}) copy-start(bf16[4,640,128]{2,1,0:T(8,128)(2,1)S(1)} %collective-permute-done.12) | copy-start | bytes 1966084
  61.3 7.1 %collective-permute-start.14 = (bf16[2,4,128,128]{3,2,1,0:T(8,128)(2,1)S(1)}, bf16[2,4,128,128]{3,2,1,0:T(8,128)(2,1)S(1)}, u32[]{:S(2)}, u32[]{:S(2)}) collective-permute-start(bf16[2,4,128,128]{3,2,1,0:T(8,128)(2,1)S(1)} %slice.176), channel_id=1, source_target_pairs={{0,20},{1,29},{2,22},{3,31},{4,24},{5,17},{6,26},{7,19},{8,28},{9,... | collective-permute-start | bytes 786440 | tf_op jit(solution)/shard_map/ppermute | solution.py:49
  62.9 8.1 %collective-permute-start.13 = (bf16[1408,128]{1,0:T(8,128)(2,1)S(1)}, bf16[1408,128]{1,0:T(8,128)(2,1)S(1)}, u32[]{:S(2)}, u32[]{:S(2)}) collective-permute-start(bf16[1408,128]{1,0:T(8,128)(2,1)S(1)} %pad_maximum_fusion.5), channel_id=1, source_target_pairs={{0,80},{1,209},{2,82},{3,211},{4,212},{5,85},{6,214},{7,87},{8,88}... | collective-permute-start | bytes 1081352 | tf_op jit(solution)/shard_map/ppermute | solution.py:49
  71.1 7.1 %copy-start.15 = (bf16[4,640,128]{2,1,0:T(8,128)(2,1)S(1)}, bf16[4,640,128]{2,1,0:T(8,128)(2,1)}, u32[]{:S(2)}) copy-start(bf16[4,640,128]{2,1,0:T(8,128)(2,1)} %copy-done.14) | copy-start | bytes 1966084
  71.1 7.1 %copy-start.20 = (bf16[4,640,128]{2,1,0:T(8,128)(2,1)S(1)}, bf16[4,640,128]{2,1,0:T(8,128)(2,1)}, u32[]{:S(2)}) copy-start(bf16[4,640,128]{2,1,0:T(8,128)(2,1)} %copy-done.19) | copy-start | bytes 1966084
  71.1 7.1 %copy-start.22 = (bf16[4,640,128]{2,1,0:T(8,128)(2,1)S(1)}, bf16[4,640,128]{2,1,0:T(8,128)(2,1)}, u32[]{:S(2)}) copy-start(bf16[4,640,128]{2,1,0:T(8,128)(2,1)} %copy-done.21) | copy-start | bytes 1966084
  71.2 4.8 %collective-permute-start.16 = (bf16[4,128,128]{2,1,0:T(8,128)(2,1)S(1)}, bf16[4,128,128]{2,1,0:T(8,128)(2,1)S(1)}, u32[]{:S(2)}, u32[]{:S(2)}) collective-permute-start(bf16[4,128,128]{2,1,0:T(8,128)(2,1)S(1)} %fusion.6), channel_id=1, source_target_pairs={{0,28},{1,21},{2,30},{3,23},{4,16},{5,25},{6,18},{7,27},{8,20},{9,... | collective-permute-start | bytes 393224 | tf_op jit(solution)/shard_map/ppermute | solution.py:49
  72.0 4.7 %collective-permute-start.15 = (bf16[4,128,128]{2,1,0:T(8,128)(2,1)S(1)}, bf16[4,128,128]{2,1,0:T(8,128)(2,1)S(1)}, u32[]{:S(2)}, u32[]{:S(2)}) collective-permute-start(bf16[4,128,128]{2,1,0:T(8,128)(2,1)S(1)} %fusion.2), channel_id=1, source_target_pairs={{0,208},{1,81},{2,210},{3,83},{4,84},{5,213},{6,86},{7,215},{8,216... | collective-permute-start | bytes 393224 | tf_op jit(solution)/shard_map/ppermute | solution.py:49
  72.0 4.8 %collective-permute-start.17 = (bf16[384,128]{1,0:T(8,128)(2,1)S(1)}, bf16[384,128]{1,0:T(8,128)(2,1)S(1)}, u32[]{:S(2)}, u32[]{:S(2)}) collective-permute-start(bf16[384,128]{1,0:T(8,128)(2,1)S(1)} %slice_select_fusion), channel_id=1, source_target_pairs={{0,17},{1,16},{2,19},{3,18},{4,21},{5,20},{6,23},{7,22},{8,25},{9,... | collective-permute-start | bytes 294920 | tf_op jit(solution)/shard_map/ppermute | solution.py:49
  76.8 7.1 %collective-permute-start.18 = (f32[2,2,128,128]{3,2,1,0:T(8,128)S(1)}, f32[2,2,128,128]{3,2,1,0:T(8,128)S(1)}, u32[]{:S(2)}, u32[]{:S(2)}) collective-permute-start(f32[2,2,128,128]{3,2,1,0:T(8,128)S(1)} %slice.115), channel_id=1, source_target_pairs={{0,17},{1,18},{2,19},{3,48},{4,55},{5,20},{6,21},{7,22},{8,25},{9,... | collective-permute-start | bytes 786440 | tf_op jit(solution)/shard_map/ppermute | solution.py:49
  79.6 33.2 %copy-start = (bf16[4,4,640,128]{3,2,1,0:T(8,128)(2,1)}, bf16[4,4,640,128]{3,2,1,0:T(8,128)(2,1)S(1)}, u32[]{:S(2)}) copy-start(bf16[4,4,640,128]{3,2,1,0:T(8,128)(2,1)S(1)} %pad_maximum_fusion.w_ref) | copy-start | bytes 7864324
  79.6 8.1 %collective-permute-start.19 = (bf16[2,384,128]{2,1,0:T(8,128)(2,1)S(1)}, bf16[2,384,128]{2,1,0:T(8,128)(2,1)S(1)}, u32[]{:S(2)}, u32[]{:S(2)}) collective-permute-start(bf16[2,384,128]{2,1,0:T(8,128)(2,1)S(1)} %pad_maximum_fusion.8), channel_id=1, source_target_pairs={{0,51},{1,18},{2,17},{3,48},{4,55},{5,22},{6,21},{7,52},{8,59},{9,... | collective-permute-start | bytes 589832 | tf_op jit(solution)/shard_map/ppermute | solution.py:49
  87.8 7.7 %collective-permute-start.23 = (bf16[4,384,128]{2,1,0:T(8,128)(2,1)S(1)}, bf16[4,384,128]{2,1,0:T(8,128)(2,1)S(1)}, u32[]{:S(2)}, u32[]{:S(2)}) collective-permute-start(bf16[4,384,128]{2,1,0:T(8,128)(2,1)S(1)} %constant_dynamic-update-slice_fusion.2), channel_id=1, source_target_pairs={{0,28},{1,21},{2,30},{3,23},{4,16},{5,25},{6,18},{7,27},{8,20},{9,... | collective-permute-start | bytes 1179656 | tf_op jit(solution)/shard_map/ppermute | solution.py:49
  89.7 4.7 %collective-permute-start.20 = (f32[2,128,128]{2,1,0:T(8,128)S(1)}, f32[2,128,128]{2,1,0:T(8,128)S(1)}, u32[]{:S(2)}, u32[]{:S(2)}) collective-permute-start(f32[2,128,128]{2,1,0:T(8,128)S(1)} %fusion.7), channel_id=1, source_target_pairs={{0,51},{1,16},{2,17},{3,18},{4,21},{5,22},{6,23},{7,52},{8,59},{9,... | collective-permute-start | bytes 393224 | tf_op jit(solution)/shard_map/ppermute | solution.py:49
  95.6 15.9 %collective-permute-start.25 = (bf16[2,4,384,128]{3,2,1,0:T(8,128)(2,1)S(1)}, bf16[2,4,384,128]{3,2,1,0:T(8,128)(2,1)}, u32[]{:S(2)}, u32[]{:S(2)}) collective-permute-start(bf16[2,4,384,128]{3,2,1,0:T(8,128)(2,1)S(1)} %pad_maximum_fusion.1), channel_id=1, source_target_pairs={{0,20},{1,29},{2,22},{3,31},{4,24},{5,17},{6,26},{7,19},{8,28},{9,... | collective-permute-start | bytes 2359304 | tf_op jit(solution)/shard_map/ppermute | solution.py:49
  96.5 7.1 %collective-permute-start.21 = (bf16[2,128,128]{2,1,0:T(8,128)(2,1)S(1)}, bf16[2,128,128]{2,1,0:T(8,128)(2,1)S(1)}, u32[]{:S(2)}, u32[]{:S(2)}) collective-permute-start(bf16[2,128,128]{2,1,0:T(8,128)(2,1)S(1)} %fusion.10), channel_id=1, source_target_pairs={{0,32},{1,33},{2,34},{3,35},{4,36},{5,37},{6,38},{7,39},{8,40},{9,... | collective-permute-start | bytes 196616 | tf_op jit(solution)/shard_map/ppermute | solution.py:49
  104.3 6.2 %collective-permute-start.22 = (f32[2,128,128]{2,1,0:T(8,128)}, f32[2,128,128]{2,1,0:T(8,128)}, u32[]{:S(2)}, u32[]{:S(2)}) collective-permute-start(f32[2,128,128]{2,1,0:T(8,128)} %get-tuple-element.106), channel_id=1, source_target_pairs={{0,208},{1,81},{2,210},{3,83},{4,84},{5,213},{6,86},{7,215},{8,216... | collective-permute-start | bytes 393224 | tf_op jit(solution)/shard_map/ppermute | solution.py:49
  112.8 1.1 copy-start.5
  113.9 3.9 %copy-start.1 = (bf16[4,4,384,128]{3,2,1,0:T(8,128)(2,1)}, bf16[4,4,384,128]{3,2,1,0:T(8,128)(2,1)S(1)}, u32[]{:S(2)}) copy-start(bf16[4,4,384,128]{3,2,1,0:T(8,128)(2,1)S(1)} %constant_dynamic-update-slice_fusion.4.r_ref) | copy-start | bytes 4718596
  113.9 14.4 %copy-start.3 = (bf16[384,1024]{1,0:T(8,128)(2,1)S(1)}, bf16[384,1024]{1,0:T(8,128)(2,1)}, u32[]{:S(2)}) copy-start(bf16[384,1024]{1,0:T(8,128)(2,1)} %cot_ref.1) | copy-start | bytes 2359300
  117.8 10.5 %collective-permute-start.26 = (bf16[384,2048]{1,0:T(8,128)(2,1)}, bf16[384,2048]{1,0:T(8,128)(2,1)S(1)}, u32[]{:S(2)}, u32[]{:S(2)}) collective-permute-start(bf16[384,2048]{1,0:T(8,128)(2,1)} %shard_map.113), channel_id=1, source_target_pairs={{0,16},{1,17},{2,18},{3,19},{4,20},{5,21},{6,22},{7,23},{8,24},{9,... | collective-permute-start | bytes 4718600 | tf_op jit(solution)/shard_map/ppermute | solution.py:49
  121.0 7.0 %collective-permute-start.24 = (f32[2,2,128,128]{3,2,1,0:T(8,128)S(1)}, f32[2,2,128,128]{3,2,1,0:T(8,128)S(1)}, u32[]{:S(2)}, u32[]{:S(2)}) collective-permute-start(f32[2,2,128,128]{3,2,1,0:T(8,128)S(1)} %pad_maximum_fusion.7), channel_id=1, source_target_pairs={{0,80},{1,209},{2,82},{3,211},{4,212},{5,85},{6,214},{7,87},{8,88}... | collective-permute-start | bytes 786440 | tf_op jit(solution)/shard_map/ppermute | solution.py:49
  128.0 8.2 %collective-permute-start.27 = (f32[4,2,128,128]{3,2,1,0:T(8,128)S(1)}, f32[4,2,128,128]{3,2,1,0:T(8,128)S(1)}, u32[]{:S(2)}, u32[]{:S(2)}) collective-permute-start(f32[4,2,128,128]{3,2,1,0:T(8,128)S(1)} %pad_maximum_fusion.4.mine_ref), channel_id=1, source_target_pairs={{0,16},{1,17},{2,18},{3,19},{4,20},{5,21},{6,22},{7,23},{8,24},{9,... | collective-permute-start | bytes 1572872 | tf_op jit(solution)/shard_map/ppermute | solution.py:49
  128.3 1.4 %copy-start.2 = (bf16[4,4,384,128]{3,2,1,0:T(8,128)(2,1)S(1)}, bf16[4,4,384,128]{3,2,1,0:T(8,128)(2,1)}, u32[]{:S(2)}) copy-start(bf16[4,4,384,128]{3,2,1,0:T(8,128)(2,1)} %copy-done.1) | copy-start | bytes 4718596
  129.7 6.5 %copy-start.6 = (f32[256,640]{1,0:T(8,128)S(1)}, f32[256,640]{1,0:T(8,128)}, u32[]{:S(2)}) copy-start(f32[256,640]{1,0:T(8,128)} %m_ref.1) | copy-start | bytes 1966084
  129.7 6.5 %copy-start.7 = (f32[256,640]{1,0:T(8,128)S(1)}, f32[256,640]{1,0:T(8,128)}, u32[]{:S(2)}) copy-start(f32[256,640]{1,0:T(8,128)} %v_ref.1) | copy-start | bytes 1966084

commit v3 on v2

--- a/solution.py
+++ b/solution.py
@@ -80,12 +80,6 @@
     rep, fsdp = lax.axis_index("rep"), lax.axis_index("fsdp")
     y, x, zl = rep // 4, fsdp // 4, fsdp % 4
     return {"y": y, "zh": rep // 2 % 2, "c": rep % 2 ^ (x + y + zl) % 2, "x": x, "zl": zl}
-
-
-def ride(value, rider, route):
-    rows = value.size // 128
-    got = send(jnp.concatenate([value.reshape(rows, 128), rider]), route)
-    return got[:rows].reshape(value.shape), got[rows:]
 
 
 def together(*values):
@@ -162,22 +156,25 @@
     )(order, tokens, their_tokens, cot, their_cot)
 
 
-def rows_kernel(s_ref, w_ref, d_ref, kept_ref, host_ref):
+def kept_kernel(s_ref, w_ref, o_ref):
     mine = pl.ds(pl.multiple_of(s_ref[0] * 128, 128), 128)
-    kept_ref[...] = w_ref[mine, :640].T
-    host_ref[...] = (w_ref[:, 640:].astype(F32) + d_ref[0]).astype(BF16).T
-
-
-def projection_rows(order, weight, delayed):
-    vmem = pl.BlockSpec(memory_space=pltpu.VMEM)
+    o_ref[...] = w_ref[mine, :640].T
+
+
+def refreshed_kernel(w_ref, d_ref, o_ref):
+    o_ref[...] = (w_ref[:, 640:].astype(F32) + d_ref[0]).astype(BF16).T
+
+
+def rows_call(kernel, shape, *args):
+    vmem, smem = pl.BlockSpec(memory_space=pltpu.VMEM), pl.BlockSpec(memory_space=pltpu.SMEM)
     return pl.pallas_call(
-        rows_kernel,
-        out_shape=(jax.ShapeDtypeStruct((640, 128), BF16), jax.ShapeDtypeStruct((384, 256), BF16)),
-        in_specs=[pl.BlockSpec(memory_space=pltpu.SMEM), vmem, vmem],
-        out_specs=(vmem, vmem),
+        kernel,
+        out_shape=jax.ShapeDtypeStruct(shape, BF16),
+        in_specs=[smem if arg.ndim == 1 else vmem for arg in args],
+        out_specs=vmem,
         compiler_params=pltpu.CompilerParams(vmem_limit_bytes=16 << 20),
         cost_estimate=pl.CostEstimate(flops=1 << 17, bytes_accessed=1 << 20, transcendentals=0),
-    )(order, weight, delayed)
+    )(*args)
 
 
 def product(s_ref, cot_ref, w_ref, r_ref, at):
@@ -214,7 +211,7 @@
         out_specs=vmem,
         compiler_params=pltpu.CompilerParams(vmem_limit_bytes=32 << 20),
         cost_estimate=pl.CostEstimate(
-            flops=2 * 384 * 2048 * 1024, bytes_accessed=3 << 20, transcendentals=0
+            flops=6 * 384 * 2048 * 1024, bytes_accessed=12 << 20, transcendentals=0
         ),
     )(where, cot, kept, host)
 
@@ -233,7 +230,7 @@
             pl.BlockSpec((384, 512), lambda x: (0, x)),
         ],
         out_specs=pl.BlockSpec((384, 1024), lambda x: (0, x)),
-        compiler_params=pltpu.CompilerParams(vmem_limit_bytes=48 << 20),
+        compiler_params=pltpu.CompilerParams(vmem_limit_bytes=36 << 20),
         cost_estimate=pl.CostEstimate(
             flops=2 * 384 * 2048 * 1024, bytes_accessed=9 << 20, transcendentals=0
         ),
@@ -292,13 +289,14 @@
 
     their_cot = send(cotangent, flip("c"))
     their_tokens = send(tokens, flip("c"))
-    kept, refreshed = projection_rows(order, weight, delayed)
-    kept_got = send(kept, partner("x", False))
+    kept = rows_call(kept_kernel, (640, 128), order, weight)
+    refreshed = rows_call(refreshed_kernel, (384, 256), weight, delayed)
     for_zh = send(
         refreshed,
         lambda c: dict(c, zh=1, zl=c["zl"] ^ 1) if c["y"] == c["zh"] == 0 and has_host(c) else None,
     )
-    order, kept, kept_got = together(order, kept, kept_got)
+    kept_got = send(kept, partner("x", False))
+    order, kept, kept_got, refreshed = together(order, kept, kept_got, refreshed)
     kept = jnp.stack([kept, kept_got])
     kept_got = send(kept, partner("x", True))
     order, kept = together(order, kept)
@@ -320,6 +318,7 @@
         lambda c: dict(c, c=1 - c["c"]) if c["y"] == 0 and has_host(c) else None,
     )
     one_held, two_held = chip_gradient(True, order, tokens, their_tokens, cotangent, their_cot)
+    one_held, two_held, one_got, two_got = together(one_held, two_held, one_got, two_got)
     one_far = (one_held[0] + one_got[0].astype(F32)).astype(BF16)
     two_far = (two_held[0] + two_got[0].astype(F32)).astype(BF16)
     host = jnp.where(first, jnp.where(core == 0, lower, upper), for_core)
@@ -328,23 +327,25 @@
     )
 
     one_got2 = send(one_far, partner("x", False))
-    two_got2, host_got = ride(two_far, host, partner("y", False))
+    two_got2 = send(two_far, partner("y", False))
+    by_y = [send(host, lambda c, k=k: dict(c, y=k) if c["y"] == 0 else None) for k in (1, 3, 2)]
     kept_c = send(kept_b, partner("zl", True))
     one = one_held[1] + one_got[1].astype(F32) + one_got2.astype(F32)
     two = two_held[1] + two_got[1].astype(F32) + two_got2.astype(F32)
-    host = jnp.where(y == jnp.where(core == 0, 3, 1), host_got, host)
+    host = jnp.where(y == 0, host, jnp.where(y == 1, by_y[0], jnp.where(y == 3, by_y[1], by_y[2])))
     one, two, host, kept_c = together(one, two, host, kept_c)
 
-    one_got, host_got = ride(one[:2].astype(BF16), host, partner("y", True))
+    one_got = send(one[:2].astype(BF16), partner("y", True))
+    host_got = send(host, neighbour("zl", 1))
     two_got = send(two[:2].astype(BF16), partner("x", True))
     one_far = (one[2] + one_got[0].astype(F32)).astype(BF16)
     two_far = (two[2] + two_got[0].astype(F32)).astype(BF16)
-    host = jnp.where((y == 2) | (y == jnp.where(core == 0, 1, 3)), host_got, host)
-    one_far, two_far, host = together(one_far, two_far, host)
+    one_far, two_far, host, host_got = together(one_far, two_far, host, host_got)
 
     one_got2 = send(one_far, partner("y", False))
     two_got2 = send(two_far, partner("x", False))
-    host_got = send(host, neighbour("zl", 1))
+    host = jnp.stack([host, host_got])
+    host_got = send(host, neighbour("zl", 3))
     both = jnp.stack(
         [
             one[3] + one_got[1].astype(F32) + one_got2.astype(F32),
@@ -355,33 +356,29 @@
     both, host, host_got = together(both, host, host_got)
 
     got = send(both[:2], partner("zl", True))
-    host = jnp.stack([host, host_got])
-    host_got = send(host, neighbour("zl", 3))
+    host = jnp.concatenate([host, host_got])
+    host_got = send(host, partner("x", False))
     kept = jnp.stack([kept, kept_b, kept_a, kept_c])
     far = both[2] + got[0]
     far, host, host_got, kept = together(far, host, host_got, kept)
     got2 = send(far, partner("zl", False))
-    host = jnp.concatenate([host, host_got])
-    host_got = send(host, partner("x", False))
+    host = jnp.stack([host, host_got])
+    host_got = send(host, partner("x", True))
     total = (both[3] + got[1] + got2).astype(BF16)
     total, host = together(total, host)
     zh_got = send(total, flip("zh"))
-    host = jnp.stack([host, host_got])
-    host_got = send(host, partner("x", True))
-    total = total.astype(F32) + zh_got.astype(F32)
-    mine_got = send(total, partner("y", False))
-    mine = jnp.stack([total, mine_got])
-    mine, host = together(mine, host)
-    mine_got = send(mine, partner("y", True))
 
     host = jnp.concatenate([host, host_got])
     theirs = their_input_gradient(where, their_cot, kept, host)
+    total, zh_got, theirs = together(total, zh_got, theirs)
     got = send(theirs, flip("c"))
+    total = total.astype(F32) + zh_got.astype(F32)
+    mine = jnp.stack([total, send(total, partner("y", False))])
+    mine_got = send(mine, partner("y", True))
+    grad_input = our_input_gradient(where, cotangent, kept, host, got)
+    mine, mine_got, grad_input = together(mine, mine_got, grad_input)
     mine = jnp.concatenate([mine, mine_got])
-    mine, theirs = together(mine, theirs)
     other = send(mine, flip("c"))
-    grad_input = our_input_gradient(where, cotangent, kept, host, got)
-    mine, grad_input = together(mine, grad_input)
     return (grad_input, *finish(norm_factor, where_y, mine, other, moment, second))
 
 

time: 139 us -> 130 us (0.935)
  waiting for transfers between devices: 55.3 us -> 44.8 us
  local copies, waits for them, and re-layouts: 9.21 us -> 12.5 us
  Pallas kernels: 26.7 us -> 24.3 us
    ppermute x28 -> x31, waiting for transfers between devices: 55.3 us -> 44.8 us  [send(): return lax.ppermute(value, AXES, pairs)]
    unnamed x49 -> x44, local copies, waits for them, and re-layouts: 5.76 us -> 9.11 us
    another operation x2, other arithmetic: 1.6 us -> 0.04 us  [on_device(): mine = jnp.stack([total, send(total, partner('y', False))])]
    ppermute x28 -> x31, starting transfers between devices: 37.2 us -> 38.3 us  [send(): return lax.ppermute(value, AXES, pairs)]
  transfers between devices with their start and end apart: 28 -> 31, of which waited for: 17 -> 18; matrix products, arithmetic and copies ran while one was open for 8% -> 9% of each run, Pallas kernels for 15% -> 17%
where the time goes in v3:
time: 130 us; the launch traced here: 129 us
  waiting for transfers between devices  44.8 us (34%)
  starting transfers between devices  38.3 us (29%)
  Pallas kernels  24.3 us (19%)
  local copies, waits for them, and re-layouts  12.5 us (10%)
  other arithmetic  8.09 us (6%)
    ppermute x31, waiting for transfers between devices, send(): return lax.ppermute(value, AXES, pairs)  44.8 us
    ppermute x31, starting transfers between devices, send(): return lax.ppermute(value, AXES, pairs)  38.3 us
    pallas_call x2, Pallas kernels, chip_gradient(): pl.pallas_call(functools.partial(grad_kernel, keep), out_shape=(jax.Shape...  13.4 us
    unnamed x44, local copies, waits for them, and re-layouts  9.11 us
    pallas_call x1, Pallas kernels, our_input_gradient(): pl.pallas_call(ours_kernel, out_shape=jax.ShapeDtypeStruct((384, 4096), B...  5.13 us
    convert_element_type x1, other arithmetic, on_device(): one_far = (one_held[0] + one_got[0].astype(F32)).astype(BF16)  2.81 us
    pallas_call x1, Pallas kernels, their_input_gradient(): pl.pallas_call(theirs_kernel, out_shape=jax.ShapeDtypeStruct((384, 2048),...  2.74 us
  transfers between devices with their start and end apart: 31, of which 18 were waited for; matrix products, arithmetic and copies ran while one was open for 9% of the time, Pallas kernels for 17%

profile of v3, /device:TPU:1, one launch (start us, length us, event | category | flops | bytes accessed | tf_op | source)
XLA Modules:
  0.0 129.2 jit_solution(14169818564426174050)
XLA Ops:
  0.6 3.3 %collective-permute-start.1 = (bf16[384,4096]{1,0:T(8,128)(2,1)}, bf16[384,4096]{1,0:T(8,128)(2,1)}, u32[]{:S(2)}, u32[]{:S(2)}) collective-permute-start(bf16[384,4096]{1,0:T(8,128)(2,1)} %t_hbm.3), channel_id=1, source_target_pairs={{0,16},{1,17},{2,18},{3,19},{4,20},{5,21},{6,22},{7,23},{8,24},{9,... | collective-permute-start | bytes 9437192 | tf_op jit(solution)/shard_map/ppermute | solution.py:49
  4.2 1.0 copy-done.3
  5.2 0.6 shard_map.110
  6.0 1.0 copy-done.4
  7.0 1.0 copy-done.7
  8.1 2.9 %collective-permute-done = bf16[640,128]{1,0:T(8,128)(2,1)S(1)} collective-permute-done((bf16[640,128]{1,0:T(8,128)(2,1)S(1)}, bf16[640,128]{1,0:T(8,128)(2,1)S(1)}, u32[]{:S(2)}, u32[]{:S(2)}) %collective-permute-start) | collective-permute-done | bytes 163872 | tf_op jit(solution)/shard_map/ppermute | solution.py:49
  11.0 0.8 collective-permute-start.3
  11.8 0.7 collective-permute-start.4
  12.6 0.9 copy-done.1
  13.5 6.3 %shard_map.112 = (bf16[2,4,4,128,128]{4,3,2,1,0:T(8,128)(2,1)}, bf16[2,4,4,128,128]{4,3,2,1,0:T(8,128)(2,1)}) custom-call(s32[13]{0:T(128)} %copy-done.8, bf16[384,4096]{1,0:T(8,128)(2,1)} %t_hbm.3, bf16[384,4096]{1,0:T(8,128)(2,1)} %collective-permute-done.1.u_hbm, bf16[384,1024]{1,0:T(8,128)(2,1)} %cot_ref.1, bf16[384,1024]{1,0:T(8,128)(2,1)} %copy-done.1), custom_call_target="tpu_custom_call" | custom-call | flops 1610612736 | bytes 9437184 | tf_op jit(solution)/shard_map/pallas_call | solution.py:144
  19.9 0.7 copy-done.18
  20.6 8.2 %collective-permute-start.5 = (bf16[2,4,4,128,128]{4,3,2,1,0:T(8,128)(2,1)}, bf16[2,4,4,128,128]{4,3,2,1,0:T(8,128)(2,1)S(1)}, u32[]{:S(2)}, u32[]{:S(2)}) collective-permute-start(bf16[2,4,4,128,128]{4,3,2,1,0:T(8,128)(2,1)} %get-tuple-element.70), channel_id=1, source_target_pairs={{0,20},{1,29},{2,22},{3,31},{4,24},{5,17},{6,26},{7,19},{8,28},{9,... | collective-permute-start | bytes 3145736 | tf_op jit(solution)/shard_map/ppermute | solution.py:49
  28.8 1.0 constant_dynamic-update-slice_fusion
  29.8 1.0 collective-permute-start.7
  30.8 0.9 collective-permute-start.8
  31.7 1.3 %collective-permute-start.9 = (bf16[384,128]{1,0:T(8,128)(2,1)S(1)}, bf16[384,128]{1,0:T(8,128)(2,1)S(1)}, u32[]{:S(2)}, u32[]{:S(2)}) collective-permute-start(bf16[384,128]{1,0:T(8,128)(2,1)S(1)} %broadcast_select_fusion.1), channel_id=1, source_target_pairs={{0,16},{1,17},{2,18},{3,19},{4,20},{5,21},{6,22},{7,23},{8,24},{9,... | collective-permute-start | bytes 294920 | tf_op jit(solution)/shard_map/ppermute | solution.py:49
  33.0 7.1 %shard_map.113 = (f32[2,4,4,128,128]{4,3,2,1,0:T(8,128)}, f32[2,4,4,128,128]{4,3,2,1,0:T(8,128)}) custom-call(s32[13]{0:T(128)} %copy-done.8, bf16[384,4096]{1,0:T(8,128)(2,1)} %t_hbm.3, bf16[384,4096]{1,0:T(8,128)(2,1)} %collective-permute-done.1.u_hbm, bf16[384,1024]{1,0:T(8,128)(2,1)} %cot_ref.1, bf16[384,1024]{1,0:T(8,128)(2,1)} %copy-done.1), custom_call_target="tpu_custom_call" | custom-call | flops 1610612736 | bytes 9437184 | tf_op jit(solution)/shard_map/pallas_call | solution.py:144
  40.2 1.6 %collective-permute-done.5 = bf16[2,4,4,128,128]{4,3,2,1,0:T(8,128)(2,1)S(1)} collective-permute-done((bf16[2,4,4,128,128]{4,3,2,1,0:T(8,128)(2,1)}, bf16[2,4,4,128,128]{4,3,2,1,0:T(8,128)(2,1)S(1)}, u32[]{:S(2)}, u32[]{:S(2)}) %collective-permute-start.5) | collective-permute-done | bytes 1048608 | tf_op jit(solution)/shard_map/ppermute | solution.py:49
  41.8 3.0 %collective-permute-done.6 = bf16[2,4,4,128,128]{4,3,2,1,0:T(8,128)(2,1)S(1)} collective-permute-done((bf16[2,4,4,128,128]{4,3,2,1,0:T(8,128)(2,1)}, bf16[2,4,4,128,128]{4,3,2,1,0:T(8,128)(2,1)S(1)}, u32[]{:S(2)}, u32[]{:S(2)}) %collective-permute-start.6) | collective-permute-done | bytes 1048608 | tf_op jit(solution)/shard_map/ppermute | solution.py:49
  44.7 1.0 copy-done.11
  45.7 2.8 %fusion = (bf16[4,4,128,128]{3,2,1,0:T(8,128)(2,1)}, bf16[4,4,128,128]{3,2,1,0:T(8,128)(2,1)}) fusion(f32[2,4,4,128,128]{4,3,2,1,0:T(8,128)} %get-tuple-element.72, bf16[2,4,4,128,128]{4,3,2,1,0:T(8,128)(2,1)S(1)} %collective-permute-done.5, bf16[2,4,4,128,128]{4,3,2,1,0:T(8,128)(2,1)S(1)} %collective-permute-done.6, f32[2,4,4,128,128]{4,3,2,1,0:T(8,128)} %get-tuple-element.74), kind=kLoop, calls=%fused_computation.6 | loop fusion | flops 1572864 | bytes 4194304 | tf_op jit(solution)/shard_map/convert_element_type | solution.py:322
  48.6 0.8 copy-done.14
  49.4 0.2 copy-done.16
  49.6 1.4 %collective-permute-start.12 = (bf16[384,128]{1,0:T(8,128)(2,1)S(1)}, bf16[384,128]{1,0:T(8,128)(2,1)S(1)}, u32[]{:S(2)}, u32[]{:S(2)}) collective-permute-start(bf16[384,128]{1,0:T(8,128)(2,1)S(1)} %select_select_fusion.1), channel_id=1, source_target_pairs={{0,80},{1,81},{2,82},{3,83},{4,84},{5,85},{6,86},{7,87},{8,88},{9,... | collective-permute-start | bytes 294920 | tf_op jit(solution)/shard_map/ppermute | solution.py:49
  51.0 1.9 %collective-permute-start.13 = (bf16[384,128]{1,0:T(8,128)(2,1)S(1)}, bf16[384,128]{1,0:T(8,128)(2,1)}, u32[]{:S(2)}, u32[]{:S(2)}) collective-permute-start(bf16[384,128]{1,0:T(8,128)(2,1)S(1)} %select_select_fusion.1), channel_id=1, source_target_pairs={{0,208},{1,209},{2,210},{3,211},{4,212},{5,213},{6,214},{7,215},{8... | collective-permute-start | bytes 294920 | tf_op jit(solution)/shard_map/ppermute | solution.py:49
  53.0 1.9 %collective-permute-start.14 = (bf16[384,128]{1,0:T(8,128)(2,1)S(1)}, bf16[384,128]{1,0:T(8,128)(2,1)}, u32[]{:S(2)}, u32[]{:S(2)}) collective-permute-start(bf16[384,128]{1,0:T(8,128)(2,1)S(1)} %select_select_fusion.1), channel_id=1, source_target_pairs={{0,128},{1,129},{2,130},{3,131},{4,132},{5,133},{6,134},{7,135},{8... | collective-permute-start | bytes 294920 | tf_op jit(solution)/shard_map/ppermute | solution.py:49
  54.9 2.4 %collective-permute-start.15 = (bf16[4,640,128]{2,1,0:T(8,128)(2,1)}, bf16[4,640,128]{2,1,0:T(8,128)(2,1)S(1)}, u32[]{:S(2)}, u32[]{:S(2)}) collective-permute-start(bf16[4,640,128]{2,1,0:T(8,128)(2,1)} %copy-done.16), channel_id=1, source_target_pairs={{0,17},{1,18},{2,19},{3,48},{4,55},{5,20},{6,21},{7,22},{8,25},{9,... | collective-permute-start | bytes 1966088 | tf_op jit(solution)/shard_map/ppermute | solution.py:49
  57.3 0.9 select_select_fusion
  58.2 0.5 collective-permute-done.10
  58.7 1.5 %bitcast_add_fusion.1 = f32[4,4,128,128]{3,2,1,0:T(8,128)S(1)} fusion(bf16[4,4,128,128]{3,2,1,0:T(8,128)(2,1)S(1)} %collective-permute-done.10, f32[2,4,4,128,128]{4,3,2,1,0:T(8,128)} %get-tuple-element.72, bf16[2,4,4,128,128]{4,3,2,1,0:T(8,128)(2,1)} %copy-done.13), kind=kLoop, calls=%fused_computation.2 | loop fusion | flops 1048576 | bytes 3145728 | tf_op jit(solution)/shard_map/add | solution.py:333
  60.2 3.7 %collective-permute-done.11 = bf16[4,4,128,128]{3,2,1,0:T(8,128)(2,1)S(1)} collective-permute-done((bf16[4,4,128,128]{3,2,1,0:T(8,128)(2,1)}, bf16[4,4,128,128]{3,2,1,0:T(8,128)(2,1)S(1)}, u32[]{:S(2)}, u32[]{:S(2)}) %collective-permute-start.11) | collective-permute-done | bytes 524320 | tf_op jit(solution)/shard_map/ppermute | solution.py:49
  64.0 0.2 bitcast_add_fusion
  64.2 2.7 %collective-permute-done.15 = bf16[4,640,128]{2,1,0:T(8,128)(2,1)S(1)} collective-permute-done((bf16[4,640,128]{2,1,0:T(8,128)(2,1)}, bf16[4,640,128]{2,1,0:T(8,128)(2,1)S(1)}, u32[]{:S(2)}, u32[]{:S(2)}) %collective-permute-start.15) | collective-permute-done | bytes 655392 | tf_op jit(solution)/shard_map/ppermute | solution.py:49
  67.1 1.9 %collective-permute-start.17 = (bf16[2,4,128,128]{3,2,1,0:T(8,128)(2,1)S(1)}, bf16[2,4,128,128]{3,2,1,0:T(8,128)(2,1)S(1)}, u32[]{:S(2)}, u32[]{:S(2)}) collective-permute-start(bf16[2,4,128,128]{3,2,1,0:T(8,128)(2,1)S(1)} %slice.154), channel_id=1, source_target_pairs={{0,20},{1,29},{2,22},{3,31},{4,24},{5,17},{6,26},{7,19},{8,28},{9,... | collective-permute-start | bytes 786440 | tf_op jit(solution)/shard_map/ppermute | solution.py:49
  69.0 5.0 %collective-permute-done.16 = bf16[2,4,128,128]{3,2,1,0:T(8,128)(2,1)S(1)} collective-permute-done((bf16[2,4,128,128]{3,2,1,0:T(8,128)(2,1)S(1)}, bf16[2,4,128,128]{3,2,1,0:T(8,128)(2,1)S(1)}, u32[]{:S(2)}, u32[]{:S(2)}) %collective-permute-start.16) | collective-permute-done | bytes 262176 | tf_op jit(solution)/shard_map/ppermute | solution.py:49
  74.2 1.3 %collective-permute-start.20 = (bf16[4,128,128]{2,1,0:T(8,128)(2,1)S(1)}, bf16[4,128,128]{2,1,0:T(8,128)(2,1)S(1)}, u32[]{:S(2)}, u32[]{:S(2)}) collective-permute-start(bf16[4,128,128]{2,1,0:T(8,128)(2,1)S(1)} %fusion.5), channel_id=1, source_target_pairs={{0,28},{1,21},{2,30},{3,23},{4,16},{5,25},{6,18},{7,27},{8,20},{9,... | collective-permute-start | bytes 393224 | tf_op jit(solution)/shard_map/ppermute | solution.py:49
  75.5 1.3 %collective-permute-start.19 = (bf16[4,128,128]{2,1,0:T(8,128)(2,1)S(1)}, bf16[4,128,128]{2,1,0:T(8,128)(2,1)S(1)}, u32[]{:S(2)}, u32[]{:S(2)}) collective-permute-start(bf16[4,128,128]{2,1,0:T(8,128)(2,1)S(1)} %fusion.4), channel_id=1, source_target_pairs={{0,208},{1,81},{2,210},{3,83},{4,84},{5,213},{6,86},{7,215},{8,216... | collective-permute-start | bytes 393224 | tf_op jit(solution)/shard_map/ppermute | solution.py:49
  76.8 1.0 collective-permute-start.21
  77.8 0.8 collective-permute-done.20
  78.7 1.5 %collective-permute-done.19 = bf16[4,128,128]{2,1,0:T(8,128)(2,1)S(1)} collective-permute-done((bf16[4,128,128]{2,1,0:T(8,128)(2,1)S(1)}, bf16[4,128,128]{2,1,0:T(8,128)(2,1)S(1)}, u32[]{:S(2)}, u32[]{:S(2)}) %collective-permute-start.19) | collective-permute-done | bytes 131104 | tf_op jit(solution)/shard_map/ppermute | solution.py:49
  80.3 5.1 %collective-permute-done.21 = bf16[2,384,128]{2,1,0:T(8,128)(2,1)S(1)} collective-permute-done((bf16[2,384,128]{2,1,0:T(8,128)(2,1)S(1)}, bf16[2,384,128]{2,1,0:T(8,128)(2,1)S(1)}, u32[]{:S(2)}, u32[]{:S(2)}) %collective-permute-start.21) | collective-permute-done | bytes 196640 | tf_op jit(solution)/shard_map/ppermute | solution.py:49
  85.6 0.9 collective-permute-start.23
  86.5 0.3 pad_maximum_fusion.w_ref
  86.8 6.0 %collective-permute-done.22 = f32[2,2,128,128]{3,2,1,0:T(8,128)S(1)} collective-permute-done((f32[2,2,128,128]{3,2,1,0:T(8,128)S(1)}, f32[2,2,128,128]{3,2,1,0:T(8,128)S(1)}, u32[]{:S(2)}, u32[]{:S(2)}) %collective-permute-start.22) | collective-permute-done | bytes 262176 | tf_op jit(solution)/shard_map/ppermute | solution.py:49
  92.8 0.3 collective-permute-done.23
  93.1 0.9 pad_maximum_fusion.1
  94.1 2.0 %collective-permute-start.26 = (bf16[2,4,384,128]{3,2,1,0:T(8,128)(2,1)}, bf16[2,4,384,128]{3,2,1,0:T(8,128)(2,1)}, u32[]{:S(2)}, u32[]{:S(2)}) collective-permute-start(bf16[2,4,384,128]{3,2,1,0:T(8,128)(2,1)} %pad_maximum_fusion.1), channel_id=1, source_target_pairs={{0,20},{1,29},{2,22},{3,31},{4,24},{5,17},{6,26},{7,19},{8,28},{9,... | collective-permute-start | bytes 2359304 | tf_op jit(solution)/shard_map/ppermute | solution.py:49
  96.1 0.7 dynamic-slice_bitcast_fusion
  96.9 4.0 %collective-permute-done.24 = f32[2,128,128]{2,1,0:T(8,128)} collective-permute-done((f32[2,128,128]{2,1,0:T(8,128)S(1)}, f32[2,128,128]{2,1,0:T(8,128)}, u32[]{:S(2)}, u32[]{:S(2)}) %collective-permute-start.24) | collective-permute-done | bytes 131104 | tf_op jit(solution)/shard_map/ppermute | solution.py:49
  100.9 1.1 fusion.9
  101.9 3.3 %collective-permute-start.25 = (bf16[2,128,128]{2,1,0:T(8,128)(2,1)S(1)}, bf16[2,128,128]{2,1,0:T(8,128)(2,1)S(1)}, u32[]{:S(2)}, u32[]{:S(2)}) collective-permute-start(bf16[2,128,128]{2,1,0:T(8,128)(2,1)S(1)} %fusion.9), channel_id=1, source_target_pairs={{0,32},{1,33},{2,34},{3,35},{4,36},{5,37},{6,38},{7,39},{8,40},{9,... | collective-permute-start | bytes 196616 | tf_op jit(solution)/shard_map/ppermute | solution.py:49
  105.2 1.2 constant_dynamic-update-slice_fusion.5
  106.4 0.6 collective-permute-done.26
  107.0 1.2 constant_dynamic-update-slice_fusion.4.r_ref
  108.3 2.7 %shard_map.114 = bf16[384,2048]{1,0:T(8,128)(2,1)S(1)} custom-call(s32[13]{0:T(128)S(1)} %concatenate.17.s_ref, bf16[384,1024]{1,0:T(8,128)(2,1)S(1)} %copy-done.2, bf16[4,4,640,128]{3,2,1,0:T(8,128)(2,1)S(1)} %pad_maximum_fusion.w_ref, bf16[4,4,384,128]{3,2,1,0:T(8,128)(2,1)S(1)} %constant_dynamic-update-slice_fusion.4.r_ref), custom_call_target="tpu_custom_call" | custom-call | flops 4831838208 | bytes 12582912 | tf_op jit(solution)/shard_map/pallas_call | solution.py:207
  111.1 0.8 collective-permute-start.29
  111.9 0.8 collective-permute-start.27
  112.7 3.9 %collective-permute-done.27 = f32[2,128,128]{2,1,0:T(8,128)S(1)} collective-permute-done((f32[2,128,128]{2,1,0:T(8,128)S(1)}, f32[2,128,128]{2,1,0:T(8,128)S(1)}, u32[]{:S(2)}, u32[]{:S(2)}) %collective-permute-start.27) | collective-permute-done | bytes 131104 | tf_op jit(solution)/shard_map/ppermute | solution.py:49
  116.7 0.7 collective-permute-start.28
  117.3 5.1 %shard_map.115 = bf16[384,4096]{1,0:T(8,128)(2,1)} custom-call(s32[13]{0:T(128)S(1)} %concatenate.17.s_ref, bf16[384,1024]{1,0:T(8,128)(2,1)S(1)} %copy-done, bf16[4,4,640,128]{3,2,1,0:T(8,128)(2,1)S(1)} %pad_maximum_fusion.w_ref, bf16[4,4,384,128]{3,2,1,0:T(8,128)(2,1)S(1)} %constant_dynamic-update-slice_fusion.4.r_ref, ...), custom_call_target="tpu_custom_call" | custom-call | flops 1610612736 | bytes 9437184 | tf_op jit(solution)/shard_map/pallas_call | solution.py:221
  122.5 1.3 %collective-permute-done.28 = f32[2,2,128,128]{3,2,1,0:T(8,128)S(1)} collective-permute-done((f32[2,2,128,128]{3,2,1,0:T(8,128)S(1)}, f32[2,2,128,128]{3,2,1,0:T(8,128)S(1)}, u32[]{:S(2)}, u32[]{:S(2)}) %collective-permute-start.28) | collective-permute-done | bytes 262176 | tf_op jit(solution)/shard_map/ppermute | solution.py:49
  124.1 1.7 %collective-permute-done.30.other_ref = f32[4,2,128,128]{3,2,1,0:T(8,128)S(1)} collective-permute-done((f32[4,2,128,128]{3,2,1,0:T(8,128)S(1)}, f32[4,2,128,128]{3,2,1,0:T(8,128)S(1)}, u32[]{:S(2)}, u32[]{:S(2)}) %collective-permute-start.30) | collective-permute-done | bytes 524320 | tf_op jit(solution)/shard_map/ppermute | solution.py:49
  125.8 1.1 copy-done.6
  126.9 2.2 %shard_map.116 = (f32[256,640]{1,0:T(8,128)}, f32[256,640]{1,0:T(8,128)}, f32[256,640]{1,0:T(8,128)}, f32[256,384]{1,0:T(8,128)}) custom-call(s32[9]{0:T(128)S(1)} %stack.205.s_ref, f32[4,2,128,128]{3,2,1,0:T(8,128)S(1)} %constant_dynamic-update-slice_fusion.6.mine_ref, f32[4,2,128,128]{3,2,1,0:T(8,128)S(1)} %collective-permute-done.30.other_ref, ...), custom_call_target="tpu_custom_call" | custom-call | flops 4194304 | bytes 6291456 | tf_op jit(solution)/shard_map/pallas_call | solution.py:263
  (80 shorter events, 1.6 us)
Async XLA Ops:
  0.6 12.0 %collective-permute-start.1 = (bf16[384,4096]{1,0:T(8,128)(2,1)}, bf16[384,4096]{1,0:T(8,128)(2,1)}, u32[]{:S(2)}, u32[]{:S(2)}) collective-permute-start(bf16[384,4096]{1,0:T(8,128)(2,1)} %t_hbm.3), channel_id=1, source_target_pairs={{0,16},{1,17},{2,18},{3,19},{4,20},{5,21},{6,22},{7,23},{8,24},{9,... | collective-permute-start | bytes 9437192 | tf_op jit(solution)/shard_map/ppermute | solution.py:49
  4.0 8.6 %collective-permute-start.2 = (bf16[384,1024]{1,0:T(8,128)(2,1)}, bf16[384,1024]{1,0:T(8,128)(2,1)S(1)}, u32[]{:S(2)}, u32[]{:S(2)}) collective-permute-start(bf16[384,1024]{1,0:T(8,128)(2,1)} %cot_ref.1), channel_id=1, source_target_pairs={{0,16},{1,17},{2,18},{3,19},{4,20},{5,21},{6,22},{7,23},{8,24},{9,... | collective-permute-start | bytes 2359304 | tf_op jit(solution)/shard_map/ppermute | solution.py:49
  4.1 1.0 copy-start.3
  5.2 7.4 %copy-start.8 = (s32[13]{0:T(128)}, s32[13]{0:T(128)S(1)}, u32[]{:S(2)}) copy-start(s32[13]{0:T(128)S(1)} %stack.168.s_ref) | copy-start | bytes 160
  5.8 5.1 %collective-permute-start = (bf16[640,128]{1,0:T(8,128)(2,1)S(1)}, bf16[640,128]{1,0:T(8,128)(2,1)S(1)}, u32[]{:S(2)}, u32[]{:S(2)}) collective-permute-start(bf16[640,128]{1,0:T(8,128)(2,1)S(1)} %shard_map.110), channel_id=1, source_target_pairs={{0,28},{1,21},{2,30},{3,23},{4,16},{5,25},{6,18},{7,27},{8,20},{9,... | collective-permute-start | bytes 491528 | tf_op jit(solution)/shard_map/ppermute | solution.py:49
  6.0 1.0 copy-start.4
  7.0 1.0 copy-start.7
  11.0 8.8 %collective-permute-start.3 = (bf16[2,640,128]{2,1,0:T(8,128)(2,1)S(1)}, bf16[2,640,128]{2,1,0:T(8,128)(2,1)S(1)}, u32[]{:S(2)}, u32[]{:S(2)}) collective-permute-start(bf16[2,640,128]{2,1,0:T(8,128)(2,1)S(1)} %pad_maximum_fusion.3), channel_id=1, source_target_pairs={{0,20},{1,29},{2,22},{3,31},{4,24},{5,17},{6,26},{7,19},{8,28},{9,... | collective-permute-start | bytes 983048 | tf_op jit(solution)/shard_map/ppermute | solution.py:49
  11.8 8.0 %collective-permute-start.4 = (bf16[384,256]{1,0:T(8,128)(2,1)S(1)}, bf16[384,256]{1,0:T(8,128)(2,1)S(1)}, u32[]{:S(2)}, u32[]{:S(2)}) collective-permute-start(bf16[384,256]{1,0:T(8,128)(2,1)S(1)} %shard_map.111), channel_id=1, source_target_pairs={{0,49},{1,48},{2,51},{3,50},{4,53},{5,52},{6,55},{7,54},{8,57},{9,... | collective-permute-start | bytes 589832 | tf_op jit(solution)/shard_map/ppermute | solution.py:49
  12.6 1.0 copy-start.1
  19.9 0.7 copy-start.18
  20.6 21.2 %collective-permute-start.5 = (bf16[2,4,4,128,128]{4,3,2,1,0:T(8,128)(2,1)}, bf16[2,4,4,128,128]{4,3,2,1,0:T(8,128)(2,1)S(1)}, u32[]{:S(2)}, u32[]{:S(2)}) collective-permute-start(bf16[2,4,4,128,128]{4,3,2,1,0:T(8,128)(2,1)} %get-tuple-element.70), channel_id=1, source_target_pairs={{0,20},{1,29},{2,22},{3,31},{4,24},{5,17},{6,26},{7,19},{8,28},{9,... | collective-permute-start | bytes 3145736 | tf_op jit(solution)/shard_map/ppermute | solution.py:49
  28.8 15.9 %collective-permute-start.6 = (bf16[2,4,4,128,128]{4,3,2,1,0:T(8,128)(2,1)}, bf16[2,4,4,128,128]{4,3,2,1,0:T(8,128)(2,1)S(1)}, u32[]{:S(2)}, u32[]{:S(2)}) collective-permute-start(bf16[2,4,4,128,128]{4,3,2,1,0:T(8,128)(2,1)} %get-tuple-element.71), channel_id=1, source_target_pairs={{0,80},{1,209},{2,82},{3,211},{4,212},{5,85},{6,214},{7,87},{8,88}... | collective-permute-start | bytes 3145736 | tf_op jit(solution)/shard_map/ppermute | solution.py:49
  29.8 18.7 %collective-permute-start.7 = (bf16[4,640,128]{2,1,0:T(8,128)(2,1)S(1)}, bf16[4,640,128]{2,1,0:T(8,128)(2,1)S(1)}, u32[]{:S(2)}, u32[]{:S(2)}) collective-permute-start(bf16[4,640,128]{2,1,0:T(8,128)(2,1)S(1)} %constant_dynamic-update-slice_fusion), channel_id=1, source_target_pairs={{0,17},{1,18},{2,19},{3,48},{4,55},{5,20},{6,21},{7,22},{8,25},{9,... | collective-permute-start | bytes 1966088 | tf_op jit(solution)/shard_map/ppermute | solution.py:49
  30.8 17.8 %collective-permute-start.8 = (bf16[4,640,128]{2,1,0:T(8,128)(2,1)S(1)}, bf16[4,640,128]{2,1,0:T(8,128)(2,1)S(1)}, u32[]{:S(2)}, u32[]{:S(2)}) collective-permute-start(bf16[4,640,128]{2,1,0:T(8,128)(2,1)S(1)} %constant_dynamic-update-slice_fusion), channel_id=1, source_target_pairs={{0,51},{1,16},{2,17},{3,18},{4,21},{5,22},{6,23},{7,52},{8,59},{9,... | collective-permute-start | bytes 1966088 | tf_op jit(solution)/shard_map/ppermute | solution.py:49
  31.7 8.4 %collective-permute-start.9 = (bf16[384,128]{1,0:T(8,128)(2,1)S(1)}, bf16[384,128]{1,0:T(8,128)(2,1)S(1)}, u32[]{:S(2)}, u32[]{:S(2)}) collective-permute-start(bf16[384,128]{1,0:T(8,128)(2,1)S(1)} %broadcast_select_fusion.1), channel_id=1, source_target_pairs={{0,16},{1,17},{2,18},{3,19},{4,20},{5,21},{6,22},{7,23},{8,24},{9,... | collective-permute-start | bytes 294920 | tf_op jit(solution)/shard_map/ppermute | solution.py:49
  41.8 6.8 %copy-start.13 = (bf16[2,4,4,128,128]{4,3,2,1,0:T(8,128)(2,1)}, bf16[2,4,4,128,128]{4,3,2,1,0:T(8,128)(2,1)S(1)}, u32[]{:S(2)}) copy-start(bf16[2,4,4,128,128]{4,3,2,1,0:T(8,128)(2,1)S(1)} %collective-permute-done.5) | copy-start | bytes 3145732
  44.7 1.0 copy-start.11
  48.5 15.4 %copy-start.10 = (f32[2,4,4,128,128]{4,3,2,1,0:T(8,128)S(1)}, f32[2,4,4,128,128]{4,3,2,1,0:T(8,128)}, u32[]{:S(2)}) copy-start(f32[2,4,4,128,128]{4,3,2,1,0:T(8,128)} %get-tuple-element.74) | copy-start | bytes 6291460
  48.5 0.8 copy-start.14
  48.6 1.0 copy-start.16
  49.6 9.1 %collective-permute-start.10 = (bf16[4,4,128,128]{3,2,1,0:T(8,128)(2,1)}, bf16[4,4,128,128]{3,2,1,0:T(8,128)(2,1)S(1)}, u32[]{:S(2)}, u32[]{:S(2)}) collective-permute-start(bf16[4,4,128,128]{3,2,1,0:T(8,128)(2,1)} %get-tuple-element.80), channel_id=1, source_target_pairs={{0,28},{1,21},{2,30},{3,23},{4,16},{5,25},{6,18},{7,27},{8,20},{9,... | collective-permute-start | bytes 1572872 | tf_op jit(solution)/shard_map/ppermute | solution.py:49
  49.6 5.3 %collective-permute-start.12 = (bf16[384,128]{1,0:T(8,128)(2,1)S(1)}, bf16[384,128]{1,0:T(8,128)(2,1)S(1)}, u32[]{:S(2)}, u32[]{:S(2)}) collective-permute-start(bf16[384,128]{1,0:T(8,128)(2,1)S(1)} %select_select_fusion.1), channel_id=1, source_target_pairs={{0,80},{1,81},{2,82},{3,83},{4,84},{5,85},{6,86},{7,87},{8,88},{9,... | collective-permute-start | bytes 294920 | tf_op jit(solution)/shard_map/ppermute | solution.py:49
  51.0 6.3 %collective-permute-start.13 = (bf16[384,128]{1,0:T(8,128)(2,1)S(1)}, bf16[384,128]{1,0:T(8,128)(2,1)}, u32[]{:S(2)}, u32[]{:S(2)}) collective-permute-start(bf16[384,128]{1,0:T(8,128)(2,1)S(1)} %select_select_fusion.1), channel_id=1, source_target_pairs={{0,208},{1,209},{2,210},{3,211},{4,212},{5,213},{6,214},{7,215},{8... | collective-permute-start | bytes 294920 | tf_op jit(solution)/shard_map/ppermute | solution.py:49
  53.0 4.3 %collective-permute-start.14 = (bf16[384,128]{1,0:T(8,128)(2,1)S(1)}, bf16[384,128]{1,0:T(8,128)(2,1)}, u32[]{:S(2)}, u32[]{:S(2)}) collective-permute-start(bf16[384,128]{1,0:T(8,128)(2,1)S(1)} %select_select_fusion.1), channel_id=1, source_target_pairs={{0,128},{1,129},{2,130},{3,131},{4,132},{5,133},{6,134},{7,135},{8... | collective-permute-start | bytes 294920 | tf_op jit(solution)/shard_map/ppermute | solution.py:49
  54.9 9.1 %copy-start.12 = (bf16[2,4,4,128,128]{4,3,2,1,0:T(8,128)(2,1)S(1)}, bf16[2,4,4,128,128]{4,3,2,1,0:T(8,128)(2,1)}, u32[]{:S(2)}) copy-start(bf16[2,4,4,128,128]{4,3,2,1,0:T(8,128)(2,1)} %copy-done.11) | copy-start | bytes 3145732
  54.9 9.1 %collective-permute-start.11 = (bf16[4,4,128,128]{3,2,1,0:T(8,128)(2,1)}, bf16[4,4,128,128]{3,2,1,0:T(8,128)(2,1)S(1)}, u32[]{:S(2)}, u32[]{:S(2)}) collective-permute-start(bf16[4,4,128,128]{3,2,1,0:T(8,128)(2,1)} %get-tuple-element.81), channel_id=1, source_target_pairs={{0,208},{1,81},{2,210},{3,83},{4,84},{5,213},{6,86},{7,215},{8,216... | collective-permute-start | bytes 1572872 | tf_op jit(solution)/shard_map/ppermute | solution.py:49
  54.9 12.0 %collective-permute-start.15 = (bf16[4,640,128]{2,1,0:T(8,128)(2,1)}, bf16[4,640,128]{2,1,0:T(8,128)(2,1)S(1)}, u32[]{:S(2)}, u32[]{:S(2)}) collective-permute-start(bf16[4,640,128]{2,1,0:T(8,128)(2,1)} %copy-done.16), channel_id=1, source_target_pairs={{0,17},{1,18},{2,19},{3,48},{4,55},{5,20},{6,21},{7,22},{8,25},{9,... | collective-permute-start | bytes 1966088 | tf_op jit(solution)/shard_map/ppermute | solution.py:49
  66.9 7.1 %collective-permute-start.16 = (bf16[2,4,128,128]{3,2,1,0:T(8,128)(2,1)S(1)}, bf16[2,4,128,128]{3,2,1,0:T(8,128)(2,1)S(1)}, u32[]{:S(2)}, u32[]{:S(2)}) collective-permute-start(bf16[2,4,128,128]{3,2,1,0:T(8,128)(2,1)S(1)} %slice.155), channel_id=1, source_target_pairs={{0,80},{1,209},{2,82},{3,211},{4,212},{5,85},{6,214},{7,87},{8,88}... | collective-permute-start | bytes 786440 | tf_op jit(solution)/shard_map/ppermute | solution.py:49
  67.1 7.1 %collective-permute-start.17 = (bf16[2,4,128,128]{3,2,1,0:T(8,128)(2,1)S(1)}, bf16[2,4,128,128]{3,2,1,0:T(8,128)(2,1)S(1)}, u32[]{:S(2)}, u32[]{:S(2)}) collective-permute-start(bf16[2,4,128,128]{3,2,1,0:T(8,128)(2,1)S(1)} %slice.154), channel_id=1, source_target_pairs={{0,20},{1,29},{2,22},{3,31},{4,24},{5,17},{6,26},{7,19},{8,28},{9,... | collective-permute-start | bytes 786440 | tf_op jit(solution)/shard_map/ppermute | solution.py:49
  69.0 5.2 %collective-permute-start.18 = (bf16[384,128]{1,0:T(8,128)(2,1)S(1)}, bf16[384,128]{1,0:T(8,128)(2,1)S(1)}, u32[]{:S(2)}, u32[]{:S(2)}) collective-permute-start(bf16[384,128]{1,0:T(8,128)(2,1)S(1)} %select_select_fusion), channel_id=1, source_target_pairs={{0,17},{1,16},{2,19},{3,18},{4,21},{5,20},{6,23},{7,22},{8,25},{9,... | collective-permute-start | bytes 294920 | tf_op jit(solution)/shard_map/ppermute | solution.py:49
  74.2 4.5 %collective-permute-start.20 = (bf16[4,128,128]{2,1,0:T(8,128)(2,1)S(1)}, bf16[4,128,128]{2,1,0:T(8,128)(2,1)S(1)}, u32[]{:S(2)}, u32[]{:S(2)}) collective-permute-start(bf16[4,128,128]{2,1,0:T(8,128)(2,1)S(1)} %fusion.5), channel_id=1, source_target_pairs={{0,28},{1,21},{2,30},{3,23},{4,16},{5,25},{6,18},{7,27},{8,20},{9,... | collective-permute-start | bytes 393224 | tf_op jit(solution)/shard_map/ppermute | solution.py:49
  75.5 4.7 %collective-permute-start.19 = (bf16[4,128,128]{2,1,0:T(8,128)(2,1)S(1)}, bf16[4,128,128]{2,1,0:T(8,128)(2,1)S(1)}, u32[]{:S(2)}, u32[]{:S(2)}) collective-permute-start(bf16[4,128,128]{2,1,0:T(8,128)(2,1)S(1)} %fusion.4), channel_id=1, source_target_pairs={{0,208},{1,81},{2,210},{3,83},{4,84},{5,213},{6,86},{7,215},{8,216... | collective-permute-start | bytes 393224 | tf_op jit(solution)/shard_map/ppermute | solution.py:49
  76.8 9.7 %copy-start.15 = (bf16[4,640,128]{2,1,0:T(8,128)(2,1)S(1)}, bf16[4,640,128]{2,1,0:T(8,128)(2,1)}, u32[]{:S(2)}) copy-start(bf16[4,640,128]{2,1,0:T(8,128)(2,1)} %copy-done.14) | copy-start | bytes 1966084
  76.8 9.7 %copy-start.17 = (bf16[4,640,128]{2,1,0:T(8,128)(2,1)S(1)}, bf16[4,640,128]{2,1,0:T(8,128)(2,1)}, u32[]{:S(2)}) copy-start(bf16[4,640,128]{2,1,0:T(8,128)(2,1)} %copy-done.16) | copy-start | bytes 1966084
  76.8 8.5 %collective-permute-start.21 = (bf16[2,384,128]{2,1,0:T(8,128)(2,1)S(1)}, bf16[2,384,128]{2,1,0:T(8,128)(2,1)S(1)}, u32[]{:S(2)}, u32[]{:S(2)}) collective-permute-start(bf16[2,384,128]{2,1,0:T(8,128)(2,1)S(1)} %pad_maximum_fusion.5), channel_id=1, source_target_pairs={{0,51},{1,18},{2,17},{3,48},{4,55},{5,22},{6,21},{7,52},{8,59},{9,... | collective-permute-start | bytes 589832 | tf_op jit(solution)/shard_map/ppermute | solution.py:49
  80.3 12.5 %copy-start.9 = (f32[4,2,128,128]{3,2,1,0:T(8,128)}, f32[4,2,128,128]{3,2,1,0:T(8,128)S(1)}, u32[]{:S(2)}) copy-start(f32[4,2,128,128]{3,2,1,0:T(8,128)S(1)} %pad_maximum_fusion.2) | copy-start | bytes 1572868
  85.4 7.4 %collective-permute-start.22 = (f32[2,2,128,128]{3,2,1,0:T(8,128)S(1)}, f32[2,2,128,128]{3,2,1,0:T(8,128)S(1)}, u32[]{:S(2)}, u32[]{:S(2)}) collective-permute-start(f32[2,2,128,128]{3,2,1,0:T(8,128)S(1)} %slice.98), channel_id=1, source_target_pairs={{0,17},{1,18},{2,19},{3,48},{4,55},{5,20},{6,21},{7,22},{8,25},{9,... | collective-permute-start | bytes 786440 | tf_op jit(solution)/shard_map/ppermute | solution.py:49
  85.6 7.6 %collective-permute-start.23 = (bf16[4,384,128]{2,1,0:T(8,128)(2,1)S(1)}, bf16[4,384,128]{2,1,0:T(8,128)(2,1)S(1)}, u32[]{:S(2)}, u32[]{:S(2)}) collective-permute-start(bf16[4,384,128]{2,1,0:T(8,128)(2,1)S(1)} %constant_dynamic-update-slice_fusion.2), channel_id=1, source_target_pairs={{0,28},{1,21},{2,30},{3,23},{4,16},{5,25},{6,18},{7,27},{8,20},{9,... | collective-permute-start | bytes 1179656 | tf_op jit(solution)/shard_map/ppermute | solution.py:49
  92.8 1.3 %copy-start.19 = (f32[2,2,128,128]{3,2,1,0:T(8,128)}, f32[2,2,128,128]{3,2,1,0:T(8,128)S(1)}, u32[]{:S(2)}) copy-start(f32[2,2,128,128]{3,2,1,0:T(8,128)S(1)} %collective-permute-done.22) | copy-start | bytes 786436
  94.1 14.2 %copy-start.2 = (bf16[384,1024]{1,0:T(8,128)(2,1)S(1)}, bf16[384,1024]{1,0:T(8,128)(2,1)}, u32[]{:S(2)}) copy-start(bf16[384,1024]{1,0:T(8,128)(2,1)} %copy-done.1) | copy-start | bytes 2359300
  94.1 12.9 %collective-permute-start.26 = (bf16[2,4,384,128]{3,2,1,0:T(8,128)(2,1)}, bf16[2,4,384,128]{3,2,1,0:T(8,128)(2,1)}, u32[]{:S(2)}, u32[]{:S(2)}) collective-permute-start(bf16[2,4,384,128]{3,2,1,0:T(8,128)(2,1)} %pad_maximum_fusion.1), channel_id=1, source_target_pairs={{0,20},{1,29},{2,22},{3,31},{4,24},{5,17},{6,26},{7,19},{8,28},{9,... | collective-permute-start | bytes 2359304 | tf_op jit(solution)/shard_map/ppermute | solution.py:49
  96.1 4.8 %collective-permute-start.24 = (f32[2,128,128]{2,1,0:T(8,128)S(1)}, f32[2,128,128]{2,1,0:T(8,128)}, u32[]{:S(2)}, u32[]{:S(2)}) collective-permute-start(f32[2,128,128]{2,1,0:T(8,128)S(1)} %fusion.6), channel_id=1, source_target_pairs={{0,51},{1,16},{2,17},{3,18},{4,21},{5,22},{6,23},{7,52},{8,59},{9,... | collective-permute-start | bytes 393224 | tf_op jit(solution)/shard_map/ppermute | solution.py:49
  101.9 9.1 %collective-permute-start.25 = (bf16[2,128,128]{2,1,0:T(8,128)(2,1)S(1)}, bf16[2,128,128]{2,1,0:T(8,128)(2,1)S(1)}, u32[]{:S(2)}, u32[]{:S(2)}) collective-permute-start(bf16[2,128,128]{2,1,0:T(8,128)(2,1)S(1)} %fusion.9), channel_id=1, source_target_pairs={{0,32},{1,33},{2,34},{3,35},{4,36},{5,37},{6,38},{7,39},{8,40},{9,... | collective-permute-start | bytes 196616 | tf_op jit(solution)/shard_map/ppermute | solution.py:49
  108.3 9.1 %copy-start = (bf16[384,1024]{1,0:T(8,128)(2,1)S(1)}, bf16[384,1024]{1,0:T(8,128)(2,1)}, u32[]{:S(2)}) copy-start(bf16[384,1024]{1,0:T(8,128)(2,1)} %cot_ref.1) | copy-start | bytes 2359300
  111.1 6.3 %collective-permute-start.29 = (bf16[384,2048]{1,0:T(8,128)(2,1)S(1)}, bf16[384,2048]{1,0:T(8,128)(2,1)S(1)}, u32[]{:S(2)}, u32[]{:S(2)}) collective-permute-start(bf16[384,2048]{1,0:T(8,128)(2,1)S(1)} %shard_map.114), channel_id=1, source_target_pairs={{0,16},{1,17},{2,18},{3,19},{4,20},{5,21},{6,22},{7,23},{8,24},{9,... | collective-permute-start | bytes 4718600 | tf_op jit(solution)/shard_map/ppermute | solution.py:49
  111.9 4.8 %collective-permute-start.27 = (f32[2,128,128]{2,1,0:T(8,128)S(1)}, f32[2,128,128]{2,1,0:T(8,128)S(1)}, u32[]{:S(2)}, u32[]{:S(2)}) collective-permute-start(f32[2,128,128]{2,1,0:T(8,128)S(1)} %get-tuple-element.114), channel_id=1, source_target_pairs={{0,208},{1,81},{2,210},{3,83},{4,84},{5,213},{6,86},{7,215},{8,216... | collective-permute-start | bytes 393224 | tf_op jit(solution)/shard_map/ppermute | solution.py:49
  116.7 9.2 %copy-start.5 = (f32[256,640]{1,0:T(8,128)S(1)}, f32[256,640]{1,0:T(8,128)}, u32[]{:S(2)}) copy-start(f32[256,640]{1,0:T(8,128)} %m_ref.1) | copy-start | bytes 1966084
  116.7 7.1 %collective-permute-start.28 = (f32[2,2,128,128]{3,2,1,0:T(8,128)S(1)}, f32[2,2,128,128]{3,2,1,0:T(8,128)S(1)}, u32[]{:S(2)}, u32[]{:S(2)}) collective-permute-start(f32[2,2,128,128]{3,2,1,0:T(8,128)S(1)} %pad_maximum_fusion.4), channel_id=1, source_target_pairs={{0,80},{1,209},{2,82},{3,211},{4,212},{5,85},{6,214},{7,87},{8,88}... | collective-permute-start | bytes 786440 | tf_op jit(solution)/shard_map/ppermute | solution.py:49
  123.8 2.0 %collective-permute-start.30 = (f32[4,2,128,128]{3,2,1,0:T(8,128)S(1)}, f32[4,2,128,128]{3,2,1,0:T(8,128)S(1)}, u32[]{:S(2)}, u32[]{:S(2)}) collective-permute-start(f32[4,2,128,128]{3,2,1,0:T(8,128)S(1)} %constant_dynamic-update-slice_fusion.6.mine_ref), channel_id=1, source_target_pairs={{0,16},{1,17},{2,18},{3,19},{4,20},{5,21},{6,22},{7,23},{8,24},{9,... | collective-permute-start | bytes 1572872 | tf_op jit(solution)/shard_map/ppermute | solution.py:49
  125.8 1.1 copy-start.6

commit v4 on v3

--- a/solution.py
+++ b/solution.py
@@ -271,10 +271,6 @@
     )(where, mine, other, moment, second)
 
 
-def has_host(c):
-    return c["c"] == c["x"] + c["zl"] + c["zh"] & 1
-
-
 def on_device(tokens, cotangent, weight, moment, second, delayed):
     me = where_am_i()
     device_cols = moment.shape[1]
@@ -291,18 +287,24 @@
     their_tokens = send(tokens, flip("c"))
     kept = rows_call(kept_kernel, (640, 128), order, weight)
     refreshed = rows_call(refreshed_kernel, (384, 256), weight, delayed)
-    for_zh = send(
-        refreshed,
-        lambda c: dict(c, zh=1, zl=c["zl"] ^ 1) if c["y"] == c["zh"] == 0 and has_host(c) else None,
+    lower, upper = refreshed[:, :128], refreshed[:, 128:]
+    host_got = send(
+        jnp.where(core == 0, upper, lower),
+        lambda c: dict(c, c=1 - c["c"]) if c["y"] == c["zh"] == 0 else None,
     )
     kept_got = send(kept, partner("x", False))
-    order, kept, kept_got, refreshed = together(order, kept, kept_got, refreshed)
+    order, kept, kept_got, lower, host_got = together(order, kept, kept_got, lower, host_got)
+    on_root = core == (me["x"] + me["zl"]) % 2
+    host = jnp.where(on_root, jnp.where(core == 0, lower, upper), host_got)
+    host_got = send(
+        host, lambda c: dict(c, zh=1, zl=c["zl"] ^ 1) if c["y"] == c["zh"] == 0 else None
+    )
     kept = jnp.stack([kept, kept_got])
     kept_got = send(kept, partner("x", True))
     order, kept = together(order, kept)
     one_out, two_out = chip_gradient(False, order, tokens, their_tokens, cotangent, their_cot)
-    one_out, two_out, order, kept, kept_got, refreshed, for_zh = together(
-        one_out, two_out, order, kept, kept_got, refreshed, for_zh
+    one_out, two_out, order, kept, kept_got, host, host_got = together(
+        one_out, two_out, order, kept, kept_got, host, host_got
     )
 
     one_got = send(one_out, partner("x", True))
@@ -310,29 +312,24 @@
     kept = jnp.concatenate([kept, kept_got])
     kept_a = send(kept, partner("zl", True))
     kept_b = send(kept, partner("zl", False))
-    refreshed = jnp.where(zh == 0, refreshed, for_zh)
-    first = core == (me["x"] + me["zl"] + zh) % 2
-    lower, upper = refreshed[:, :128], refreshed[:, 128:]
-    for_core = send(
-        jnp.where(core == 0, upper, lower),
-        lambda c: dict(c, c=1 - c["c"]) if c["y"] == 0 and has_host(c) else None,
-    )
+    host = jnp.where(zh == 0, host, host_got)
+    host_got = send(host, partner("y", True))
     one_held, two_held = chip_gradient(True, order, tokens, their_tokens, cotangent, their_cot)
     one_held, two_held, one_got, two_got = together(one_held, two_held, one_got, two_got)
     one_far = (one_held[0] + one_got[0].astype(F32)).astype(BF16)
     two_far = (two_held[0] + two_got[0].astype(F32)).astype(BF16)
-    host = jnp.where(first, jnp.where(core == 0, lower, upper), for_core)
+    host = jnp.where(y == jnp.where(core == 0, 1, 3), host_got, host)
     one_far, two_far, kept, kept_a, kept_b, host = together(
         one_far, two_far, kept, kept_a, kept_b, host
     )
 
     one_got2 = send(one_far, partner("x", False))
     two_got2 = send(two_far, partner("y", False))
-    by_y = [send(host, lambda c, k=k: dict(c, y=k) if c["y"] == 0 else None) for k in (1, 3, 2)]
+    host_got = send(host, partner("y", False))
     kept_c = send(kept_b, partner("zl", True))
     one = one_held[1] + one_got[1].astype(F32) + one_got2.astype(F32)
     two = two_held[1] + two_got[1].astype(F32) + two_got2.astype(F32)
-    host = jnp.where(y == 0, host, jnp.where(y == 1, by_y[0], jnp.where(y == 3, by_y[1], by_y[2])))
+    host = jnp.where((y == 2) | (y == jnp.where(core == 0, 3, 1)), host_got, host)
     one, two, host, kept_c = together(one, two, host, kept_c)
 
     one_got = send(one[:2].astype(BF16), partner("y", True))
@@ -346,6 +343,7 @@
     two_got2 = send(two_far, partner("x", False))
     host = jnp.stack([host, host_got])
     host_got = send(host, neighbour("zl", 3))
+    one_got2, two_got2, host_got = together(one_got2, two_got2, host_got)
     both = jnp.stack(
         [
             one[3] + one_got[1].astype(F32) + one_got2.astype(F32),
@@ -359,8 +357,8 @@
     host = jnp.concatenate([host, host_got])
     host_got = send(host, partner("x", False))
     kept = jnp.stack([kept, kept_b, kept_a, kept_c])
+    got, host, host_got, kept = together(got, host, host_got, kept)
     far = both[2] + got[0]
-    far, host, host_got, kept = together(far, host, host_got, kept)
     got2 = send(far, partner("zl", False))
     host = jnp.stack([host, host_got])
     host_got = send(host, partner("x", True))

time: 130 us -> 125 us (0.962)
  starting transfers between devices: 38.3 us -> 32.2 us
    ppermute x31 -> x30, starting transfers between devices: 38.3 us -> 32.2 us  [send(): return lax.ppermute(value, AXES, pairs)]
    ppermute x31 -> x30, waiting for transfers between devices: 44.8 us -> 46 us  [send(): return lax.ppermute(value, AXES, pairs)]
  transfers between devices with their start and end apart: 31 -> 30, of which waited for: 18 -> 15; matrix products, arithmetic and copies ran while one was open for 9% -> 9% of each run, Pallas kernels for 17% -> 18%
where the time goes in v4:
time: 125 us
  waiting for transfers between devices  46 us (37%)
  starting transfers between devices  32.2 us (26%)
  Pallas kernels  24.3 us (19%)
  local copies, waits for them, and re-layouts  13.4 us (11%)
  other arithmetic  7.8 us (6%)
    ppermute x30, waiting for transfers between devices, send(): return lax.ppermute(value, AXES, pairs)  46 us
    ppermute x30, starting transfers between devices, send(): return lax.ppermute(value, AXES, pairs)  32.2 us
    pallas_call x2, Pallas kernels, chip_gradient(): pl.pallas_call(functools.partial(grad_kernel, keep), out_shape=(jax.Shape...  13.4 us
    unnamed x44, local copies, waits for them, and re-layouts  10.1 us
    pallas_call x1, Pallas kernels, our_input_gradient(): pl.pallas_call(ours_kernel, out_shape=jax.ShapeDtypeStruct((384, 4096), B...  5.13 us
    convert_element_type x1, other arithmetic, on_device(): one_far = (one_held[0] + one_got[0].astype(F32)).astype(BF16)  2.79 us
    pallas_call x1, Pallas kernels, their_input_gradient(): pl.pallas_call(theirs_kernel, out_shape=jax.ShapeDtypeStruct((384, 2048),...  2.74 us
  transfers between devices with their start and end apart: 30, of which 15 were waited for; matrix products, arithmetic and copies ran while one was open for 9% of the time, Pallas kernels for 18%

profile of v4, /device:TPU:1, one launch (start us, length us, event | category | flops | bytes accessed | tf_op | source)
XLA Modules:
  0.0 124.8 jit_solution(5914186910278137870)
XLA Ops:
  0.6 3.3 %collective-permute-start.2 = (bf16[384,4096]{1,0:T(8,128)(2,1)}, bf16[384,4096]{1,0:T(8,128)(2,1)}, u32[]{:S(2)}, u32[]{:S(2)}) collective-permute-start(bf16[384,4096]{1,0:T(8,128)(2,1)} %t_hbm.3), channel_id=1, source_target_pairs={{0,16},{1,17},{2,18},{3,19},{4,20},{5,21},{6,22},{7,23},{8,24},{9,... | collective-permute-start | bytes 9437192 | tf_op jit(solution)/shard_map/ppermute | solution.py:49
  4.0 0.1 collective-permute-start.3
  4.2 1.0 copy-done.3
  5.2 0.6 shard_map.110
  5.8 0.1 collective-permute-start
  6.0 1.0 copy-done.4
  7.0 1.0 copy-done.7
  8.0 0.1 shard_map.111
  8.1 3.0 %collective-permute-start.1 = (bf16[384,128]{1,0:T(8,128)(2,1)S(1)}, bf16[384,128]{1,0:T(8,128)(2,1)S(1)}, u32[]{:S(2)}, u32[]{:S(2)}) collective-permute-start(bf16[384,128]{1,0:T(8,128)(2,1)S(1)} %get-tuple-element.121), channel_id=1, source_target_pairs={{0,16},{1,17},{2,18},{3,19},{4,20},{5,21},{6,22},{7,23},{8,24},{9,... | collective-permute-start | bytes 294920 | tf_op jit(solution)/shard_map/ppermute | solution.py:49
  11.2 0.9 collective-permute-done.1
  12.1 2.3 %collective-permute-start.4 = (bf16[2,640,128]{2,1,0:T(8,128)(2,1)S(1)}, bf16[2,640,128]{2,1,0:T(8,128)(2,1)S(1)}, u32[]{:S(2)}, u32[]{:S(2)}) collective-permute-start(bf16[2,640,128]{2,1,0:T(8,128)(2,1)S(1)} %pad_maximum_fusion.3), channel_id=1, source_target_pairs={{0,20},{1,29},{2,22},{3,31},{4,24},{5,17},{6,26},{7,19},{8,28},{9,... | collective-permute-start | bytes 983048 | tf_op jit(solution)/shard_map/ppermute | solution.py:49
  14.5 6.1 %collective-permute-start.5 = (bf16[384,128]{1,0:T(8,128)(2,1)S(1)}, bf16[384,128]{1,0:T(8,128)(2,1)S(1)}, u32[]{:S(2)}, u32[]{:S(2)}) collective-permute-start(bf16[384,128]{1,0:T(8,128)(2,1)S(1)} %select_select_fusion), channel_id=1, source_target_pairs={{0,49},{1,48},{2,51},{3,50},{4,53},{5,52},{6,55},{7,54},{8,57},{9,... | collective-permute-start | bytes 294920 | tf_op jit(solution)/shard_map/ppermute | solution.py:49
  20.6 0.9 copy-done.1
  21.5 6.3 %shard_map.112 = (bf16[2,4,4,128,128]{4,3,2,1,0:T(8,128)(2,1)}, bf16[2,4,4,128,128]{4,3,2,1,0:T(8,128)(2,1)}) custom-call(s32[13]{0:T(128)} %copy-done.8, bf16[384,4096]{1,0:T(8,128)(2,1)} %t_hbm.3, bf16[384,4096]{1,0:T(8,128)(2,1)} %collective-permute-done.2.u_hbm, bf16[384,1024]{1,0:T(8,128)(2,1)} %cot_ref.1, bf16[384,1024]{1,0:T(8,128)(2,1)} %copy-done.1), custom_call_target="tpu_custom_call" | custom-call | flops 1610612736 | bytes 9437184 | tf_op jit(solution)/shard_map/pallas_call | solution.py:144
  27.8 0.7 copy-done.18
  28.6 0.2 collective-permute-start.6
  28.8 1.0 constant_dynamic-update-slice_fusion
  29.8 1.0 collective-permute-start.8
  30.8 0.9 collective-permute-start.9
  31.7 3.0 %collective-permute-start.10 = (bf16[384,128]{1,0:T(8,128)(2,1)S(1)}, bf16[384,128]{1,0:T(8,128)(2,1)S(1)}, u32[]{:S(2)}, u32[]{:S(2)}) collective-permute-start(bf16[384,128]{1,0:T(8,128)(2,1)S(1)} %broadcast_select_fusion.1), channel_id=1, source_target_pairs={{0,80},{1,209},{2,82},{3,211},{4,212},{5,85},{6,214},{7,87},{8,88}... | collective-permute-start | bytes 294920 | tf_op jit(solution)/shard_map/ppermute | solution.py:49
  34.7 7.1 %shard_map.113 = (f32[2,4,4,128,128]{4,3,2,1,0:T(8,128)}, f32[2,4,4,128,128]{4,3,2,1,0:T(8,128)}) custom-call(s32[13]{0:T(128)} %copy-done.8, bf16[384,4096]{1,0:T(8,128)(2,1)} %t_hbm.3, bf16[384,4096]{1,0:T(8,128)(2,1)} %collective-permute-done.2.u_hbm, bf16[384,1024]{1,0:T(8,128)(2,1)} %cot_ref.1, bf16[384,1024]{1,0:T(8,128)(2,1)} %copy-done.1), custom_call_target="tpu_custom_call" | custom-call | flops 1610612736 | bytes 9437184 | tf_op jit(solution)/shard_map/pallas_call | solution.py:144
  41.8 3.9 %collective-permute-done.10 = bf16[384,128]{1,0:T(8,128)(2,1)S(1)} collective-permute-done((bf16[384,128]{1,0:T(8,128)(2,1)S(1)}, bf16[384,128]{1,0:T(8,128)(2,1)S(1)}, u32[]{:S(2)}, u32[]{:S(2)}) %collective-permute-start.10) | collective-permute-done | bytes 98336 | tf_op jit(solution)/shard_map/ppermute | solution.py:49
  45.8 0.9 copy-done.13
  46.7 0.4 copy-done.11
  47.1 2.8 %fusion = (bf16[4,4,128,128]{3,2,1,0:T(8,128)(2,1)}, bf16[4,4,128,128]{3,2,1,0:T(8,128)(2,1)}) fusion(f32[2,4,4,128,128]{4,3,2,1,0:T(8,128)} %get-tuple-element.77, bf16[2,4,4,128,128]{4,3,2,1,0:T(8,128)(2,1)S(1)} %collective-permute-done.6, bf16[2,4,4,128,128]{4,3,2,1,0:T(8,128)(2,1)S(1)} %collective-permute-done.7, f32[2,4,4,128,128]{4,3,2,1,0:T(8,128)} %get-tuple-element.79), kind=kLoop, calls=%fused_computation.6 | loop fusion | flops 1572864 | bytes 4194304 | tf_op jit(solution)/shard_map/convert_element_type | solution.py:319
  49.9 0.8 copy-done.14
  50.7 0.8 copy-done.16
  51.6 1.7 %collective-permute-start.12 = (bf16[4,4,128,128]{3,2,1,0:T(8,128)(2,1)}, bf16[4,4,128,128]{3,2,1,0:T(8,128)(2,1)S(1)}, u32[]{:S(2)}, u32[]{:S(2)}) collective-permute-start(bf16[4,4,128,128]{3,2,1,0:T(8,128)(2,1)} %get-tuple-element.86), channel_id=1, source_target_pairs={{0,208},{1,81},{2,210},{3,83},{4,84},{5,213},{6,86},{7,215},{8,216... | collective-permute-start | bytes 1572872 | tf_op jit(solution)/shard_map/ppermute | solution.py:49
  53.3 2.6 %collective-permute-done.13 = bf16[384,128]{1,0:T(8,128)(2,1)S(1)} collective-permute-done((bf16[384,128]{1,0:T(8,128)(2,1)S(1)}, bf16[384,128]{1,0:T(8,128)(2,1)S(1)}, u32[]{:S(2)}, u32[]{:S(2)}) %collective-permute-start.13) | collective-permute-done | bytes 98336 | tf_op jit(solution)/shard_map/ppermute | solution.py:49
  55.9 4.8 %collective-permute-done.11 = bf16[4,4,128,128]{3,2,1,0:T(8,128)(2,1)S(1)} collective-permute-done((bf16[4,4,128,128]{3,2,1,0:T(8,128)(2,1)}, bf16[4,4,128,128]{3,2,1,0:T(8,128)(2,1)S(1)}, u32[]{:S(2)}, u32[]{:S(2)}) %collective-permute-start.11) | collective-permute-done | bytes 524320 | tf_op jit(solution)/shard_map/ppermute | solution.py:49
  60.7 1.5 %bitcast_add_fusion.1 = f32[4,4,128,128]{3,2,1,0:T(8,128)S(1)} fusion(bf16[4,4,128,128]{3,2,1,0:T(8,128)(2,1)S(1)} %collective-permute-done.11, f32[2,4,4,128,128]{4,3,2,1,0:T(8,128)} %get-tuple-element.77, bf16[2,4,4,128,128]{4,3,2,1,0:T(8,128)(2,1)} %copy-done.13), kind=kLoop, calls=%fused_computation.2 | loop fusion | flops 1048576 | bytes 3145728 | tf_op jit(solution)/shard_map/add | solution.py:330
  62.3 0.2 bitcast_add_fusion
  62.4 2.3 %collective-permute-done.14 = bf16[4,640,128]{2,1,0:T(8,128)(2,1)S(1)} collective-permute-done((bf16[4,640,128]{2,1,0:T(8,128)(2,1)}, bf16[4,640,128]{2,1,0:T(8,128)(2,1)S(1)}, u32[]{:S(2)}, u32[]{:S(2)}) %collective-permute-start.14) | collective-permute-done | bytes 655392 | tf_op jit(solution)/shard_map/ppermute | solution.py:49
  65.0 2.6 %collective-permute-start.16 = (bf16[2,4,128,128]{3,2,1,0:T(8,128)(2,1)S(1)}, bf16[2,4,128,128]{3,2,1,0:T(8,128)(2,1)S(1)}, u32[]{:S(2)}, u32[]{:S(2)}) collective-permute-start(bf16[2,4,128,128]{3,2,1,0:T(8,128)(2,1)S(1)} %slice.143), channel_id=1, source_target_pairs={{0,20},{1,29},{2,22},{3,31},{4,24},{5,17},{6,26},{7,19},{8,28},{9,... | collective-permute-start | bytes 786440 | tf_op jit(solution)/shard_map/ppermute | solution.py:49
  67.5 4.4 %collective-permute-done.15 = bf16[2,4,128,128]{3,2,1,0:T(8,128)(2,1)S(1)} collective-permute-done((bf16[2,4,128,128]{3,2,1,0:T(8,128)(2,1)S(1)}, bf16[2,4,128,128]{3,2,1,0:T(8,128)(2,1)S(1)}, u32[]{:S(2)}, u32[]{:S(2)}) %collective-permute-start.15) | collective-permute-done | bytes 262176 | tf_op jit(solution)/shard_map/ppermute | solution.py:49
  71.9 0.1 collective-permute-done.16
  72.2 1.0 collective-permute-start.20
  73.1 1.0 collective-permute-start.19
  74.1 3.7 %collective-permute-done.18 = bf16[4,128,128]{2,1,0:T(8,128)(2,1)S(1)} collective-permute-done((bf16[4,128,128]{2,1,0:T(8,128)(2,1)S(1)}, bf16[4,128,128]{2,1,0:T(8,128)(2,1)S(1)}, u32[]{:S(2)}, u32[]{:S(2)}) %collective-permute-start.18) | collective-permute-done | bytes 131104 | tf_op jit(solution)/shard_map/ppermute | solution.py:49
  77.8 2.7 %collective-permute-done.20 = bf16[2,384,128]{2,1,0:T(8,128)(2,1)S(1)} collective-permute-done((bf16[2,384,128]{2,1,0:T(8,128)(2,1)S(1)}, bf16[2,384,128]{2,1,0:T(8,128)(2,1)S(1)}, u32[]{:S(2)}, u32[]{:S(2)}) %collective-permute-start.20) | collective-permute-done | bytes 196640 | tf_op jit(solution)/shard_map/ppermute | solution.py:49
  80.7 1.7 %collective-permute-start.22 = (bf16[4,384,128]{2,1,0:T(8,128)(2,1)S(1)}, bf16[4,384,128]{2,1,0:T(8,128)(2,1)S(1)}, u32[]{:S(2)}, u32[]{:S(2)}) collective-permute-start(bf16[4,384,128]{2,1,0:T(8,128)(2,1)S(1)} %constant_dynamic-update-slice_fusion.2), channel_id=1, source_target_pairs={{0,28},{1,21},{2,30},{3,23},{4,16},{5,25},{6,18},{7,27},{8,20},{9,... | collective-permute-start | bytes 1179656 | tf_op jit(solution)/shard_map/ppermute | solution.py:49
  82.4 0.1 collective-permute-start.21
  82.5 0.3 pad_maximum_fusion.w_ref
  82.9 6.6 %collective-permute-done.21 = f32[2,2,128,128]{3,2,1,0:T(8,128)S(1)} collective-permute-done((f32[2,2,128,128]{3,2,1,0:T(8,128)S(1)}, f32[2,2,128,128]{3,2,1,0:T(8,128)S(1)}, u32[]{:S(2)}, u32[]{:S(2)}) %collective-permute-start.21) | collective-permute-done | bytes 262176 | tf_op jit(solution)/shard_map/ppermute | solution.py:49
  89.5 1.0 pad_maximum_fusion.1
  90.5 0.6 collective-permute-start.25
  91.1 0.7 add_bitcast_fusion
  91.7 0.7 dynamic-slice_bitcast_fusion
  92.5 4.2 %collective-permute-done.23 = f32[2,128,128]{2,1,0:T(8,128)S(1)} collective-permute-done((f32[2,128,128]{2,1,0:T(8,128)}, f32[2,128,128]{2,1,0:T(8,128)S(1)}, u32[]{:S(2)}, u32[]{:S(2)}) %collective-permute-start.23) | collective-permute-done | bytes 131104 | tf_op jit(solution)/shard_map/ppermute | solution.py:49
  96.7 1.0 fusion.6
  97.7 2.5 %collective-permute-start.24 = (bf16[2,128,128]{2,1,0:T(8,128)(2,1)S(1)}, bf16[2,128,128]{2,1,0:T(8,128)(2,1)S(1)}, u32[]{:S(2)}, u32[]{:S(2)}) collective-permute-start(bf16[2,128,128]{2,1,0:T(8,128)(2,1)S(1)} %fusion.6), channel_id=1, source_target_pairs={{0,32},{1,33},{2,34},{3,35},{4,36},{5,37},{6,38},{7,39},{8,40},{9,... | collective-permute-start | bytes 196616 | tf_op jit(solution)/shard_map/ppermute | solution.py:49
  100.2 1.2 constant_dynamic-update-slice_fusion.5
  101.4 2.0 %collective-permute-done.25 = bf16[2,4,384,128]{3,2,1,0:T(8,128)(2,1)} collective-permute-done((bf16[2,4,384,128]{3,2,1,0:T(8,128)(2,1)}, bf16[2,4,384,128]{3,2,1,0:T(8,128)(2,1)}, u32[]{:S(2)}, u32[]{:S(2)}) %collective-permute-start.25) | collective-permute-done | bytes 786464 | tf_op jit(solution)/shard_map/ppermute | solution.py:49
  103.4 1.2 constant_dynamic-update-slice_fusion.4.r_ref
  104.7 2.7 %shard_map.114 = bf16[384,2048]{1,0:T(8,128)(2,1)S(1)} custom-call(s32[13]{0:T(128)S(1)} %concatenate.17.s_ref, bf16[384,1024]{1,0:T(8,128)(2,1)S(1)} %copy-done.2, bf16[4,4,640,128]{3,2,1,0:T(8,128)(2,1)S(1)} %pad_maximum_fusion.w_ref, bf16[4,4,384,128]{3,2,1,0:T(8,128)(2,1)S(1)} %constant_dynamic-update-slice_fusion.4.r_ref), custom_call_target="tpu_custom_call" | custom-call | flops 4831838208 | bytes 12582912 | tf_op jit(solution)/shard_map/pallas_call | solution.py:207
  107.6 0.1 collective-permute-start.26
  107.7 4.7 %collective-permute-done.26 = f32[2,128,128]{2,1,0:T(8,128)S(1)} collective-permute-done((f32[2,128,128]{2,1,0:T(8,128)S(1)}, f32[2,128,128]{2,1,0:T(8,128)S(1)}, u32[]{:S(2)}, u32[]{:S(2)}) %collective-permute-start.26) | collective-permute-done | bytes 131104 | tf_op jit(solution)/shard_map/ppermute | solution.py:49
  112.4 0.5 collective-permute-start.27
  112.8 5.1 %shard_map.115 = bf16[384,4096]{1,0:T(8,128)(2,1)} custom-call(s32[13]{0:T(128)S(1)} %concatenate.17.s_ref, bf16[384,1024]{1,0:T(8,128)(2,1)S(1)} %copy-done, bf16[4,4,640,128]{3,2,1,0:T(8,128)(2,1)S(1)} %pad_maximum_fusion.w_ref, bf16[4,4,384,128]{3,2,1,0:T(8,128)(2,1)S(1)} %constant_dynamic-update-slice_fusion.4.r_ref, ...), custom_call_target="tpu_custom_call" | custom-call | flops 1610612736 | bytes 9437184 | tf_op jit(solution)/shard_map/pallas_call | solution.py:221
  118.0 1.5 %collective-permute-done.27 = f32[2,2,128,128]{3,2,1,0:T(8,128)S(1)} collective-permute-done((f32[2,2,128,128]{3,2,1,0:T(8,128)S(1)}, f32[2,2,128,128]{3,2,1,0:T(8,128)S(1)}, u32[]{:S(2)}, u32[]{:S(2)}) %collective-permute-start.27) | collective-permute-done | bytes 262176 | tf_op jit(solution)/shard_map/ppermute | solution.py:49
  119.5 0.3 collective-permute-start.29
  119.9 1.6 %collective-permute-done.29.other_ref = f32[4,2,128,128]{3,2,1,0:T(8,128)S(1)} collective-permute-done((f32[4,2,128,128]{3,2,1,0:T(8,128)S(1)}, f32[4,2,128,128]{3,2,1,0:T(8,128)S(1)}, u32[]{:S(2)}, u32[]{:S(2)}) %collective-permute-start.29) | collective-permute-done | bytes 524320 | tf_op jit(solution)/shard_map/ppermute | solution.py:49
  121.5 1.1 copy-done.6
  122.6 2.2 %shard_map.116 = (f32[256,640]{1,0:T(8,128)}, f32[256,640]{1,0:T(8,128)}, f32[256,640]{1,0:T(8,128)}, f32[256,384]{1,0:T(8,128)}) custom-call(s32[9]{0:T(128)S(1)} %stack.205.s_ref, f32[4,2,128,128]{3,2,1,0:T(8,128)S(1)} %constant_dynamic-update-slice_fusion.6.mine_ref, f32[4,2,128,128]{3,2,1,0:T(8,128)S(1)} %collective-permute-done.29.other_ref, ...), custom_call_target="tpu_custom_call" | custom-call | flops 4194304 | bytes 6291456 | tf_op jit(solution)/shard_map/pallas_call | solution.py:263
  (79 shorter events, 1.2 us)
Async XLA Ops:
  0.6 19.9 %collective-permute-start.2 = (bf16[384,4096]{1,0:T(8,128)(2,1)}, bf16[384,4096]{1,0:T(8,128)(2,1)}, u32[]{:S(2)}, u32[]{:S(2)}) collective-permute-start(bf16[384,4096]{1,0:T(8,128)(2,1)} %t_hbm.3), channel_id=1, source_target_pairs={{0,16},{1,17},{2,18},{3,19},{4,20},{5,21},{6,22},{7,23},{8,24},{9,... | collective-permute-start | bytes 9437192 | tf_op jit(solution)/shard_map/ppermute | solution.py:49
  4.0 16.6 %collective-permute-start.3 = (bf16[384,1024]{1,0:T(8,128)(2,1)}, bf16[384,1024]{1,0:T(8,128)(2,1)S(1)}, u32[]{:S(2)}, u32[]{:S(2)}) collective-permute-start(bf16[384,1024]{1,0:T(8,128)(2,1)} %cot_ref.1), channel_id=1, source_target_pairs={{0,16},{1,17},{2,18},{3,19},{4,20},{5,21},{6,22},{7,23},{8,24},{9,... | collective-permute-start | bytes 2359304 | tf_op jit(solution)/shard_map/ppermute | solution.py:49
  4.1 1.0 copy-start.3
  5.2 15.4 %copy-start.8 = (s32[13]{0:T(128)}, s32[13]{0:T(128)S(1)}, u32[]{:S(2)}) copy-start(s32[13]{0:T(128)S(1)} %stack.168.s_ref) | copy-start | bytes 160
  5.8 6.2 %collective-permute-start = (bf16[640,128]{1,0:T(8,128)(2,1)S(1)}, bf16[640,128]{1,0:T(8,128)(2,1)S(1)}, u32[]{:S(2)}, u32[]{:S(2)}) collective-permute-start(bf16[640,128]{1,0:T(8,128)(2,1)S(1)} %shard_map.110), channel_id=1, source_target_pairs={{0,28},{1,21},{2,30},{3,23},{4,16},{5,25},{6,18},{7,27},{8,20},{9,... | collective-permute-start | bytes 491528 | tf_op jit(solution)/shard_map/ppermute | solution.py:49
  6.0 1.0 copy-start.4
  7.0 1.0 copy-start.7
  8.1 4.0 %collective-permute-start.1 = (bf16[384,128]{1,0:T(8,128)(2,1)S(1)}, bf16[384,128]{1,0:T(8,128)(2,1)S(1)}, u32[]{:S(2)}, u32[]{:S(2)}) collective-permute-start(bf16[384,128]{1,0:T(8,128)(2,1)S(1)} %get-tuple-element.121), channel_id=1, source_target_pairs={{0,16},{1,17},{2,18},{3,19},{4,20},{5,21},{6,22},{7,23},{8,24},{9,... | collective-permute-start | bytes 294920 | tf_op jit(solution)/shard_map/ppermute | solution.py:49
  12.1 15.7 %collective-permute-start.4 = (bf16[2,640,128]{2,1,0:T(8,128)(2,1)S(1)}, bf16[2,640,128]{2,1,0:T(8,128)(2,1)S(1)}, u32[]{:S(2)}, u32[]{:S(2)}) collective-permute-start(bf16[2,640,128]{2,1,0:T(8,128)(2,1)S(1)} %pad_maximum_fusion.3), channel_id=1, source_target_pairs={{0,20},{1,29},{2,22},{3,31},{4,24},{5,17},{6,26},{7,19},{8,28},{9,... | collective-permute-start | bytes 983048 | tf_op jit(solution)/shard_map/ppermute | solution.py:49
  14.5 13.4 %collective-permute-start.5 = (bf16[384,128]{1,0:T(8,128)(2,1)S(1)}, bf16[384,128]{1,0:T(8,128)(2,1)S(1)}, u32[]{:S(2)}, u32[]{:S(2)}) collective-permute-start(bf16[384,128]{1,0:T(8,128)(2,1)S(1)} %select_select_fusion), channel_id=1, source_target_pairs={{0,49},{1,48},{2,51},{3,50},{4,53},{5,52},{6,55},{7,54},{8,57},{9,... | collective-permute-start | bytes 294920 | tf_op jit(solution)/shard_map/ppermute | solution.py:49
  20.5 1.0 copy-start.1
  27.8 0.7 copy-start.18
  28.6 17.2 %collective-permute-start.6 = (bf16[2,4,4,128,128]{4,3,2,1,0:T(8,128)(2,1)}, bf16[2,4,4,128,128]{4,3,2,1,0:T(8,128)(2,1)S(1)}, u32[]{:S(2)}, u32[]{:S(2)}) collective-permute-start(bf16[2,4,4,128,128]{4,3,2,1,0:T(8,128)(2,1)} %get-tuple-element.75), channel_id=1, source_target_pairs={{0,20},{1,29},{2,22},{3,31},{4,24},{5,17},{6,26},{7,19},{8,28},{9,... | collective-permute-start | bytes 3145736 | tf_op jit(solution)/shard_map/ppermute | solution.py:49
  28.8 17.0 %collective-permute-start.7 = (bf16[2,4,4,128,128]{4,3,2,1,0:T(8,128)(2,1)}, bf16[2,4,4,128,128]{4,3,2,1,0:T(8,128)(2,1)S(1)}, u32[]{:S(2)}, u32[]{:S(2)}) collective-permute-start(bf16[2,4,4,128,128]{4,3,2,1,0:T(8,128)(2,1)} %get-tuple-element.76), channel_id=1, source_target_pairs={{0,80},{1,209},{2,82},{3,211},{4,212},{5,85},{6,214},{7,87},{8,88}... | collective-permute-start | bytes 3145736 | tf_op jit(solution)/shard_map/ppermute | solution.py:49
  29.8 20.1 %collective-permute-start.8 = (bf16[4,640,128]{2,1,0:T(8,128)(2,1)S(1)}, bf16[4,640,128]{2,1,0:T(8,128)(2,1)S(1)}, u32[]{:S(2)}, u32[]{:S(2)}) collective-permute-start(bf16[4,640,128]{2,1,0:T(8,128)(2,1)S(1)} %constant_dynamic-update-slice_fusion), channel_id=1, source_target_pairs={{0,17},{1,18},{2,19},{3,48},{4,55},{5,20},{6,21},{7,22},{8,25},{9,... | collective-permute-start | bytes 1966088 | tf_op jit(solution)/shard_map/ppermute | solution.py:49
  30.8 19.1 %collective-permute-start.9 = (bf16[4,640,128]{2,1,0:T(8,128)(2,1)S(1)}, bf16[4,640,128]{2,1,0:T(8,128)(2,1)S(1)}, u32[]{:S(2)}, u32[]{:S(2)}) collective-permute-start(bf16[4,640,128]{2,1,0:T(8,128)(2,1)S(1)} %constant_dynamic-update-slice_fusion), channel_id=1, source_target_pairs={{0,51},{1,16},{2,17},{3,18},{4,21},{5,22},{6,23},{7,52},{8,59},{9,... | collective-permute-start | bytes 1966088 | tf_op jit(solution)/shard_map/ppermute | solution.py:49
  31.7 14.1 %collective-permute-start.10 = (bf16[384,128]{1,0:T(8,128)(2,1)S(1)}, bf16[384,128]{1,0:T(8,128)(2,1)S(1)}, u32[]{:S(2)}, u32[]{:S(2)}) collective-permute-start(bf16[384,128]{1,0:T(8,128)(2,1)S(1)} %broadcast_select_fusion.1), channel_id=1, source_target_pairs={{0,80},{1,209},{2,82},{3,211},{4,212},{5,85},{6,214},{7,87},{8,88}... | collective-permute-start | bytes 294920 | tf_op jit(solution)/shard_map/ppermute | solution.py:49
  45.8 1.0 copy-start.13
  45.8 1.3 %copy-start.11 = (bf16[2,4,4,128,128]{4,3,2,1,0:T(8,128)(2,1)}, bf16[2,4,4,128,128]{4,3,2,1,0:T(8,128)(2,1)S(1)}, u32[]{:S(2)}) copy-start(bf16[2,4,4,128,128]{4,3,2,1,0:T(8,128)(2,1)S(1)} %collective-permute-done.7) | copy-start | bytes 3145732
  49.9 12.3 %copy-start.10 = (f32[2,4,4,128,128]{4,3,2,1,0:T(8,128)S(1)}, f32[2,4,4,128,128]{4,3,2,1,0:T(8,128)}, u32[]{:S(2)}) copy-start(f32[2,4,4,128,128]{4,3,2,1,0:T(8,128)} %get-tuple-element.79) | copy-start | bytes 6291460
  49.9 0.8 copy-start.14
  50.7 0.8 copy-start.16
  51.6 9.1 %collective-permute-start.11 = (bf16[4,4,128,128]{3,2,1,0:T(8,128)(2,1)}, bf16[4,4,128,128]{3,2,1,0:T(8,128)(2,1)S(1)}, u32[]{:S(2)}, u32[]{:S(2)}) collective-permute-start(bf16[4,4,128,128]{3,2,1,0:T(8,128)(2,1)} %get-tuple-element.85), channel_id=1, source_target_pairs={{0,28},{1,21},{2,30},{3,23},{4,16},{5,25},{6,18},{7,27},{8,20},{9,... | collective-permute-start | bytes 1572872 | tf_op jit(solution)/shard_map/ppermute | solution.py:49
  51.6 4.3 %collective-permute-start.13 = (bf16[384,128]{1,0:T(8,128)(2,1)S(1)}, bf16[384,128]{1,0:T(8,128)(2,1)S(1)}, u32[]{:S(2)}, u32[]{:S(2)}) collective-permute-start(bf16[384,128]{1,0:T(8,128)(2,1)S(1)} %broadcast_select_fusion.2), channel_id=1, source_target_pairs={{0,208},{1,81},{2,210},{3,83},{4,84},{5,213},{6,86},{7,215},{8,216... | collective-permute-start | bytes 294920 | tf_op jit(solution)/shard_map/ppermute | solution.py:49
  51.6 10.7 %copy-start.12 = (bf16[2,4,4,128,128]{4,3,2,1,0:T(8,128)(2,1)S(1)}, bf16[2,4,4,128,128]{4,3,2,1,0:T(8,128)(2,1)}, u32[]{:S(2)}) copy-start(bf16[2,4,4,128,128]{4,3,2,1,0:T(8,128)(2,1)} %copy-done.11) | copy-start | bytes 3145732
  51.6 10.6 %collective-permute-start.12 = (bf16[4,4,128,128]{3,2,1,0:T(8,128)(2,1)}, bf16[4,4,128,128]{3,2,1,0:T(8,128)(2,1)S(1)}, u32[]{:S(2)}, u32[]{:S(2)}) collective-permute-start(bf16[4,4,128,128]{3,2,1,0:T(8,128)(2,1)} %get-tuple-element.86), channel_id=1, source_target_pairs={{0,208},{1,81},{2,210},{3,83},{4,84},{5,213},{6,86},{7,215},{8,216... | collective-permute-start | bytes 1572872 | tf_op jit(solution)/shard_map/ppermute | solution.py:49
  53.3 11.4 %collective-permute-start.14 = (bf16[4,640,128]{2,1,0:T(8,128)(2,1)}, bf16[4,640,128]{2,1,0:T(8,128)(2,1)S(1)}, u32[]{:S(2)}, u32[]{:S(2)}) collective-permute-start(bf16[4,640,128]{2,1,0:T(8,128)(2,1)} %copy-done.16), channel_id=1, source_target_pairs={{0,17},{1,18},{2,19},{3,48},{4,55},{5,20},{6,21},{7,22},{8,25},{9,... | collective-permute-start | bytes 1966088 | tf_op jit(solution)/shard_map/ppermute | solution.py:49
  64.8 7.1 %collective-permute-start.15 = (bf16[2,4,128,128]{3,2,1,0:T(8,128)(2,1)S(1)}, bf16[2,4,128,128]{3,2,1,0:T(8,128)(2,1)S(1)}, u32[]{:S(2)}, u32[]{:S(2)}) collective-permute-start(bf16[2,4,128,128]{3,2,1,0:T(8,128)(2,1)S(1)} %slice.144), channel_id=1, source_target_pairs={{0,80},{1,209},{2,82},{3,211},{4,212},{5,85},{6,214},{7,87},{8,88}... | collective-permute-start | bytes 786440 | tf_op jit(solution)/shard_map/ppermute | solution.py:49
  65.0 7.1 %collective-permute-start.16 = (bf16[2,4,128,128]{3,2,1,0:T(8,128)(2,1)S(1)}, bf16[2,4,128,128]{3,2,1,0:T(8,128)(2,1)S(1)}, u32[]{:S(2)}, u32[]{:S(2)}) collective-permute-start(bf16[2,4,128,128]{3,2,1,0:T(8,128)(2,1)S(1)} %slice.143), channel_id=1, source_target_pairs={{0,20},{1,29},{2,22},{3,31},{4,24},{5,17},{6,26},{7,19},{8,28},{9,... | collective-permute-start | bytes 786440 | tf_op jit(solution)/shard_map/ppermute | solution.py:49
  67.5 4.6 %collective-permute-start.17 = (bf16[384,128]{1,0:T(8,128)(2,1)S(1)}, bf16[384,128]{1,0:T(8,128)(2,1)S(1)}, u32[]{:S(2)}, u32[]{:S(2)}) collective-permute-start(bf16[384,128]{1,0:T(8,128)(2,1)S(1)} %broadcast_select_fusion), channel_id=1, source_target_pairs={{0,17},{1,16},{2,19},{3,18},{4,21},{5,20},{6,23},{7,22},{8,25},{9,... | collective-permute-start | bytes 294920 | tf_op jit(solution)/shard_map/ppermute | solution.py:49
  72.1 10.4 %copy-start.15 = (bf16[4,640,128]{2,1,0:T(8,128)(2,1)S(1)}, bf16[4,640,128]{2,1,0:T(8,128)(2,1)}, u32[]{:S(2)}) copy-start(bf16[4,640,128]{2,1,0:T(8,128)(2,1)} %copy-done.14) | copy-start | bytes 1966084
  72.1 10.4 %copy-start.17 = (bf16[4,640,128]{2,1,0:T(8,128)(2,1)S(1)}, bf16[4,640,128]{2,1,0:T(8,128)(2,1)}, u32[]{:S(2)}) copy-start(bf16[4,640,128]{2,1,0:T(8,128)(2,1)} %copy-done.16) | copy-start | bytes 1966084
  72.2 8.3 %collective-permute-start.20 = (bf16[2,384,128]{2,1,0:T(8,128)(2,1)S(1)}, bf16[2,384,128]{2,1,0:T(8,128)(2,1)S(1)}, u32[]{:S(2)}, u32[]{:S(2)}) collective-permute-start(bf16[2,384,128]{2,1,0:T(8,128)(2,1)S(1)} %pad_maximum_fusion.5), channel_id=1, source_target_pairs={{0,51},{1,18},{2,17},{3,48},{4,55},{5,22},{6,21},{7,52},{8,59},{9,... | collective-permute-start | bytes 589832 | tf_op jit(solution)/shard_map/ppermute | solution.py:49
  73.1 4.7 %collective-permute-start.18 = (bf16[4,128,128]{2,1,0:T(8,128)(2,1)S(1)}, bf16[4,128,128]{2,1,0:T(8,128)(2,1)S(1)}, u32[]{:S(2)}, u32[]{:S(2)}) collective-permute-start(bf16[4,128,128]{2,1,0:T(8,128)(2,1)S(1)} %fusion.4), channel_id=1, source_target_pairs={{0,208},{1,81},{2,210},{3,83},{4,84},{5,213},{6,86},{7,215},{8,216... | collective-permute-start | bytes 393224 | tf_op jit(solution)/shard_map/ppermute | solution.py:49
  73.1 4.7 %collective-permute-start.19 = (bf16[4,128,128]{2,1,0:T(8,128)(2,1)S(1)}, bf16[4,128,128]{2,1,0:T(8,128)(2,1)S(1)}, u32[]{:S(2)}, u32[]{:S(2)}) collective-permute-start(bf16[4,128,128]{2,1,0:T(8,128)(2,1)S(1)} %fusion.5), channel_id=1, source_target_pairs={{0,28},{1,21},{2,30},{3,23},{4,16},{5,25},{6,18},{7,27},{8,20},{9,... | collective-permute-start | bytes 393224 | tf_op jit(solution)/shard_map/ppermute | solution.py:49
  80.6 10.4 %copy-start.9 = (f32[4,2,128,128]{3,2,1,0:T(8,128)}, f32[4,2,128,128]{3,2,1,0:T(8,128)S(1)}, u32[]{:S(2)}) copy-start(f32[4,2,128,128]{3,2,1,0:T(8,128)S(1)} %pad_maximum_fusion.2) | copy-start | bytes 1572868
  80.7 8.8 %collective-permute-start.22 = (bf16[4,384,128]{2,1,0:T(8,128)(2,1)S(1)}, bf16[4,384,128]{2,1,0:T(8,128)(2,1)S(1)}, u32[]{:S(2)}, u32[]{:S(2)}) collective-permute-start(bf16[4,384,128]{2,1,0:T(8,128)(2,1)S(1)} %constant_dynamic-update-slice_fusion.2), channel_id=1, source_target_pairs={{0,28},{1,21},{2,30},{3,23},{4,16},{5,25},{6,18},{7,27},{8,20},{9,... | collective-permute-start | bytes 1179656 | tf_op jit(solution)/shard_map/ppermute | solution.py:49
  82.4 7.1 %collective-permute-start.21 = (f32[2,2,128,128]{3,2,1,0:T(8,128)S(1)}, f32[2,2,128,128]{3,2,1,0:T(8,128)S(1)}, u32[]{:S(2)}, u32[]{:S(2)}) collective-permute-start(f32[2,2,128,128]{3,2,1,0:T(8,128)S(1)} %slice.98), channel_id=1, source_target_pairs={{0,17},{1,18},{2,19},{3,48},{4,55},{5,20},{6,21},{7,22},{8,25},{9,... | collective-permute-start | bytes 786440 | tf_op jit(solution)/shard_map/ppermute | solution.py:49
  89.5 2.2 %copy-start.19 = (f32[2,2,128,128]{3,2,1,0:T(8,128)}, f32[2,2,128,128]{3,2,1,0:T(8,128)S(1)}, u32[]{:S(2)}) copy-start(f32[2,2,128,128]{3,2,1,0:T(8,128)S(1)} %collective-permute-done.21) | copy-start | bytes 786436
  90.5 14.2 %copy-start.2 = (bf16[384,1024]{1,0:T(8,128)(2,1)S(1)}, bf16[384,1024]{1,0:T(8,128)(2,1)}, u32[]{:S(2)}) copy-start(bf16[384,1024]{1,0:T(8,128)(2,1)} %copy-done.1) | copy-start | bytes 2359300
  90.5 12.9 %collective-permute-start.25 = (bf16[2,4,384,128]{3,2,1,0:T(8,128)(2,1)}, bf16[2,4,384,128]{3,2,1,0:T(8,128)(2,1)}, u32[]{:S(2)}, u32[]{:S(2)}) collective-permute-start(bf16[2,4,384,128]{3,2,1,0:T(8,128)(2,1)} %pad_maximum_fusion.1), channel_id=1, source_target_pairs={{0,20},{1,29},{2,22},{3,31},{4,24},{5,17},{6,26},{7,19},{8,28},{9,... | collective-permute-start | bytes 2359304 | tf_op jit(solution)/shard_map/ppermute | solution.py:49
  91.7 5.0 %collective-permute-start.23 = (f32[2,128,128]{2,1,0:T(8,128)}, f32[2,128,128]{2,1,0:T(8,128)S(1)}, u32[]{:S(2)}, u32[]{:S(2)}) collective-permute-start(f32[2,128,128]{2,1,0:T(8,128)} %add_bitcast_fusion), channel_id=1, source_target_pairs={{0,51},{1,16},{2,17},{3,18},{4,21},{5,22},{6,23},{7,52},{8,59},{9,... | collective-permute-start | bytes 393224 | tf_op jit(solution)/shard_map/ppermute | solution.py:49
  97.7 9.7 %collective-permute-start.24 = (bf16[2,128,128]{2,1,0:T(8,128)(2,1)S(1)}, bf16[2,128,128]{2,1,0:T(8,128)(2,1)S(1)}, u32[]{:S(2)}, u32[]{:S(2)}) collective-permute-start(bf16[2,128,128]{2,1,0:T(8,128)(2,1)S(1)} %fusion.6), channel_id=1, source_target_pairs={{0,32},{1,33},{2,34},{3,35},{4,36},{5,37},{6,38},{7,39},{8,40},{9,... | collective-permute-start | bytes 196616 | tf_op jit(solution)/shard_map/ppermute | solution.py:49
  104.7 8.2 %copy-start = (bf16[384,1024]{1,0:T(8,128)(2,1)S(1)}, bf16[384,1024]{1,0:T(8,128)(2,1)}, u32[]{:S(2)}) copy-start(bf16[384,1024]{1,0:T(8,128)(2,1)} %cot_ref.1) | copy-start | bytes 2359300
  107.4 5.4 %collective-permute-start.28 = (bf16[384,2048]{1,0:T(8,128)(2,1)S(1)}, bf16[384,2048]{1,0:T(8,128)(2,1)S(1)}, u32[]{:S(2)}, u32[]{:S(2)}) collective-permute-start(bf16[384,2048]{1,0:T(8,128)(2,1)S(1)} %shard_map.114), channel_id=1, source_target_pairs={{0,16},{1,17},{2,18},{3,19},{4,20},{5,21},{6,22},{7,23},{8,24},{9,... | collective-permute-start | bytes 4718600 | tf_op jit(solution)/shard_map/ppermute | solution.py:49
  107.6 4.8 %collective-permute-start.26 = (f32[2,128,128]{2,1,0:T(8,128)S(1)}, f32[2,128,128]{2,1,0:T(8,128)S(1)}, u32[]{:S(2)}, u32[]{:S(2)}) collective-permute-start(f32[2,128,128]{2,1,0:T(8,128)S(1)} %get-tuple-element.124), channel_id=1, source_target_pairs={{0,208},{1,81},{2,210},{3,83},{4,84},{5,213},{6,86},{7,215},{8,216... | collective-permute-start | bytes 393224 | tf_op jit(solution)/shard_map/ppermute | solution.py:49
  112.4 9.2 %copy-start.5 = (f32[256,640]{1,0:T(8,128)S(1)}, f32[256,640]{1,0:T(8,128)}, u32[]{:S(2)}) copy-start(f32[256,640]{1,0:T(8,128)} %m_ref.1) | copy-start | bytes 1966084
  112.4 7.1 %collective-permute-start.27 = (f32[2,2,128,128]{3,2,1,0:T(8,128)S(1)}, f32[2,2,128,128]{3,2,1,0:T(8,128)S(1)}, u32[]{:S(2)}, u32[]{:S(2)}) collective-permute-start(f32[2,2,128,128]{3,2,1,0:T(8,128)S(1)} %pad_maximum_fusion.4), channel_id=1, source_target_pairs={{0,80},{1,209},{2,82},{3,211},{4,212},{5,85},{6,214},{7,87},{8,88}... | collective-permute-start | bytes 786440 | tf_op jit(solution)/shard_map/ppermute | solution.py:49
  119.5 2.0 %collective-permute-start.29 = (f32[4,2,128,128]{3,2,1,0:T(8,128)S(1)}, f32[4,2,128,128]{3,2,1,0:T(8,128)S(1)}, u32[]{:S(2)}, u32[]{:S(2)}) collective-permute-start(f32[4,2,128,128]{3,2,1,0:T(8,128)S(1)} %constant_dynamic-update-slice_fusion.6.mine_ref), channel_id=1, source_target_pairs={{0,16},{1,17},{2,18},{3,19},{4,20},{5,21},{6,22},{7,23},{8,24},{9,... | collective-permute-start | bytes 1572872 | tf_op jit(solution)/shard_map/ppermute | solution.py:49
  121.5 1.1 copy-start.6

commit v5 on v4

--- a/solution.py
+++ b/solution.py
@@ -149,7 +149,7 @@
         scratch_shapes=[pltpu.VMEM((4, 384, 1024), BF16)] * 2
         + [pltpu.VMEM((384, 1024), BF16)] * 2
         + [pltpu.SemaphoreType.DMA((10,))],
-        compiler_params=pltpu.CompilerParams(vmem_limit_bytes=56 << 20),
+        compiler_params=pltpu.CompilerParams(vmem_limit_bytes=(44 if keep else 56) << 20),
         cost_estimate=pl.CostEstimate(
             flops=768 * 2048 * 1024, bytes_accessed=9 << 20, transcendentals=0
         ),

time: 125 us -> 124 us (level)
  starting transfers between devices: 32.2 us -> 37.7 us
  waiting for transfers between devices: 46 us -> 41.5 us
  Pallas kernels: 24.3 us -> 22.1 us
  local copies, waits for them, and re-layouts: 13.4 us -> 11.9 us
  other arithmetic: 7.8 us -> 9.24 us
    ppermute x30, starting transfers between devices: 32.2 us -> 37.7 us  [send(): return lax.ppermute(value, AXES, pairs)]
    ppermute x30, waiting for transfers between devices: 46 us -> 41.5 us  [send(): return lax.ppermute(value, AXES, pairs)]
    pallas_call x2, Pallas kernels: 13.4 us -> 11.2 us  [chip_gradient(): pl.pallas_call(functools.partial(grad_kernel, keep), out_shape=(jax.Shape...]
    unnamed x44 -> x56, local copies, waits for them, and re-layouts: 10.1 us -> 8.4 us
  transfers between devices with their start and end apart: 30 -> 30, of which waited for: 15 -> 16; matrix products, arithmetic and copies ran while one was open for 9% -> 10% of each run, Pallas kernels for 18% -> 16%
where the time goes in v5:
time: 124 us
  waiting for transfers between devices  41.5 us (33%)
  starting transfers between devices  37.7 us (30%)
  Pallas kernels  22.1 us (18%)
  local copies, waits for them, and re-layouts  11.9 us (10%)
  other arithmetic  9.24 us (7%)
    ppermute x30, waiting for transfers between devices, send(): return lax.ppermute(value, AXES, pairs)  41.5 us
    ppermute x30, starting transfers between devices, send(): return lax.ppermute(value, AXES, pairs)  37.7 us
    pallas_call x2, Pallas kernels, chip_gradient(): pl.pallas_call(functools.partial(grad_kernel, keep), out_shape=(jax.Shape...  11.2 us
    unnamed x56, local copies, waits for them, and re-layouts  8.4 us
    pallas_call x1, Pallas kernels, our_input_gradient(): pl.pallas_call(ours_kernel, out_shape=jax.ShapeDtypeStruct((384, 4096), B...  5.13 us
    pallas_call x1, Pallas kernels, their_input_gradient(): pl.pallas_call(theirs_kernel, out_shape=jax.ShapeDtypeStruct((384, 2048),...  2.74 us
  transfers between devices with their start and end apart: 30, of which 16 were waited for; matrix products, arithmetic and copies ran while one was open for 10% of the time, Pallas kernels for 16%

profile of v5, /device:TPU:1, one launch (start us, length us, event | category | flops | bytes accessed | tf_op | source)
XLA Modules:
  0.0 123.5 jit_solution(4453647947380625310)
XLA Ops:
  0.6 3.3 %collective-permute-start.2 = (bf16[384,4096]{1,0:T(8,128)(2,1)}, bf16[384,4096]{1,0:T(8,128)(2,1)}, u32[]{:S(2)}, u32[]{:S(2)}) collective-permute-start(bf16[384,4096]{1,0:T(8,128)(2,1)} %t_hbm.3), channel_id=1, source_target_pairs={{0,16},{1,17},{2,18},{3,19},{4,20},{5,21},{6,22},{7,23},{8,24},{9,... | collective-permute-start | bytes 9437192 | tf_op jit(solution)/shard_map/ppermute | solution.py:49
  4.0 0.1 collective-permute-start.3
  4.2 1.0 copy-done.9
  5.2 0.6 shard_map.110
  6.0 1.0 copy-done.12
  7.0 0.1 shard_map.111
  7.1 3.0 %collective-permute-start.1 = (bf16[384,128]{1,0:T(8,128)(2,1)S(1)}, bf16[384,128]{1,0:T(8,128)(2,1)S(1)}, u32[]{:S(2)}, u32[]{:S(2)}) collective-permute-start(bf16[384,128]{1,0:T(8,128)(2,1)S(1)} %get-tuple-element.121), channel_id=1, source_target_pairs={{0,16},{1,17},{2,18},{3,19},{4,20},{5,21},{6,22},{7,23},{8,24},{9,... | collective-permute-start | bytes 294920 | tf_op jit(solution)/shard_map/ppermute | solution.py:49
  10.1 0.9 collective-permute-done.1
  11.1 2.3 %collective-permute-start.4 = (bf16[2,640,128]{2,1,0:T(8,128)(2,1)S(1)}, bf16[2,640,128]{2,1,0:T(8,128)(2,1)S(1)}, u32[]{:S(2)}, u32[]{:S(2)}) collective-permute-start(bf16[2,640,128]{2,1,0:T(8,128)(2,1)S(1)} %pad_maximum_fusion.3), channel_id=1, source_target_pairs={{0,20},{1,29},{2,22},{3,31},{4,24},{5,17},{6,26},{7,19},{8,28},{9,... | collective-permute-start | bytes 983048 | tf_op jit(solution)/shard_map/ppermute | solution.py:49
  13.4 7.1 %collective-permute-start.5 = (bf16[384,128]{1,0:T(8,128)(2,1)S(1)}, bf16[384,128]{1,0:T(8,128)(2,1)S(1)}, u32[]{:S(2)}, u32[]{:S(2)}) collective-permute-start(bf16[384,128]{1,0:T(8,128)(2,1)S(1)} %select_select_fusion), channel_id=1, source_target_pairs={{0,49},{1,48},{2,51},{3,50},{4,53},{5,52},{6,55},{7,54},{8,57},{9,... | collective-permute-start | bytes 294920 | tf_op jit(solution)/shard_map/ppermute | solution.py:49
  20.6 0.9 copy-done.3
  21.5 6.6 %shard_map.112 = (bf16[2,4,4,128,128]{4,3,2,1,0:T(8,128)(2,1)}, bf16[2,4,4,128,128]{4,3,2,1,0:T(8,128)(2,1)}) custom-call(s32[13]{0:T(128)} %copy-done.13, bf16[384,4096]{1,0:T(8,128)(2,1)} %t_hbm.3, bf16[384,4096]{1,0:T(8,128)(2,1)} %collective-permute-done.2.u_hbm, bf16[384,1024]{1,0:T(8,128)(2,1)} %cot_ref.1, bf16[384,1024]{1,0:T(8,128)(2,1)} %copy-done.3), custom_call_target="tpu_custom_call" | custom-call | flops 1610612736 | bytes 9437184 | tf_op jit(solution)/shard_map/pallas_call | solution.py:144
  28.2 0.7 copy-done.23
  28.9 0.2 collective-permute-start.6
  29.1 1.1 constant_dynamic-update-slice_fusion
  30.3 1.0 collective-permute-start.8
  31.2 0.9 collective-permute-start.9
  32.1 0.9 broadcast_select_fusion.1
  33.0 3.0 %collective-permute-start.10 = (bf16[384,128]{1,0:T(8,128)(2,1)S(1)}, bf16[384,128]{1,0:T(8,128)(2,1)S(1)}, u32[]{:S(2)}, u32[]{:S(2)}) collective-permute-start(bf16[384,128]{1,0:T(8,128)(2,1)S(1)} %broadcast_select_fusion.1), channel_id=1, source_target_pairs={{0,80},{1,209},{2,82},{3,211},{4,212},{5,85},{6,214},{7,87},{8,88}... | collective-permute-start | bytes 294920 | tf_op jit(solution)/shard_map/ppermute | solution.py:49
  36.1 0.6 copy-done.14
  36.7 4.6 %shard_map.113 = (f32[2,4,4,128,128]{4,3,2,1,0:T(8,128)S(1)}, f32[2,4,4,128,128]{4,3,2,1,0:T(8,128)S(1)}) custom-call(s32[13]{0:T(128)S(1)} %copy-done.14, bf16[384,4096]{1,0:T(8,128)(2,1)S(1)} %copy-done, bf16[384,4096]{1,0:T(8,128)(2,1)} %collective-permute-done.2.u_hbm, bf16[384,1024]{1,0:T(8,128)(2,1)S(1)} %copy-done.1, bf16[384,1024]{1,0:T(8,128)(2,1)S(1)} %copy-done.4), custom_call_target="tpu_custom_call" | custom-call | flops 1610612736 | bytes 9437184 | tf_op jit(solution)/shard_map/pallas_call | solution.py:144
  41.4 4.7 %collective-permute-done.10 = bf16[384,128]{1,0:T(8,128)(2,1)S(1)} collective-permute-done((bf16[384,128]{1,0:T(8,128)(2,1)S(1)}, bf16[384,128]{1,0:T(8,128)(2,1)S(1)}, u32[]{:S(2)}, u32[]{:S(2)}) %collective-permute-start.10) | collective-permute-done | bytes 98336 | tf_op jit(solution)/shard_map/ppermute | solution.py:49
  46.1 2.3 %fusion = (bf16[4,4,128,128]{3,2,1,0:T(8,128)(2,1)}, bf16[4,4,128,128]{3,2,1,0:T(8,128)(2,1)S(1)}) fusion(f32[2,4,4,128,128]{4,3,2,1,0:T(8,128)S(1)} %get-tuple-element.77, bf16[2,4,4,128,128]{4,3,2,1,0:T(8,128)(2,1)} %collective-permute-done.6, bf16[2,4,4,128,128]{4,3,2,1,0:T(8,128)(2,1)} %collective-permute-done.7, ...), kind=kLoop, calls=%fused_computation.6 | loop fusion | flops 1572864 | bytes 4194304 | tf_op jit(solution)/shard_map/convert_element_type | solution.py:319
  48.4 0.1 collective-permute-done.8
  48.5 0.8 copy-done.18
  49.4 0.8 copy-done.20
  50.2 1.7 %collective-permute-start.12 = (bf16[4,4,128,128]{3,2,1,0:T(8,128)(2,1)S(1)}, bf16[4,4,128,128]{3,2,1,0:T(8,128)(2,1)S(1)}, u32[]{:S(2)}, u32[]{:S(2)}) collective-permute-start(bf16[4,4,128,128]{3,2,1,0:T(8,128)(2,1)S(1)} %get-tuple-element.86), channel_id=1, source_target_pairs={{0,208},{1,81},{2,210},{3,83},{4,84},{5,213},{6,86},{7,215},{8,216... | collective-permute-start | bytes 1572872 | tf_op jit(solution)/shard_map/ppermute | solution.py:49
  52.0 0.8 collective-permute-start.14
  52.8 1.7 %collective-permute-done.13 = bf16[384,128]{1,0:T(8,128)(2,1)S(1)} collective-permute-done((bf16[384,128]{1,0:T(8,128)(2,1)S(1)}, bf16[384,128]{1,0:T(8,128)(2,1)S(1)}, u32[]{:S(2)}, u32[]{:S(2)}) %collective-permute-start.13) | collective-permute-done | bytes 98336 | tf_op jit(solution)/shard_map/ppermute | solution.py:49
  54.6 4.8 %collective-permute-done.11 = bf16[4,4,128,128]{3,2,1,0:T(8,128)(2,1)S(1)} collective-permute-done((bf16[4,4,128,128]{3,2,1,0:T(8,128)(2,1)}, bf16[4,4,128,128]{3,2,1,0:T(8,128)(2,1)S(1)}, u32[]{:S(2)}, u32[]{:S(2)}) %collective-permute-start.11) | collective-permute-done | bytes 524320 | tf_op jit(solution)/shard_map/ppermute | solution.py:49
  59.3 1.5 %bitcast_add_fusion.1 = f32[4,4,128,128]{3,2,1,0:T(8,128)S(1)} fusion(bf16[4,4,128,128]{3,2,1,0:T(8,128)(2,1)S(1)} %collective-permute-done.11, f32[2,4,4,128,128]{4,3,2,1,0:T(8,128)} %copy-done.8, bf16[2,4,4,128,128]{4,3,2,1,0:T(8,128)(2,1)} %collective-permute-done.6), kind=kLoop, calls=%fused_computation.2 | loop fusion | flops 1048576 | bytes 3145728 | tf_op jit(solution)/shard_map/add | solution.py:330
  60.9 1.2 bitcast_add_fusion
  62.1 1.3 %collective-permute-done.14 = bf16[4,640,128]{2,1,0:T(8,128)(2,1)S(1)} collective-permute-done((bf16[4,640,128]{2,1,0:T(8,128)(2,1)}, bf16[4,640,128]{2,1,0:T(8,128)(2,1)S(1)}, u32[]{:S(2)}, u32[]{:S(2)}) %collective-permute-start.14) | collective-permute-done | bytes 655392 | tf_op jit(solution)/shard_map/ppermute | solution.py:49
  63.6 2.5 %collective-permute-start.16 = (bf16[2,4,128,128]{3,2,1,0:T(8,128)(2,1)S(1)}, bf16[2,4,128,128]{3,2,1,0:T(8,128)(2,1)S(1)}, u32[]{:S(2)}, u32[]{:S(2)}) collective-permute-start(bf16[2,4,128,128]{3,2,1,0:T(8,128)(2,1)S(1)} %slice.143), channel_id=1, source_target_pairs={{0,20},{1,29},{2,22},{3,31},{4,24},{5,17},{6,26},{7,19},{8,28},{9,... | collective-permute-start | bytes 786440 | tf_op jit(solution)/shard_map/ppermute | solution.py:49
  66.0 4.5 %collective-permute-done.15 = bf16[2,4,128,128]{3,2,1,0:T(8,128)(2,1)S(1)} collective-permute-done((bf16[2,4,128,128]{3,2,1,0:T(8,128)(2,1)S(1)}, bf16[2,4,128,128]{3,2,1,0:T(8,128)(2,1)S(1)}, u32[]{:S(2)}, u32[]{:S(2)}) %collective-permute-start.15) | collective-permute-done | bytes 262176 | tf_op jit(solution)/shard_map/ppermute | solution.py:49
  70.6 0.1 collective-permute-done.16
  70.8 2.8 %collective-permute-start.20 = (bf16[2,384,128]{2,1,0:T(8,128)(2,1)S(1)}, bf16[2,384,128]{2,1,0:T(8,128)(2,1)S(1)}, u32[]{:S(2)}, u32[]{:S(2)}) collective-permute-start(bf16[2,384,128]{2,1,0:T(8,128)(2,1)S(1)} %pad_maximum_fusion.5), channel_id=1, source_target_pairs={{0,51},{1,18},{2,17},{3,48},{4,55},{5,22},{6,21},{7,52},{8,59},{9,... | collective-permute-start | bytes 589832 | tf_op jit(solution)/shard_map/ppermute | solution.py:49
  73.6 0.6 collective-permute-start.19
  74.2 4.1 %collective-permute-done.18 = bf16[4,128,128]{2,1,0:T(8,128)(2,1)S(1)} collective-permute-done((bf16[4,128,128]{2,1,0:T(8,128)(2,1)S(1)}, bf16[4,128,128]{2,1,0:T(8,128)(2,1)S(1)}, u32[]{:S(2)}, u32[]{:S(2)}) %collective-permute-start.18) | collective-permute-done | bytes 131104 | tf_op jit(solution)/shard_map/ppermute | solution.py:49
  78.3 1.1 collective-permute-done.20
  79.6 1.5 %collective-permute-start.22 = (bf16[4,384,128]{2,1,0:T(8,128)(2,1)S(1)}, bf16[4,384,128]{2,1,0:T(8,128)(2,1)S(1)}, u32[]{:S(2)}, u32[]{:S(2)}) collective-permute-start(bf16[4,384,128]{2,1,0:T(8,128)(2,1)S(1)} %constant_dynamic-update-slice_fusion.2), channel_id=1, source_target_pairs={{0,28},{1,21},{2,30},{3,23},{4,16},{5,25},{6,18},{7,27},{8,20},{9,... | collective-permute-start | bytes 1179656 | tf_op jit(solution)/shard_map/ppermute | solution.py:49
  81.1 1.1 collective-permute-start.21
  82.2 0.3 pad_maximum_fusion.w_ref
  82.5 5.7 %collective-permute-done.21 = f32[2,2,128,128]{3,2,1,0:T(8,128)S(1)} collective-permute-done((f32[2,2,128,128]{3,2,1,0:T(8,128)S(1)}, f32[2,2,128,128]{3,2,1,0:T(8,128)S(1)}, u32[]{:S(2)}, u32[]{:S(2)}) %collective-permute-start.21) | collective-permute-done | bytes 262176 | tf_op jit(solution)/shard_map/ppermute | solution.py:49
  88.2 1.0 pad_maximum_fusion.1
  89.2 0.7 collective-permute-start.25
  89.9 0.7 add_bitcast_fusion
  90.6 0.7 dynamic-slice_bitcast_fusion
  91.3 4.2 %collective-permute-done.23 = f32[2,128,128]{2,1,0:T(8,128)S(1)} collective-permute-done((f32[2,128,128]{2,1,0:T(8,128)}, f32[2,128,128]{2,1,0:T(8,128)S(1)}, u32[]{:S(2)}, u32[]{:S(2)}) %collective-permute-start.23) | collective-permute-done | bytes 131104 | tf_op jit(solution)/shard_map/ppermute | solution.py:49
  95.6 1.0 fusion.6
  96.6 2.3 %collective-permute-start.24 = (bf16[2,128,128]{2,1,0:T(8,128)(2,1)S(1)}, bf16[2,128,128]{2,1,0:T(8,128)(2,1)S(1)}, u32[]{:S(2)}, u32[]{:S(2)}) collective-permute-start(bf16[2,128,128]{2,1,0:T(8,128)(2,1)S(1)} %fusion.6), channel_id=1, source_target_pairs={{0,32},{1,33},{2,34},{3,35},{4,36},{5,37},{6,38},{7,39},{8,40},{9,... | collective-permute-start | bytes 196616 | tf_op jit(solution)/shard_map/ppermute | solution.py:49
  98.9 1.2 constant_dynamic-update-slice_fusion.5
  100.0 2.1 %collective-permute-done.25 = bf16[2,4,384,128]{3,2,1,0:T(8,128)(2,1)} collective-permute-done((bf16[2,4,384,128]{3,2,1,0:T(8,128)(2,1)}, bf16[2,4,384,128]{3,2,1,0:T(8,128)(2,1)}, u32[]{:S(2)}, u32[]{:S(2)}) %collective-permute-start.25) | collective-permute-done | bytes 786464 | tf_op jit(solution)/shard_map/ppermute | solution.py:49
  102.1 1.2 %constant_dynamic-update-slice_fusion.4.r_ref = bf16[4,4,384,128]{3,2,1,0:T(8,128)(2,1)S(1)} fusion(bf16[4,4,384,128]{3,2,1,0:T(8,128)(2,1)S(1)} %constant_dynamic-update-slice_fusion.5, bf16[2,4,384,128]{3,2,1,0:T(8,128)(2,1)} %collective-permute-done.25), kind=kLoop, calls=%fused_computation.35 | loop fusion | bytes 1572864 | tf_op jit(solution)/shard_map/concatenate | solution.py:369
  103.4 2.7 %shard_map.114 = bf16[384,2048]{1,0:T(8,128)(2,1)S(1)} custom-call(s32[13]{0:T(128)S(1)} %concatenate.17.s_ref, bf16[384,1024]{1,0:T(8,128)(2,1)S(1)} %copy-done.5, bf16[4,4,640,128]{3,2,1,0:T(8,128)(2,1)S(1)} %pad_maximum_fusion.w_ref, bf16[4,4,384,128]{3,2,1,0:T(8,128)(2,1)S(1)} %constant_dynamic-update-slice_fusion.4.r_ref), custom_call_target="tpu_custom_call" | custom-call | flops 4831838208 | bytes 12582912 | tf_op jit(solution)/shard_map/pallas_call | solution.py:207
  106.3 0.7 collective-permute-start.26
  107.0 4.0 %collective-permute-done.26 = f32[2,128,128]{2,1,0:T(8,128)S(1)} collective-permute-done((f32[2,128,128]{2,1,0:T(8,128)S(1)}, f32[2,128,128]{2,1,0:T(8,128)S(1)}, u32[]{:S(2)}, u32[]{:S(2)}) %collective-permute-start.26) | collective-permute-done | bytes 131104 | tf_op jit(solution)/shard_map/ppermute | solution.py:49
  111.1 1.4 %collective-permute-start.27 = (f32[2,2,128,128]{3,2,1,0:T(8,128)S(1)}, f32[2,2,128,128]{3,2,1,0:T(8,128)S(1)}, u32[]{:S(2)}, u32[]{:S(2)}) collective-permute-start(f32[2,2,128,128]{3,2,1,0:T(8,128)S(1)} %pad_maximum_fusion.4), channel_id=1, source_target_pairs={{0,80},{1,209},{2,82},{3,211},{4,212},{5,85},{6,214},{7,87},{8,88}... | collective-permute-start | bytes 786440 | tf_op jit(solution)/shard_map/ppermute | solution.py:49
  112.5 5.1 %shard_map.115 = bf16[384,4096]{1,0:T(8,128)(2,1)} custom-call(s32[13]{0:T(128)S(1)} %concatenate.17.s_ref, bf16[384,1024]{1,0:T(8,128)(2,1)S(1)} %copy-done.2, bf16[4,4,640,128]{3,2,1,0:T(8,128)(2,1)S(1)} %pad_maximum_fusion.w_ref, bf16[4,4,384,128]{3,2,1,0:T(8,128)(2,1)S(1)} %constant_dynamic-update-slice_fusion.4.r_ref, ...), custom_call_target="tpu_custom_call" | custom-call | flops 1610612736 | bytes 9437184 | tf_op jit(solution)/shard_map/pallas_call | solution.py:221
  117.7 0.5 collective-permute-done.27
  118.2 0.3 collective-permute-start.29
  118.6 1.6 %collective-permute-done.29.other_ref = f32[4,2,128,128]{3,2,1,0:T(8,128)S(1)} collective-permute-done((f32[4,2,128,128]{3,2,1,0:T(8,128)S(1)}, f32[4,2,128,128]{3,2,1,0:T(8,128)S(1)}, u32[]{:S(2)}, u32[]{:S(2)}) %collective-permute-start.29) | collective-permute-done | bytes 524320 | tf_op jit(solution)/shard_map/ppermute | solution.py:49
  120.2 1.1 copy-done.11
  121.3 2.2 %shard_map.116 = (f32[256,640]{1,0:T(8,128)}, f32[256,640]{1,0:T(8,128)}, f32[256,640]{1,0:T(8,128)}, f32[256,384]{1,0:T(8,128)}) custom-call(s32[9]{0:T(128)S(1)} %stack.205.s_ref, f32[4,2,128,128]{3,2,1,0:T(8,128)S(1)} %constant_dynamic-update-slice_fusion.6.mine_ref, f32[4,2,128,128]{3,2,1,0:T(8,128)S(1)} %collective-permute-done.29.other_ref, ...), custom_call_target="tpu_custom_call" | custom-call | flops 4194304 | bytes 6291456 | tf_op jit(solution)/shard_map/pallas_call | solution.py:263
  (91 shorter events, 1.2 us)
Async XLA Ops:
  0.6 20.8 %collective-permute-start.2 = (bf16[384,4096]{1,0:T(8,128)(2,1)}, bf16[384,4096]{1,0:T(8,128)(2,1)}, u32[]{:S(2)}, u32[]{:S(2)}) collective-permute-start(bf16[384,4096]{1,0:T(8,128)(2,1)} %t_hbm.3), channel_id=1, source_target_pairs={{0,16},{1,17},{2,18},{3,19},{4,20},{5,21},{6,22},{7,23},{8,24},{9,... | collective-permute-start | bytes 9437192 | tf_op jit(solution)/shard_map/ppermute | solution.py:49
  4.0 16.6 %collective-permute-start.3 = (bf16[384,1024]{1,0:T(8,128)(2,1)}, bf16[384,1024]{1,0:T(8,128)(2,1)S(1)}, u32[]{:S(2)}, u32[]{:S(2)}) collective-permute-start(bf16[384,1024]{1,0:T(8,128)(2,1)} %cot_ref.1), channel_id=1, source_target_pairs={{0,16},{1,17},{2,18},{3,19},{4,20},{5,21},{6,22},{7,23},{8,24},{9,... | collective-permute-start | bytes 2359304 | tf_op jit(solution)/shard_map/ppermute | solution.py:49
  4.1 1.0 copy-start.9
  5.2 16.3 %copy-start.13 = (s32[13]{0:T(128)}, s32[13]{0:T(128)S(1)}, u32[]{:S(2)}) copy-start(s32[13]{0:T(128)S(1)} %stack.168.s_ref) | copy-start | bytes 160
  5.8 5.2 %collective-permute-start = (bf16[640,128]{1,0:T(8,128)(2,1)S(1)}, bf16[640,128]{1,0:T(8,128)(2,1)S(1)}, u32[]{:S(2)}, u32[]{:S(2)}) collective-permute-start(bf16[640,128]{1,0:T(8,128)(2,1)S(1)} %shard_map.110), channel_id=1, source_target_pairs={{0,28},{1,21},{2,30},{3,23},{4,16},{5,25},{6,18},{7,27},{8,20},{9,... | collective-permute-start | bytes 491528 | tf_op jit(solution)/shard_map/ppermute | solution.py:49
  6.0 1.0 copy-start.12
  7.1 4.0 %collective-permute-start.1 = (bf16[384,128]{1,0:T(8,128)(2,1)S(1)}, bf16[384,128]{1,0:T(8,128)(2,1)S(1)}, u32[]{:S(2)}, u32[]{:S(2)}) collective-permute-start(bf16[384,128]{1,0:T(8,128)(2,1)S(1)} %get-tuple-element.121), channel_id=1, source_target_pairs={{0,16},{1,17},{2,18},{3,19},{4,20},{5,21},{6,22},{7,23},{8,24},{9,... | collective-permute-start | bytes 294920 | tf_op jit(solution)/shard_map/ppermute | solution.py:49
  11.1 17.1 %collective-permute-start.4 = (bf16[2,640,128]{2,1,0:T(8,128)(2,1)S(1)}, bf16[2,640,128]{2,1,0:T(8,128)(2,1)S(1)}, u32[]{:S(2)}, u32[]{:S(2)}) collective-permute-start(bf16[2,640,128]{2,1,0:T(8,128)(2,1)S(1)} %pad_maximum_fusion.3), channel_id=1, source_target_pairs={{0,20},{1,29},{2,22},{3,31},{4,24},{5,17},{6,26},{7,19},{8,28},{9,... | collective-permute-start | bytes 983048 | tf_op jit(solution)/shard_map/ppermute | solution.py:49
  13.4 14.7 %copy-start.22 = (bf16[384,128]{1,0:T(8,128)(2,1)}, bf16[384,128]{1,0:T(8,128)(2,1)S(1)}, u32[]{:S(2)}) copy-start(bf16[384,128]{1,0:T(8,128)(2,1)S(1)} %select_select_fusion) | copy-start | bytes 294916
  13.4 14.7 %collective-permute-start.5 = (bf16[384,128]{1,0:T(8,128)(2,1)S(1)}, bf16[384,128]{1,0:T(8,128)(2,1)S(1)}, u32[]{:S(2)}, u32[]{:S(2)}) collective-permute-start(bf16[384,128]{1,0:T(8,128)(2,1)S(1)} %select_select_fusion), channel_id=1, source_target_pairs={{0,49},{1,48},{2,51},{3,50},{4,53},{5,52},{6,55},{7,54},{8,57},{9,... | collective-permute-start | bytes 294920 | tf_op jit(solution)/shard_map/ppermute | solution.py:49
  20.5 0.9 copy-start.3
  21.5 14.6 %copy-start = (bf16[384,4096]{1,0:T(8,128)(2,1)S(1)}, bf16[384,4096]{1,0:T(8,128)(2,1)}, u32[]{:S(2)}) copy-start(bf16[384,4096]{1,0:T(8,128)(2,1)} %t_hbm.3) | copy-start | bytes 9437188
  28.1 0.8 copy-start.25
  28.2 0.7 copy-start.23
  28.9 17.2 %collective-permute-start.6 = (bf16[2,4,4,128,128]{4,3,2,1,0:T(8,128)(2,1)}, bf16[2,4,4,128,128]{4,3,2,1,0:T(8,128)(2,1)}, u32[]{:S(2)}, u32[]{:S(2)}) collective-permute-start(bf16[2,4,4,128,128]{4,3,2,1,0:T(8,128)(2,1)} %get-tuple-element.75), channel_id=1, source_target_pairs={{0,20},{1,29},{2,22},{3,31},{4,24},{5,17},{6,26},{7,19},{8,28},{9,... | collective-permute-start | bytes 3145736 | tf_op jit(solution)/shard_map/ppermute | solution.py:49
  29.1 17.0 %collective-permute-start.7 = (bf16[2,4,4,128,128]{4,3,2,1,0:T(8,128)(2,1)}, bf16[2,4,4,128,128]{4,3,2,1,0:T(8,128)(2,1)}, u32[]{:S(2)}, u32[]{:S(2)}) collective-permute-start(bf16[2,4,4,128,128]{4,3,2,1,0:T(8,128)(2,1)} %get-tuple-element.76), channel_id=1, source_target_pairs={{0,80},{1,209},{2,82},{3,211},{4,212},{5,85},{6,214},{7,87},{8,88}... | collective-permute-start | bytes 3145736 | tf_op jit(solution)/shard_map/ppermute | solution.py:49
  29.1 7.0 %copy-start.1 = (bf16[384,1024]{1,0:T(8,128)(2,1)S(1)}, bf16[384,1024]{1,0:T(8,128)(2,1)}, u32[]{:S(2)}) copy-start(bf16[384,1024]{1,0:T(8,128)(2,1)} %cot_ref.1) | copy-start | bytes 2359300
  29.1 7.0 %copy-start.4 = (bf16[384,1024]{1,0:T(8,128)(2,1)S(1)}, bf16[384,1024]{1,0:T(8,128)(2,1)}, u32[]{:S(2)}) copy-start(bf16[384,1024]{1,0:T(8,128)(2,1)} %copy-done.3) | copy-start | bytes 2359300
  30.3 11.1 %copy-start.16 = (bf16[4,640,128]{2,1,0:T(8,128)(2,1)}, bf16[4,640,128]{2,1,0:T(8,128)(2,1)S(1)}, u32[]{:S(2)}) copy-start(bf16[4,640,128]{2,1,0:T(8,128)(2,1)S(1)} %constant_dynamic-update-slice_fusion) | copy-start | bytes 1966084
  30.3 18.3 %collective-permute-start.8 = (bf16[4,640,128]{2,1,0:T(8,128)(2,1)S(1)}, bf16[4,640,128]{2,1,0:T(8,128)(2,1)S(1)}, u32[]{:S(2)}, u32[]{:S(2)}) collective-permute-start(bf16[4,640,128]{2,1,0:T(8,128)(2,1)S(1)} %constant_dynamic-update-slice_fusion), channel_id=1, source_target_pairs={{0,17},{1,18},{2,19},{3,48},{4,55},{5,20},{6,21},{7,22},{8,25},{9,... | collective-permute-start | bytes 1966088 | tf_op jit(solution)/shard_map/ppermute | solution.py:49
  31.2 17.3 %collective-permute-start.9 = (bf16[4,640,128]{2,1,0:T(8,128)(2,1)S(1)}, bf16[4,640,128]{2,1,0:T(8,128)(2,1)S(1)}, u32[]{:S(2)}, u32[]{:S(2)}) collective-permute-start(bf16[4,640,128]{2,1,0:T(8,128)(2,1)S(1)} %constant_dynamic-update-slice_fusion), channel_id=1, source_target_pairs={{0,51},{1,16},{2,17},{3,18},{4,21},{5,22},{6,23},{7,52},{8,59},{9,... | collective-permute-start | bytes 1966088 | tf_op jit(solution)/shard_map/ppermute | solution.py:49
  33.0 13.1 %collective-permute-start.10 = (bf16[384,128]{1,0:T(8,128)(2,1)S(1)}, bf16[384,128]{1,0:T(8,128)(2,1)S(1)}, u32[]{:S(2)}, u32[]{:S(2)}) collective-permute-start(bf16[384,128]{1,0:T(8,128)(2,1)S(1)} %broadcast_select_fusion.1), channel_id=1, source_target_pairs={{0,80},{1,209},{2,82},{3,211},{4,212},{5,85},{6,214},{7,87},{8,88}... | collective-permute-start | bytes 294920 | tf_op jit(solution)/shard_map/ppermute | solution.py:49
  36.1 0.7 copy-start.14
  41.4 7.1 %copy-start.6 = (f32[2,4,4,128,128]{4,3,2,1,0:T(8,128)}, f32[2,4,4,128,128]{4,3,2,1,0:T(8,128)S(1)}, u32[]{:S(2)}) copy-start(f32[2,4,4,128,128]{4,3,2,1,0:T(8,128)S(1)} %get-tuple-element.79) | copy-start | bytes 6291460
  41.4 7.1 %copy-start.8 = (f32[2,4,4,128,128]{4,3,2,1,0:T(8,128)}, f32[2,4,4,128,128]{4,3,2,1,0:T(8,128)S(1)}, u32[]{:S(2)}) copy-start(f32[2,4,4,128,128]{4,3,2,1,0:T(8,128)S(1)} %get-tuple-element.77) | copy-start | bytes 6291460
  48.5 0.8 copy-start.18
  48.5 12.3 %copy-start.7 = (f32[2,4,4,128,128]{4,3,2,1,0:T(8,128)S(1)}, f32[2,4,4,128,128]{4,3,2,1,0:T(8,128)}, u32[]{:S(2)}) copy-start(f32[2,4,4,128,128]{4,3,2,1,0:T(8,128)} %copy-done.6) | copy-start | bytes 6291460
  49.4 0.8 copy-start.20
  50.2 9.1 %collective-permute-start.11 = (bf16[4,4,128,128]{3,2,1,0:T(8,128)(2,1)}, bf16[4,4,128,128]{3,2,1,0:T(8,128)(2,1)S(1)}, u32[]{:S(2)}, u32[]{:S(2)}) collective-permute-start(bf16[4,4,128,128]{3,2,1,0:T(8,128)(2,1)} %get-tuple-element.85), channel_id=1, source_target_pairs={{0,28},{1,21},{2,30},{3,23},{4,16},{5,25},{6,18},{7,27},{8,20},{9,... | collective-permute-start | bytes 1572872 | tf_op jit(solution)/shard_map/ppermute | solution.py:49
  50.2 4.3 %collective-permute-start.13 = (bf16[384,128]{1,0:T(8,128)(2,1)S(1)}, bf16[384,128]{1,0:T(8,128)(2,1)S(1)}, u32[]{:S(2)}, u32[]{:S(2)}) collective-permute-start(bf16[384,128]{1,0:T(8,128)(2,1)S(1)} %broadcast_select_fusion.2), channel_id=1, source_target_pairs={{0,208},{1,81},{2,210},{3,83},{4,84},{5,213},{6,86},{7,215},{8,216... | collective-permute-start | bytes 294920 | tf_op jit(solution)/shard_map/ppermute | solution.py:49
  50.2 10.6 %collective-permute-start.12 = (bf16[4,4,128,128]{3,2,1,0:T(8,128)(2,1)S(1)}, bf16[4,4,128,128]{3,2,1,0:T(8,128)(2,1)S(1)}, u32[]{:S(2)}, u32[]{:S(2)}) collective-permute-start(bf16[4,4,128,128]{3,2,1,0:T(8,128)(2,1)S(1)} %get-tuple-element.86), channel_id=1, source_target_pairs={{0,208},{1,81},{2,210},{3,83},{4,84},{5,213},{6,86},{7,215},{8,216... | collective-permute-start | bytes 1572872 | tf_op jit(solution)/shard_map/ppermute | solution.py:49
  52.0 11.4 %collective-permute-start.14 = (bf16[4,640,128]{2,1,0:T(8,128)(2,1)}, bf16[4,640,128]{2,1,0:T(8,128)(2,1)S(1)}, u32[]{:S(2)}, u32[]{:S(2)}) collective-permute-start(bf16[4,640,128]{2,1,0:T(8,128)(2,1)} %copy-done.20), channel_id=1, source_target_pairs={{0,17},{1,18},{2,19},{3,48},{4,55},{5,20},{6,21},{7,22},{8,25},{9,... | collective-permute-start | bytes 1966088 | tf_op jit(solution)/shard_map/ppermute | solution.py:49
  63.4 7.1 %collective-permute-start.15 = (bf16[2,4,128,128]{3,2,1,0:T(8,128)(2,1)S(1)}, bf16[2,4,128,128]{3,2,1,0:T(8,128)(2,1)S(1)}, u32[]{:S(2)}, u32[]{:S(2)}) collective-permute-start(bf16[2,4,128,128]{3,2,1,0:T(8,128)(2,1)S(1)} %slice.144), channel_id=1, source_target_pairs={{0,80},{1,209},{2,82},{3,211},{4,212},{5,85},{6,214},{7,87},{8,88}... | collective-permute-start | bytes 786440 | tf_op jit(solution)/shard_map/ppermute | solution.py:49
  63.6 7.1 %collective-permute-start.16 = (bf16[2,4,128,128]{3,2,1,0:T(8,128)(2,1)S(1)}, bf16[2,4,128,128]{3,2,1,0:T(8,128)(2,1)S(1)}, u32[]{:S(2)}, u32[]{:S(2)}) collective-permute-start(bf16[2,4,128,128]{3,2,1,0:T(8,128)(2,1)S(1)} %slice.143), channel_id=1, source_target_pairs={{0,20},{1,29},{2,22},{3,31},{4,24},{5,17},{6,26},{7,19},{8,28},{9,... | collective-permute-start | bytes 786440 | tf_op jit(solution)/shard_map/ppermute | solution.py:49
  66.0 4.7 %collective-permute-start.17 = (bf16[384,128]{1,0:T(8,128)(2,1)S(1)}, bf16[384,128]{1,0:T(8,128)(2,1)S(1)}, u32[]{:S(2)}, u32[]{:S(2)}) collective-permute-start(bf16[384,128]{1,0:T(8,128)(2,1)S(1)} %broadcast_select_fusion), channel_id=1, source_target_pairs={{0,17},{1,16},{2,19},{3,18},{4,21},{5,20},{6,23},{7,22},{8,25},{9,... | collective-permute-start | bytes 294920 | tf_op jit(solution)/shard_map/ppermute | solution.py:49
  70.7 11.4 %copy-start.17 = (bf16[4,640,128]{2,1,0:T(8,128)(2,1)S(1)}, bf16[4,640,128]{2,1,0:T(8,128)(2,1)}, u32[]{:S(2)}) copy-start(bf16[4,640,128]{2,1,0:T(8,128)(2,1)} %copy-done.16) | copy-start | bytes 1966084
  70.7 11.4 %copy-start.19 = (bf16[4,640,128]{2,1,0:T(8,128)(2,1)S(1)}, bf16[4,640,128]{2,1,0:T(8,128)(2,1)}, u32[]{:S(2)}) copy-start(bf16[4,640,128]{2,1,0:T(8,128)(2,1)} %copy-done.18) | copy-start | bytes 1966084
  70.8 11.4 %copy-start.21 = (bf16[4,640,128]{2,1,0:T(8,128)(2,1)S(1)}, bf16[4,640,128]{2,1,0:T(8,128)(2,1)}, u32[]{:S(2)}) copy-start(bf16[4,640,128]{2,1,0:T(8,128)(2,1)} %copy-done.20) | copy-start | bytes 1966084
  70.8 8.6 %collective-permute-start.20 = (bf16[2,384,128]{2,1,0:T(8,128)(2,1)S(1)}, bf16[2,384,128]{2,1,0:T(8,128)(2,1)S(1)}, u32[]{:S(2)}, u32[]{:S(2)}) collective-permute-start(bf16[2,384,128]{2,1,0:T(8,128)(2,1)S(1)} %pad_maximum_fusion.5), channel_id=1, source_target_pairs={{0,51},{1,18},{2,17},{3,48},{4,55},{5,22},{6,21},{7,52},{8,59},{9,... | collective-permute-start | bytes 589832 | tf_op jit(solution)/shard_map/ppermute | solution.py:49
  73.6 4.7 %collective-permute-start.18 = (bf16[4,128,128]{2,1,0:T(8,128)(2,1)S(1)}, bf16[4,128,128]{2,1,0:T(8,128)(2,1)S(1)}, u32[]{:S(2)}, u32[]{:S(2)}) collective-permute-start(bf16[4,128,128]{2,1,0:T(8,128)(2,1)S(1)} %fusion.4), channel_id=1, source_target_pairs={{0,208},{1,81},{2,210},{3,83},{4,84},{5,213},{6,86},{7,215},{8,216... | collective-permute-start | bytes 393224 | tf_op jit(solution)/shard_map/ppermute | solution.py:49
  73.6 4.7 %collective-permute-start.19 = (bf16[4,128,128]{2,1,0:T(8,128)(2,1)S(1)}, bf16[4,128,128]{2,1,0:T(8,128)(2,1)S(1)}, u32[]{:S(2)}, u32[]{:S(2)}) collective-permute-start(bf16[4,128,128]{2,1,0:T(8,128)(2,1)S(1)} %fusion.5), channel_id=1, source_target_pairs={{0,28},{1,21},{2,30},{3,23},{4,16},{5,25},{6,18},{7,27},{8,20},{9,... | collective-permute-start | bytes 393224 | tf_op jit(solution)/shard_map/ppermute | solution.py:49
  79.6 10.3 %copy-start.15 = (f32[4,2,128,128]{3,2,1,0:T(8,128)}, f32[4,2,128,128]{3,2,1,0:T(8,128)S(1)}, u32[]{:S(2)}) copy-start(f32[4,2,128,128]{3,2,1,0:T(8,128)S(1)} %pad_maximum_fusion.2) | copy-start | bytes 1572868
  79.6 8.6 %collective-permute-start.22 = (bf16[4,384,128]{2,1,0:T(8,128)(2,1)S(1)}, bf16[4,384,128]{2,1,0:T(8,128)(2,1)S(1)}, u32[]{:S(2)}, u32[]{:S(2)}) collective-permute-start(bf16[4,384,128]{2,1,0:T(8,128)(2,1)S(1)} %constant_dynamic-update-slice_fusion.2), channel_id=1, source_target_pairs={{0,28},{1,21},{2,30},{3,23},{4,16},{5,25},{6,18},{7,27},{8,20},{9,... | collective-permute-start | bytes 1179656 | tf_op jit(solution)/shard_map/ppermute | solution.py:49
  81.1 7.1 %collective-permute-start.21 = (f32[2,2,128,128]{3,2,1,0:T(8,128)S(1)}, f32[2,2,128,128]{3,2,1,0:T(8,128)S(1)}, u32[]{:S(2)}, u32[]{:S(2)}) collective-permute-start(f32[2,2,128,128]{3,2,1,0:T(8,128)S(1)} %slice.98), channel_id=1, source_target_pairs={{0,17},{1,18},{2,19},{3,48},{4,55},{5,20},{6,21},{7,22},{8,25},{9,... | collective-permute-start | bytes 786440 | tf_op jit(solution)/shard_map/ppermute | solution.py:49
  88.2 2.4 %copy-start.24 = (f32[2,2,128,128]{3,2,1,0:T(8,128)}, f32[2,2,128,128]{3,2,1,0:T(8,128)S(1)}, u32[]{:S(2)}) copy-start(f32[2,2,128,128]{3,2,1,0:T(8,128)S(1)} %collective-permute-done.21) | copy-start | bytes 786436
  89.2 14.2 %copy-start.5 = (bf16[384,1024]{1,0:T(8,128)(2,1)S(1)}, bf16[384,1024]{1,0:T(8,128)(2,1)}, u32[]{:S(2)}) copy-start(bf16[384,1024]{1,0:T(8,128)(2,1)} %copy-done.3) | copy-start | bytes 2359300
  89.2 12.9 %collective-permute-start.25 = (bf16[2,4,384,128]{3,2,1,0:T(8,128)(2,1)}, bf16[2,4,384,128]{3,2,1,0:T(8,128)(2,1)}, u32[]{:S(2)}, u32[]{:S(2)}) collective-permute-start(bf16[2,4,384,128]{3,2,1,0:T(8,128)(2,1)} %pad_maximum_fusion.1), channel_id=1, source_target_pairs={{0,20},{1,29},{2,22},{3,31},{4,24},{5,17},{6,26},{7,19},{8,28},{9,... | collective-permute-start | bytes 2359304 | tf_op jit(solution)/shard_map/ppermute | solution.py:49
  90.6 5.0 %collective-permute-start.23 = (f32[2,128,128]{2,1,0:T(8,128)}, f32[2,128,128]{2,1,0:T(8,128)S(1)}, u32[]{:S(2)}, u32[]{:S(2)}) collective-permute-start(f32[2,128,128]{2,1,0:T(8,128)} %add_bitcast_fusion), channel_id=1, source_target_pairs={{0,51},{1,16},{2,17},{3,18},{4,21},{5,22},{6,23},{7,52},{8,59},{9,... | collective-permute-start | bytes 393224 | tf_op jit(solution)/shard_map/ppermute | solution.py:49
  96.6 9.6 %collective-permute-start.24 = (bf16[2,128,128]{2,1,0:T(8,128)(2,1)S(1)}, bf16[2,128,128]{2,1,0:T(8,128)(2,1)S(1)}, u32[]{:S(2)}, u32[]{:S(2)}) collective-permute-start(bf16[2,128,128]{2,1,0:T(8,128)(2,1)S(1)} %fusion.6), channel_id=1, source_target_pairs={{0,32},{1,33},{2,34},{3,35},{4,36},{5,37},{6,38},{7,39},{8,40},{9,... | collective-permute-start | bytes 196616 | tf_op jit(solution)/shard_map/ppermute | solution.py:49
  103.4 9.2 %copy-start.2 = (bf16[384,1024]{1,0:T(8,128)(2,1)S(1)}, bf16[384,1024]{1,0:T(8,128)(2,1)}, u32[]{:S(2)}) copy-start(bf16[384,1024]{1,0:T(8,128)(2,1)} %cot_ref.1) | copy-start | bytes 2359300
  106.1 6.4 %collective-permute-start.28 = (bf16[384,2048]{1,0:T(8,128)(2,1)S(1)}, bf16[384,2048]{1,0:T(8,128)(2,1)S(1)}, u32[]{:S(2)}, u32[]{:S(2)}) collective-permute-start(bf16[384,2048]{1,0:T(8,128)(2,1)S(1)} %shard_map.114), channel_id=1, source_target_pairs={{0,16},{1,17},{2,18},{3,19},{4,20},{5,21},{6,22},{7,23},{8,24},{9,... | collective-permute-start | bytes 4718600 | tf_op jit(solution)/shard_map/ppermute | solution.py:49
  106.3 4.8 %collective-permute-start.26 = (f32[2,128,128]{2,1,0:T(8,128)S(1)}, f32[2,128,128]{2,1,0:T(8,128)S(1)}, u32[]{:S(2)}, u32[]{:S(2)}) collective-permute-start(f32[2,128,128]{2,1,0:T(8,128)S(1)} %get-tuple-element.124), channel_id=1, source_target_pairs={{0,208},{1,81},{2,210},{3,83},{4,84},{5,213},{6,86},{7,215},{8,216... | collective-permute-start | bytes 393224 | tf_op jit(solution)/shard_map/ppermute | solution.py:49
  111.1 9.2 %copy-start.10 = (f32[256,640]{1,0:T(8,128)S(1)}, f32[256,640]{1,0:T(8,128)}, u32[]{:S(2)}) copy-start(f32[256,640]{1,0:T(8,128)} %m_ref.1) | copy-start | bytes 1966084
  111.1 7.1 %collective-permute-start.27 = (f32[2,2,128,128]{3,2,1,0:T(8,128)S(1)}, f32[2,2,128,128]{3,2,1,0:T(8,128)S(1)}, u32[]{:S(2)}, u32[]{:S(2)}) collective-permute-start(f32[2,2,128,128]{3,2,1,0:T(8,128)S(1)} %pad_maximum_fusion.4), channel_id=1, source_target_pairs={{0,80},{1,209},{2,82},{3,211},{4,212},{5,85},{6,214},{7,87},{8,88}... | collective-permute-start | bytes 786440 | tf_op jit(solution)/shard_map/ppermute | solution.py:49
  118.2 2.0 %collective-permute-start.29 = (f32[4,2,128,128]{3,2,1,0:T(8,128)S(1)}, f32[4,2,128,128]{3,2,1,0:T(8,128)S(1)}, u32[]{:S(2)}, u32[]{:S(2)}) collective-permute-start(f32[4,2,128,128]{3,2,1,0:T(8,128)S(1)} %constant_dynamic-update-slice_fusion.6.mine_ref), channel_id=1, source_target_pairs={{0,16},{1,17},{2,18},{3,19},{4,20},{5,21},{6,22},{7,23},{8,24},{9,... | collective-permute-start | bytes 1572872 | tf_op jit(solution)/shard_map/ppermute | solution.py:49
  120.2 1.1 copy-start.11
